TPU v7x, 32 devices: a whole 2x2x4 slice. The times are simulated.
32 devices in a mesh: dp: 8 (over y, x, core), tensor: 4 (over z).
Axes of the slice: x: 2, y: 2, z: 4, core: 2. Of those that a mesh axis runs over, the one named last changes fastest.
Arguments:
- activations: bfloat16 [6144, 8192], P('dp'), may hold values from -48 to 48
- cotangent: bfloat16 [6144, 1024], P('dp', 'tensor'), may hold values from -0.375 to 0.375
- sampled_rows: int32 [512], P('dp'), may hold values from 0 to 767
- block_owner: int32 [32], replicated, may hold values from 0 to 7, as said below
Outputs:
- natural_step: float32 [8192, 1024], P('dp', 'tensor')
- owner_block_inverses: float32 [32, 256, 256], P('dp')
Inputs may be any that keep to these rules, and one draw needn't show every extreme that they name: `block_owner`: each index of dp owns either no block or exactly 4 blocks; block 0 is owned by index 4.
All inputs are finite; a program needn't handle non-finite values. Where the computation divides by a largest or mean magnitude, that divisor is 1e-20 or more.
Results may differ from a plain program's by a relative error of at most 0.0003.
Values may be sent and summed in bfloat16 or wider, within the bound.
No kernel may reach another device: no remote copies, remote signals or barrier semaphores. Data moves between devices by JAX's collectives and lax.ppermute only.
A program may use at most 128 MiB of HBM per device.

v0:
```python
import jax
import jax.numpy as jnp
from jax import lax
from jax.sharding import PartitionSpec as P

S_DEV = 64
FACTOR_BLOCK = 256
ITERS = 10


DAMPING = 0.05
precise_mode = lax.Precision.HIGHEST


def from_partner(block, axis, apart):
    count = lax.axis_size(axis)
    route = []
    for low in range(count):
        high = low | 1 << apart
        if high != low and high < count:
            route += [(low, high), (high, low)]
    return lax.ppermute(block, axis, route)


def newton_inverse(matrix):
    extent = matrix.shape[-1]
    identity = jnp.eye(extent, dtype=jnp.float32)
    row_bound = jnp.max(jnp.sum(jnp.abs(matrix), axis=2), axis=1)
    initial = identity[None, :, :] / row_bound[:, None, None]

    def advance(turn_index, current):
        product = jnp.einsum("nij,njk->nik", matrix, current, precision=precise_mode)
        return jnp.einsum(
            "nij,njk->nik", current, 2.0 * identity[None, :, :] - product, precision=precise_mode
        )

    return lax.fori_loop(0, ITERS, advance, initial)


def block_rank(block_owner):
    block_total = block_owner.shape[0]
    same_owner = block_owner[:, None] == block_owner[None, :]
    positions = jnp.arange(block_total, dtype=jnp.int32)
    before = positions[None, :] < positions[:, None]
    return jnp.sum((same_owner & before).astype(jnp.int32), axis=1)


def owner_grams(received):
    return jnp.einsum("pcsk,pcsl->ckl", received, received, preferred_element_type=jnp.float32)


def per_device(activations, cotangent, sampled_rows, block_owner):
    tok_local = activations.shape[0]
    model_width = activations.shape[1]
    group_w = cotangent.shape[1]
    dp_count = lax.axis_size("dp")
    my_dp = lax.axis_index("dp")
    block_total = model_width // FACTOR_BLOCK
    capacity = max(1, block_total // dp_count)
    row_share = model_width // dp_count
    samples_all = S_DEV * dp_count
    grad_rows = lax.psum_scatter(
        lax.dot_general(
            activations, cotangent, (((0,), (0,)), ((), ())), preferred_element_type=jnp.float32
        ),
        "dp",
        scatter_dimension=0,
        tiled=True,
    )
    picked_acts = jnp.take(activations, sampled_rows, axis=0)
    picked_grads = jnp.take(cotangent, sampled_rows, axis=0)
    g_partial = lax.dot_general(
        picked_grads, picked_grads, (((0,), (0,)), ((), ())), preferred_element_type=jnp.float32
    )
    g_total = lax.psum(g_partial, "dp")
    g_factor = g_total * (tok_local / S_DEV) + DAMPING * jnp.eye(group_w, dtype=jnp.float32)
    slot_of = block_owner * capacity + block_rank(block_owner)
    dest_ids = jnp.arange(dp_count * capacity, dtype=jnp.int32)
    chooser = (slot_of[None, :] == dest_ids[:, None]).astype(jnp.bfloat16)
    row_blocks = picked_acts.reshape(S_DEV, block_total, FACTOR_BLOCK)
    outgoing = lax.dot_general(
        chooser, row_blocks, (((1,), (1,)), ((), ())), preferred_element_type=jnp.float32
    )
    outgoing = outgoing.astype(jnp.bfloat16).reshape(dp_count, capacity, S_DEV, FACTOR_BLOCK)
    gram_slots = owner_grams(
        lax.all_to_all(outgoing, "dp", split_axis=0, concat_axis=0, tiled=True)
    )
    a_factor = (
        gram_slots / samples_all + DAMPING * jnp.eye(FACTOR_BLOCK, dtype=jnp.float32)[None, :, :]
    )
    input_factor_inverse = newton_inverse(a_factor)
    owned_count = jnp.sum((block_owner == my_dp).astype(jnp.int32))
    slot_used = jnp.arange(capacity, dtype=jnp.int32) < owned_count
    owned_out = jnp.where(slot_used[:, None, None], input_factor_inverse, 0.0)
    g_inverse = newton_inverse(g_factor[None, :, :])[0]
    per_dev = max(1, row_share // FACTOR_BLOCK)
    rows_each = min(row_share, FACTOR_BLOCK)
    first_block = my_dp * row_share // FACTOR_BLOCK
    need_ids = first_block + jnp.arange(per_dev, dtype=jnp.int32)
    need_slots = jnp.take(slot_of, need_ids)
    row_offset = my_dp * row_share % FACTOR_BLOCK
    shard_piece = lax.all_gather(owned_out, "dp", axis=0, tiled=True)
    rows_part = lax.dynamic_slice_in_dim(shard_piece, row_offset, rows_each, 1)
    slot_ids = jnp.arange(shard_piece.shape[0], dtype=jnp.int32)
    selector = (need_slots[:, None] == slot_ids[None, :]).astype(jnp.float32)
    inverse_rows = jnp.einsum("jm,mkl->jkl", selector, rows_part, precision=precise_mode)
    grad_right = jnp.dot(
        grad_rows, g_inverse, precision=precise_mode, preferred_element_type=jnp.float32
    )
    if row_share < FACTOR_BLOCK:
        partner = from_partner(grad_right, "dp", 0)
        is_lower = my_dp % 2 == 0
        joined = jnp.where(
            is_lower,
            jnp.concatenate([grad_right, partner], 0),
            jnp.concatenate([partner, grad_right], 0),
        )
        complete_rows = joined[None, :, :]
    else:
        complete_rows = grad_right.reshape(per_dev, FACTOR_BLOCK, group_w)
    natural_step = jnp.einsum("jrk,jkl->jrl", inverse_rows, complete_rows, precision=precise_mode)
    return (natural_step.reshape(row_share, group_w), owned_out)


def solution(mesh):
    return jax.shard_map(
        per_device,
        mesh=mesh,
        in_specs=(P("dp", None), P("dp", "tensor"), P("dp"), P()),
        out_specs=(P("dp", "tensor"), P("dp", None, None)),
        check_vma=False,
    )
```

profile of v0, /device:TPU:0, one launch (start us, length us, event | category | flops | bytes accessed | tf_op | source)
XLA Modules:
  0.0 219.8 jit_solution(17187886332431609402)
XLA Ops:
  7.2 0.7 compare_select_fusion
  7.9 0.7 compare_and_fusion
  8.6 0.7 gather_fusion.2
  9.3 1.0 fusion.20
  10.4 11.3 %fusion.34 = f32[8192,256]{1,0:T(8,128)} fusion(bf16[768,8192]{1,0:T(8,128)(2,1)} %param.8, bf16[768,256]{1,0:T(8,128)(2,1)S(1)} %copy-done), kind=kOutput, calls=%fused_computation.63 | convolution fusion | flops 3221225472 | bytes 21364736 | tf_op jit(solution)/shard_map/dot_general | solution.py:63
  21.7 8.4 %gather_fusion.1 = bf16[64,8192]{1,0:T(8,128)(2,1)S(1)} fusion(bf16[768,8192]{1,0:T(8,128)(2,1)} %param.8, s32[1024]{0:T(1024)S(1)} %pad_clamp_fusion), kind=kCustom, calls=%fused_computation.1 | custom fusion | bytes 2097408 | tf_op jit(solution)/shard_map/jit(_take)/gather | solution.py:70
  30.6 0.7 fusion.31
  31.8 1.6 copy.46
  33.4 5.2 %all-to-all-start = ((bf16[8,4,64,256]{3,2,1,0:T(8,128)(2,1)}), bf16[8,4,64,256]{3,2,1,0:T(8,128)(2,1)S(1)}, u32[]{:S(2)}, u32[]{:S(2)}) async-start(bf16[8,4,64,256]{3,2,1,0:T(8,128)(2,1)} %bitcast.3), calls=%async_computation | async-start | bytes 2097152 | tf_op jit(solution)/shard_map/all_to_all | solution.py:86
  39.0 0.8 copy.34
  39.8 0.6 iota_compare_fusion.7
  40.5 13.9 %all-to-all-done = bf16[8,4,64,256]{3,2,1,0:T(8,128)(2,1)S(1)} async-done(((bf16[8,4,64,256]{3,2,1,0:T(8,128)(2,1)}), bf16[8,4,64,256]{3,2,1,0:T(8,128)(2,1)S(1)}, u32[]{:S(2)}, u32[]{:S(2)}) %all-to-all-start) | async-done | bytes 1048608 | tf_op jit(solution)/shard_map/all_to_all | solution.py:86
  54.3 0.6 abs_reduce_fusion
  55.4 1.1 broadcast_divide_fusion
  56.5 32.1 %while.22 = (s32[]{:T(128)}, f32[4,256,256]{1,2,0:T(8,128)S(1)}, f32[4,256,256]{2,1,0:T(8,128)S(1)}, s32[]{:T(128)}) while((s32[]{:T(128)}, f32[4,256,256]{1,2,0:T(8,128)S(1)}, f32[4,256,256]{2,1,0:T(8,128)S(1)}, s32[]{:T(128)}) %tuple.51), condition=%wide.region_5.6_spmd.clone, body=%wide.region_4.5_spmd.clone.sunk | while | flops 1611005952 | bytes 8912949 | solution.py:37
  56.6 1.2 convolution_subtract_fusion.4
  57.8 1.9 convolution_bitcast_fusion.5
  59.8 1.2 convolution_subtract_fusion.4
  61.0 1.9 convolution_bitcast_fusion.5
  63.0 1.2 convolution_subtract_fusion.4
  64.2 1.9 convolution_bitcast_fusion.5
  66.2 1.2 convolution_subtract_fusion.4
  67.4 1.9 convolution_bitcast_fusion.5
  69.4 1.2 convolution_subtract_fusion.4
  70.6 1.9 convolution_bitcast_fusion.5
  72.6 1.2 convolution_subtract_fusion.4
  73.8 1.9 convolution_bitcast_fusion.5
  75.8 1.2 convolution_subtract_fusion.4
  77.0 1.9 convolution_bitcast_fusion.5
  79.0 1.2 convolution_subtract_fusion.4
  80.2 1.9 convolution_bitcast_fusion.5
  82.3 1.2 convolution_subtract_fusion.4
  83.4 1.9 convolution_bitcast_fusion.5
  85.5 1.2 convolution_subtract_fusion.4
  86.6 1.9 convolution_bitcast_fusion.5
  88.9 1.1 broadcast_select_fusion
  90.1 0.6 gather_fusion
  90.8 1.1 fusion.19
  91.8 0.6 reduce_max.19
  93.1 10.9 %while.23 = (s32[]{:T(128)}, f32[1,256,256]{1,2,0:T(8,128)S(1)}, f32[1,256,256]{2,1,0:T(8,128)S(1)}, s32[]{:T(128)}) while((s32[]{:T(128)}, f32[1,256,256]{1,2,0:T(8,128)S(1)}, f32[1,256,256]{2,1,0:T(8,128)S(1)}, s32[]{:T(128)}) %tuple.48), condition=%wide.region_11.12_spmd.clone, body=%wide.region_10.11_spmd.clone.sunk | while | flops 402849792 | bytes 2097205 | solution.py:37
  93.6 0.6 convolution_bitcast_fusion.6
  94.3 0.4 convolution_subtract_fusion.5
  94.7 0.6 convolution_bitcast_fusion.6
  95.3 0.4 convolution_subtract_fusion.5
  95.7 0.6 convolution_bitcast_fusion.6
  96.4 0.4 convolution_subtract_fusion.5
  96.8 0.6 convolution_bitcast_fusion.6
  97.5 0.4 convolution_subtract_fusion.5
  97.9 0.6 convolution_bitcast_fusion.6
  98.5 0.4 convolution_subtract_fusion.5
  99.0 0.6 convolution_bitcast_fusion.6
  99.6 0.4 convolution_subtract_fusion.5
  100.0 0.6 convolution_bitcast_fusion.6
  100.7 0.4 convolution_subtract_fusion.5
  101.1 0.6 convolution_bitcast_fusion.6
  101.7 0.4 convolution_subtract_fusion.5
  102.2 0.6 convolution_bitcast_fusion.6
  102.8 0.4 convolution_subtract_fusion.5
  103.2 0.6 convolution_bitcast_fusion.6
  104.1 39.6 %reduce-scatter.2.cloned.1.call-done = f32[1024,256]{1,0:T(8,128)} async-done(((f32[8192,256]{1,0:T(8,128)}), f32[1024,256]{1,0:T(8,128)}) %reduce-scatter.2.cloned.1.call-update) | async-done | bytes 1048592 | tf_op jit(solution)/shard_map/reduce_scatter | solution.py:62
  143.7 2.2 %fusion.14 = f32[4,256,256]{2,1,0:T(8,128)S(1)} fusion(f32[4,256,256]{2,1,0:T(8,128)} %bitcast.75, f32[1,256,256]{1,2,0:T(8,128)S(1)} %get-tuple-element.47), kind=kOutput, calls=%fused_computation.27 | convolution fusion | flops 805306368 | bytes 2359296 | tf_op jit(solution)/shard_map/dot_general | solution.py:107
  145.9 54.6 %all-gather.2.cloned.1.call-done = f32[32,256,256]{2,1,0:T(8,128)} async-done(((f32[4,256,256]{2,1,0:T(8,128)}), f32[32,256,256]{2,1,0:T(8,128)}) %all-gather.2.cloned.1.call-update) | async-done | bytes 8388624 | tf_op jit(solution)/shard_map/all_gather | solution.py:102
  200.6 10.5 %fusion.8 = f32[4,256,256]{2,0,1:T(4,128)S(1)} fusion(f32[32,256,256]{2,1,0:T(8,128)} %all-gather.2.cloned.1.call-done, s32[4]{0:T(128)S(1)} %and_select_fusion), kind=kOutput, calls=%fused_computation.15 | convolution fusion | flops 100663424 | bytes 9437200 | tf_op jit(solution)/shard_map/jm,mkl->jkl/dot_general | solution.py:106
  211.0 2.2 fusion.12
  (57 shorter events, 4.0 us)
Async XLA Ops:
  7.2 1.4 copy-start
  7.2 83.6 %all-reduce.2.cloned.1.call-start = ((), (), s32[]{:S(2)}) async-start(), calls=%async_computation.4 | async-start | bytes 524288 | tf_op jit(solution)/shard_map/psum | solution.py:75
  10.3 133.3 %reduce-scatter.2.cloned.1.call-start = ((), (), s32[]{:S(2)}) async-start(), calls=%async_computation.3 | async-start | bytes 9437184 | tf_op jit(solution)/shard_map/reduce_scatter | solution.py:62
  21.7 8.7 %copy-start.1 = (s32[32]{0:T(128)S(1)}, s32[32]{0:T(128)}, u32[]{:S(2)}) copy-start(s32[32]{0:T(128)} %param.11) | copy-start | bytes 388
  33.4 21.0 %all-to-all-start = ((bf16[8,4,64,256]{3,2,1,0:T(8,128)(2,1)}), bf16[8,4,64,256]{3,2,1,0:T(8,128)(2,1)S(1)}, u32[]{:S(2)}, u32[]{:S(2)}) async-start(bf16[8,4,64,256]{3,2,1,0:T(8,128)(2,1)} %bitcast.3), calls=%async_computation | async-start | bytes 2097152 | tf_op jit(solution)/shard_map/all_to_all | solution.py:86
  38.6 162.0 %all-gather.2.cloned.1.call-start = ((), (), s32[]{:S(2)}) async-start(), calls=%async_computation.2 | async-start | bytes 9437184 | tf_op jit(solution)/shard_map/all_gather | solution.py:102
Sparse Core Ops, SparseCore 0:
  11.1 58.0 all-reduce.1
  73.0 70.6 reduce-scatter.1
  146.2 54.3 all-gather.1
where the time goes:
time: 220 us
  waiting for transfers between devices  108 us (49%)
  matrix products  68.9 us (31%)
  between operations  14.6 us (7%)
  local copies, waits for them, and re-layouts  14.1 us (6%)
  other arithmetic  7.31 us (3%)
  starting transfers between devices  5.49 us (2%)
    all_gather x1, waiting for transfers between devices, per_device(): shard_piece = lax.all_gather(owned_out, 'dp', axis=0, tiled=True)  54.6 us
    reduce_scatter x1, waiting for transfers between devices, per_device(): lax.psum_scatter(lax.dot_general(activations, cotangent, (((0,), (0,)), (...  39.6 us
    dot_general x20, matrix products, advance(): jnp.einsum('nij,njk->nik', current, 2.0 * identity[None, :, :] - product,...  25 us
    dot_general x20, matrix products, advance(): jnp.einsum('nij,njk->nik', matrix, current, precision=precise_mode)  15.8 us
    all_to_all x1, waiting for transfers between devices, per_device(): lax.all_to_all(outgoing, 'dp', split_axis=0, concat_axis=0, tiled=True)  13.9 us
    dot_general x1, matrix products, per_device(): lax.dot_general(activations, cotangent, (((0,), (0,)), ((), ())), preferr...  11.3 us
    dot_general x1, matrix products, per_device(): jnp.einsum('jm,mkl->jkl', selector, rows_part, precision=precise_mode)  10.5 us
    gather x1, local copies, waits for them, and re-layouts, per_device(): picked_acts = jnp.take(activations, sampled_rows, axis=0)  8.38 us
  transfers between devices with their start and end apart: 4, of which 3 were waited for; matrix products, arithmetic and copies ran while one was open for 34% of the time, Pallas kernels for 0%

commit v1 on v0

--- a/solution.py
+++ b/solution.py
@@ -1,6 +1,8 @@
 import jax
 import jax.numpy as jnp
 from jax import lax
+from jax.experimental import pallas as pl
+from jax.experimental.pallas import tpu as pltpu
 from jax.sharding import PartitionSpec as P
 
 S_DEV = 64
@@ -10,6 +12,16 @@
 
 DAMPING = 0.05
 precise_mode = lax.Precision.HIGHEST
+f32 = jnp.float32
+bf16 = jnp.bfloat16
+
+
+def block_rank(block_owner):
+    block_total = block_owner.shape[0]
+    same_owner = block_owner[:, None] == block_owner[None, :]
+    positions = jnp.arange(block_total, dtype=jnp.int32)
+    before = positions[None, :] < positions[:, None]
+    return jnp.sum((same_owner & before).astype(jnp.int32), axis=1)
 
 
 def from_partner(block, axis, apart):
@@ -37,19 +49,11 @@
     return lax.fori_loop(0, ITERS, advance, initial)
 
 
-def block_rank(block_owner):
-    block_total = block_owner.shape[0]
-    same_owner = block_owner[:, None] == block_owner[None, :]
-    positions = jnp.arange(block_total, dtype=jnp.int32)
-    before = positions[None, :] < positions[:, None]
-    return jnp.sum((same_owner & before).astype(jnp.int32), axis=1)
-
-
 def owner_grams(received):
     return jnp.einsum("pcsk,pcsl->ckl", received, received, preferred_element_type=jnp.float32)
 
 
-def per_device(activations, cotangent, sampled_rows, block_owner):
+def general_device(activations, cotangent, sampled_rows, block_owner):
     tok_local = activations.shape[0]
     model_width = activations.shape[1]
     group_w = cotangent.shape[1]
@@ -122,7 +126,300 @@
     return (natural_step.reshape(row_share, group_w), owned_out)
 
 
+VMEM_LIMIT = 48 * 1024 * 1024
+
+
+def vmem(shape=None, index_map=None):
+    if shape is None:
+        return pl.BlockSpec(memory_space=pltpu.VMEM)
+    return pl.BlockSpec(shape, index_map)
+
+
+def pick_body(ids, rows_ref, cot_ref, act_ref, out_ref, held, sems):
+    count = held.shape[0]
+    dests = count // 2
+
+    def copy(i):
+        start = pl.multiple_of(ids[i] * FACTOR_BLOCK, FACTOR_BLOCK)
+        return pltpu.make_async_copy(
+            act_ref.at[:, pl.ds(start, FACTOR_BLOCK)], held.at[i], sems.at[i]
+        )
+
+    for i in range(count):
+        copy(i).start()
+    samples = rows_ref.shape[0]
+    tokens = cot_ref.shape[0]
+    places = lax.broadcasted_iota(jnp.int32, (samples, tokens), 1)
+    chooser = (places == rows_ref[...]).astype(bf16)
+    picked = jnp.dot(chooser, cot_ref[...], preferred_element_type=f32).astype(bf16)
+    for d in range(dests):
+        out_ref[d, :, 2 * FACTOR_BLOCK :] = picked
+    for i in range(count):
+        copy(i).wait()
+        picked = jnp.dot(chooser, held[i], preferred_element_type=f32).astype(bf16)
+        out_ref[i // 2, :, (i % 2) * FACTOR_BLOCK : (i % 2 + 1) * FACTOR_BLOCK] = picked
+
+
+def pick_rows(ids, sampled_rows, cotangent, activations):
+    count = ids.shape[0]
+    samples = sampled_rows.shape[0]
+    tokens, group_w = cotangent.shape
+    return pl.pallas_call(
+        pick_body,
+        out_shape=jax.ShapeDtypeStruct(
+            (count // 2, samples, 2 * FACTOR_BLOCK + group_w), bf16
+        ),
+        grid_spec=pltpu.PrefetchScalarGridSpec(
+            num_scalar_prefetch=1,
+            grid=(),
+            in_specs=[vmem(), vmem(), pl.BlockSpec(memory_space=pl.ANY)],
+            out_specs=vmem(),
+            scratch_shapes=[
+                pltpu.VMEM((count, tokens, FACTOR_BLOCK), bf16),
+                pltpu.SemaphoreType.DMA((count,)),
+            ],
+        ),
+        compiler_params=pltpu.CompilerParams(vmem_limit_bytes=VMEM_LIMIT),
+        cost_estimate=pl.CostEstimate(
+            flops=2 * samples * tokens * count * FACTOR_BLOCK,
+            bytes_accessed=2 * tokens * count * FACTOR_BLOCK,
+            transcendentals=0,
+        ),
+        name="pick_rows",
+    )(ids, sampled_rows[:, None], cotangent, activations)
+
+
+def grad_body(ids, cot_ref, act_ref, first_ref, second_ref, turned):
+    half = pl.num_programs(0) // 2
+    step = pl.program_id(0)
+
+    @pl.when(step == 0)
+    def _():
+        turned[...] = cot_ref[...].astype(f32).T.astype(bf16)
+
+    product = jnp.dot(turned[...], act_ref[...], preferred_element_type=f32)
+
+    @pl.when(step < half)
+    def _():
+        first_ref[0] = product
+
+    @pl.when(step >= half)
+    def _():
+        second_ref[0] = product
+
+
+def partial_grads(ids, cotangent, activations, row_share):
+    tokens, group_w = cotangent.shape
+    steps = ids.shape[0]
+    half = steps // 2
+    one = jax.ShapeDtypeStruct((half, group_w, row_share), f32)
+    return pl.pallas_call(
+        grad_body,
+        out_shape=(one, one),
+        grid_spec=pltpu.PrefetchScalarGridSpec(
+            num_scalar_prefetch=1,
+            grid=(steps,),
+            in_specs=[
+                pl.BlockSpec((tokens, group_w), lambda i, ids: (0, 0)),
+                pl.BlockSpec((tokens, row_share), lambda i, ids: (0, ids[i])),
+            ],
+            out_specs=[
+                pl.BlockSpec((1, group_w, row_share), lambda i, ids: (jnp.minimum(i, half - 1), 0, 0)),
+                pl.BlockSpec((1, group_w, row_share), lambda i, ids: (jnp.maximum(i - half, 0), 0, 0)),
+            ],
+            scratch_shapes=[pltpu.VMEM((group_w, tokens), bf16)],
+        ),
+        compiler_params=pltpu.CompilerParams(vmem_limit_bytes=VMEM_LIMIT),
+        cost_estimate=pl.CostEstimate(
+            flops=2 * tokens * group_w * row_share * steps,
+            bytes_accessed=steps * row_share * (2 * tokens + 4 * group_w),
+            transcendentals=0,
+        ),
+        name="partial_grads",
+    )(ids, cotangent, activations)
+
+
+def exact_dot(left, right, dims=(((1,), (0,)), ((), ()))):
+    return lax.dot_general(left, right, dims, precision=precise_mode, preferred_element_type=f32)
+
+
+def invert_body(scales, rows_ref, need_ref, own_ref, out_ref):
+    width = FACTOR_BLOCK
+    eye = (
+        lax.broadcasted_iota(jnp.int32, (width, width), 0)
+        == lax.broadcasted_iota(jnp.int32, (width, width), 1)
+    ).astype(f32)
+    states = []
+    for m in range(3):
+        rows = rows_ref[:, m * width : (m + 1) * width]
+        gram = lax.dot_general(
+            rows, rows, (((0,), (0,)), ((), ())), preferred_element_type=f32
+        )
+        matrix = gram * scales[m] + DAMPING * eye
+        bound = jnp.max(jnp.sum(jnp.abs(matrix), axis=1, keepdims=True), axis=0, keepdims=True)
+        inverse_bound = 1.0 / bound
+        low = matrix * inverse_bound
+        states.append((low, (2.0 * eye - low) * inverse_bound))
+    lows = [2.0 * low - exact_dot(low, low) for low, _ in states]
+    currents = [current for _, current in states]
+    for turn in range(1, ITERS):
+        if turn < ITERS - 1:
+            both = [
+                exact_dot(jnp.concatenate([current, low], axis=0), low)
+                for current, low in zip(currents, lows)
+            ]
+            currents = [2.0 * current - b[:width] for current, b in zip(currents, both)]
+            lows = [2.0 * low - b[width:] for low, b in zip(lows, both)]
+        else:
+            currents = [
+                2.0 * current - exact_dot(current, low) for current, low in zip(currents, lows)
+            ]
+    need_ref[...] = currents[0]
+    own_ref[...] = currents[1] * scales[3]
+    out_ref[...] = currents[2]
+
+
+def invert_factors(scales, rows):
+    one = jax.ShapeDtypeStruct((FACTOR_BLOCK, FACTOR_BLOCK), f32)
+    return pl.pallas_call(
+        invert_body,
+        out_shape=(one, one, one),
+        in_specs=[pl.BlockSpec(memory_space=pltpu.SMEM), vmem()],
+        out_specs=(vmem(), vmem(), vmem()),
+        compiler_params=pltpu.CompilerParams(vmem_limit_bytes=VMEM_LIMIT),
+        cost_estimate=pl.CostEstimate(
+            flops=2 * 6 * 3 * 19 * FACTOR_BLOCK**3, bytes_accessed=2 << 20, transcendentals=0
+        ),
+        name="invert_factors",
+    )(scales, rows)
+
+
+def finish_body(order, *refs):
+    (self_own, self_got, x_a, x_b, y_a, y_b, g_ref) = refs[:7]
+    needs, owns = refs[7:11], refs[11:15]
+    step_ref, owned_ref = refs[15:]
+    half = x_a.shape[0]
+    top = self_own[0, :half] + self_got[0, :half] + (x_a[...] + y_a[...])
+    low = self_own[0, half:] + self_got[0, half:] + (x_b[...] + y_b[...])
+    total = jnp.concatenate([top, low], axis=0)
+    right = exact_dot(g_ref[...], total, (((0,), (0,)), ((), ())))
+    tmp = right
+    blocks = []
+    for j in range(len(needs)):
+        blocks.append(tmp[:, j * FACTOR_BLOCK : (j + 1) * FACTOR_BLOCK])
+    for k in range(len(needs)):
+        j = order[k]
+        owned_ref[j] = owns[k][...]
+        chosen = blocks[0]
+        for other in range(1, len(needs)):
+            chosen = jnp.where(j == other, blocks[other], chosen)
+        start = pl.multiple_of(j * FACTOR_BLOCK, FACTOR_BLOCK)
+        step_ref[pl.ds(start, FACTOR_BLOCK), :] = exact_dot(
+            needs[k][...], chosen, (((1,), (1,)), ((), ()))
+        )
+
+
+def finish(order, pieces, needs, owns):
+    group_w, row_share = pieces[0].shape[1:]
+    count = len(needs)
+    return pl.pallas_call(
+        finish_body,
+        out_shape=(
+            jax.ShapeDtypeStruct((row_share, group_w), f32),
+            jax.ShapeDtypeStruct((count, FACTOR_BLOCK, FACTOR_BLOCK), f32),
+        ),
+        in_specs=[pl.BlockSpec(memory_space=pltpu.SMEM)] + [vmem()] * (7 + 2 * count),
+        out_specs=(vmem(), vmem()),
+        compiler_params=pltpu.CompilerParams(vmem_limit_bytes=VMEM_LIMIT),
+        cost_estimate=pl.CostEstimate(
+            flops=2 * 6 * 2 * row_share * group_w * FACTOR_BLOCK,
+            bytes_accessed=9 << 20,
+            transcendentals=0,
+        ),
+        name="finish",
+    )(order, *pieces, *needs, *owns)
+
+
+def square_device(activations, cotangent, sampled_rows, block_owner):
+    tok_local, model_width = activations.shape
+    dp_count = lax.axis_size("dp")
+    depth = lax.axis_size("tensor")
+    me = lax.axis_index("dp")
+    z = lax.axis_index("tensor")
+    samples = sampled_rows.shape[0]
+    row_share = model_width // dp_count
+    block_total = block_owner.shape[0]
+    capacity = block_total // dp_count
+
+    def swap(block, bit):
+        return lax.ppermute(block, "dp", [(i, i ^ bit) for i in range(dp_count)])
+
+    def shift(block, by):
+        return lax.ppermute(block, "tensor", [(i, (i + by) % depth) for i in range(depth)])
+
+    core, across_x, across_y = 1, 2, 4
+
+    slot_of = block_owner * capacity + block_rank(block_owner)
+    dests = jnp.arange(dp_count, dtype=jnp.int32)
+    my_slots = dests * capacity + z
+    blocks = jnp.arange(block_total, dtype=jnp.int32)
+    in_slot = slot_of[None, :] == my_slots[:, None]
+    slot_block = jnp.sum(jnp.where(in_slot, blocks[None, :], 0), axis=1)
+    ids = jnp.stack([my_slots, slot_block], axis=1).reshape(2 * dp_count)
+    owned_count = jnp.sum((block_owner == me).astype(jnp.int32))
+    used = (z < owned_count).astype(f32)
+    scales = jnp.stack(
+        [
+            jnp.asarray(1.0 / (samples * dp_count), f32),
+            jnp.asarray(1.0 / (samples * dp_count), f32),
+            jnp.asarray(tok_local / samples, f32),
+            used,
+        ]
+    )
+
+    def grads(masks):
+        to = [me ^ m ^ core for m in masks] + [me ^ m for m in masks]
+        return partial_grads(jnp.stack(to).astype(jnp.int32), cotangent, activations, row_share)
+
+    far_theirs, far_mine = grads([across_x | across_y])
+    far_got = swap(far_theirs, core)
+    picked = pick_rows(ids, sampled_rows, cotangent, activations)
+    got = lax.all_to_all(picked, "dp", split_axis=0, concat_axis=0, tiled=True)
+    half = cotangent.shape[1] // 2
+    far_x = swap(far_mine[0, :half] + far_got[0, :half], across_x)
+    far_y = swap(far_mine[0, half:] + far_got[0, half:], across_y)
+
+    near_theirs, near_mine = grads([across_x, across_y])
+    near_got = swap(near_theirs, core)
+    self_theirs, self_mine = grads([0])
+    self_got = swap(self_theirs, core)
+
+    x_a = swap(near_mine[0, :half] + near_got[0, :half], across_x)
+    y_b = swap(near_mine[1, half:] + near_got[1, half:], across_y)
+    x_b = swap(near_mine[0, half:] + near_got[0, half:] + far_y, across_x)
+    y_a = swap(near_mine[1, :half] + near_got[1, :half] + far_x, across_y)
+
+    need, own, g_inverse = invert_factors(scales, got.reshape(-1, got.shape[-1]))
+    needs = [need] + [shift(need, by) for by in range(1, depth)]
+    owns = [own] + [shift(own, by) for by in range(1, depth)]
+    order = jnp.stack([(z - by) % depth for by in range(depth)]).astype(jnp.int32)
+    return finish(order, (self_mine, self_got, x_a, x_b, y_a, y_b, g_inverse), needs, owns)
+
+
 def solution(mesh):
+    def per_device(activations, cotangent, sampled_rows, block_owner):
+        block_total = activations.shape[1] // FACTOR_BLOCK
+        dp_count, depth = mesh.shape["dp"], mesh.shape["tensor"]
+        fits = (
+            dp_count == 8
+            and block_total == dp_count * depth
+            and cotangent.shape[1] == FACTOR_BLOCK
+            and sampled_rows.shape[0] % 16 == 0
+            and activations.shape[0] % 128 == 0
+        )
+        run = square_device if fits else general_device
+        return run(activations, cotangent, sampled_rows, block_owner)
+
     return jax.shard_map(
         per_device,
         mesh=mesh,

time: 220 us -> 136 us (0.62)
  matrix products: 68.9 us -> 0 us
  waiting for transfers between devices: 108 us -> 39.1 us
  Pallas kernels: 0 us -> 40.9 us
  starting transfers between devices: 5.49 us -> 30.4 us
  between operations: 14.6 us -> 1.4 us
    dot_general x47 -> x0, matrix products: 68.9 us -> none  [the longest x20 25 us: advance(): jnp.einsum('nij,njk->nik', current, 2.0 * identity[None, :, :] - product,...]
    all_gather x1 -> x0, waiting for transfers between devices: 54.6 us -> none  [per_device(): shard_piece = lax.all_gather(owned_out, 'dp', axis=0, tiled=True)]
    pallas_call x0 -> x6, Pallas kernels: none -> 40.9 us  [the longest x3 15.7 us: partial_grads(): pl.pallas_call(grad_body, out_shape=(one, one), grid_spec=pltpu.PrefetchS...]
    reduce_scatter x1 -> x0, waiting for transfers between devices: 39.6 us -> none  [per_device(): lax.psum_scatter(lax.dot_general(activations, cotangent, (((0,), (0,)), (...]
    ppermute x0 -> x15, waiting for transfers between devices: none -> 38.5 us  [the longest x6 19.8 us: shift(): lax.ppermute(block, 'tensor', [(i, (i + by) % depth) for i in range(depth)])]
    ppermute x0 -> x15, starting transfers between devices: none -> 25.2 us  [the longest x6 18.3 us: shift(): lax.ppermute(block, 'tensor', [(i, (i + by) % depth) for i in range(depth)])]
    unnamed x6 -> x50, local copies, waits for them, and re-layouts: 0.6 us -> 14.1 us
    all_to_all x1, waiting for transfers between devices: 13.9 us -> 0.64 us  [square_device(): got = lax.all_to_all(picked, 'dp', split_axis=0, concat_axis=0, tiled=True)]
  transfers between devices with their start and end apart: 4 -> 16, of which waited for: 3 -> 7; matrix products, arithmetic and copies ran while one was open for 34% -> 7% of each run, Pallas kernels for 0% -> 23%
where the time goes in v1:
time: 136 us; the launch traced here: 135 us
  Pallas kernels  40.9 us (30%)
  waiting for transfers between devices  39.1 us (29%)
  starting transfers between devices  30.4 us (22%)
  local copies, waits for them, and re-layouts  15 us (11%)
  other arithmetic  8.51 us (6%)
  between operations  1.4 us (1%)
    ppermute x6, waiting for transfers between devices, shift(): lax.ppermute(block, 'tensor', [(i, (i + by) % depth) for i in range(depth)])  19.8 us
    ppermute x9, waiting for transfers between devices, swap(): return lax.ppermute(block, 'dp', [(i, i ^ bit) for i in range(dp_count)])  18.7 us
    ppermute x6, starting transfers between devices, shift(): lax.ppermute(block, 'tensor', [(i, (i + by) % depth) for i in range(depth)])  18.3 us
    pallas_call x3, Pallas kernels, partial_grads(): pl.pallas_call(grad_body, out_shape=(one, one), grid_spec=pltpu.PrefetchS...  15.7 us
    unnamed x50, local copies, waits for them, and re-layouts  14.1 us
    pallas_call x1, Pallas kernels, invert_factors(): pl.pallas_call(invert_body, out_shape=(one, one, one), in_specs=[pl.Block...  13.8 us
    ppermute x9, starting transfers between devices, swap(): return lax.ppermute(block, 'dp', [(i, i ^ bit) for i in range(dp_count)])  6.92 us
    pallas_call x1, Pallas kernels, pick_rows(): pl.pallas_call(pick_body, out_shape=jax.ShapeDtypeStruct((count // 2, sam...  6.56 us
  transfers between devices with their start and end apart: 16, of which 7 were waited for; matrix products, arithmetic and copies ran while one was open for 7% of the time, Pallas kernels for 23%

profile of v1, /device:TPU:0, one launch (start us, length us, event | category | flops | bytes accessed | tf_op | source)
XLA Modules:
  0.0 135.4 jit_solution(8359179224661119307)
XLA Ops:
  0.6 0.1 pad_add_fusion.4.ids
  0.7 1.0 copy-done
  1.7 4.4 %partial_grads.5 = (f32[1,256,1024]{2,1,0:T(8,128)}, f32[1,256,1024]{2,1,0:T(8,128)S(1)}) custom-call(s32[2]{0:T(128)S(1)} %pad_add_fusion.4.ids, bf16[768,256]{1,0:T(8,128)(2,1)S(1)} %copy-done, bf16[768,8192]{1,0:T(8,128)(2,1)} %act_ref.7), custom_call_target="tpu_custom_call" | custom-call | flops 805306368 | bytes 5242880 | tf_op jit(solution)/shard_map/partial_grads/pallas_call | solution.py:216
  6.1 0.5 collective-permute-start.3
  6.6 0.1 pad_add_fusion.3.ids
  6.6 6.9 %partial_grads.4 = (f32[2,256,1024]{2,1,0:T(8,128)}, f32[2,256,1024]{2,1,0:T(8,128)S(1)}) custom-call(s32[4]{0:T(128)S(1)} %pad_add_fusion.3.ids, bf16[768,256]{1,0:T(8,128)(2,1)S(1)} %copy-done.1, bf16[768,8192]{1,0:T(8,128)(2,1)} %act_ref.7), custom_call_target="tpu_custom_call" | custom-call | flops 1610612736 | bytes 10485760 | tf_op jit(solution)/shard_map/partial_grads/pallas_call | solution.py:216
  13.5 0.1 collective-permute-start.1
  13.6 0.2 convert_reduce_fusion
  13.8 0.6 multiply_add_fusion.1
  14.4 0.2 select_reduce_fusion
  14.6 0.1 copy.10
  14.7 0.1 reshape.30.ids
  14.8 0.7 copy.11.rows_ref
  15.5 0.8 copy-done.22
  16.3 6.6 %pick_rows.1 = bf16[8,64,768]{2,1,0:T(8,128)(2,1)} custom-call(s32[16]{0:T(128)S(1)} %reshape.30.ids, s32[64,1]{1,0:T(8,128)S(1)} %copy-done.22, bf16[768,256]{1,0:T(8,128)(2,1)S(1)} %copy-done.1, bf16[768,8192]{1,0:T(8,128)(2,1)} %act_ref.7), custom_call_target="tpu_custom_call" | custom-call | flops 402653184 | bytes 6291456 | tf_op jit(solution)/shard_map/pick_rows/pallas_call | solution.py:167
  22.8 5.2 %all-to-all-start = ((bf16[8,64,768]{2,1,0:T(8,128)(2,1)}), bf16[8,64,768]{2,1,0:T(8,128)(2,1)}, u32[]{:S(2)}, u32[]{:S(2)}) async-start(bf16[8,64,768]{2,1,0:T(8,128)(2,1)} %pick_rows.1), calls=%async_computation | async-start | bytes 1572864 | tf_op jit(solution)/shard_map/all_to_all | solution.py:387
  28.0 0.1 pad_add_fusion.2.ids
  28.1 4.4 %partial_grads.3 = (f32[1,256,1024]{2,1,0:T(8,128)}, f32[1,256,1024]{2,1,0:T(8,128)S(1)}) custom-call(s32[2]{0:T(128)S(1)} %pad_add_fusion.2.ids, bf16[768,256]{1,0:T(8,128)(2,1)S(1)} %copy-done.1, bf16[768,8192]{1,0:T(8,128)(2,1)} %act_ref.7), custom_call_target="tpu_custom_call" | custom-call | flops 805306368 | bytes 5242880 | tf_op jit(solution)/shard_map/partial_grads/pallas_call | solution.py:216
  32.5 1.0 copy-done.2
  33.5 0.5 collective-permute-start
  34.6 0.1 pad_maximum_fusion.scales
  34.7 0.0 collective-permute-done.3
  34.7 2.3 %fusion.1 = (f32[128,1024]{1,0:T(8,128)}, f32[128,1024]{1,0:T(8,128)}) fusion(f32[1,256,1024]{2,1,0:T(8,128)} %collective-permute-done.3, f32[1,256,1024]{2,1,0:T(8,128)S(1)} %get-tuple-element.15), kind=kLoop, calls=%fused_computation.3 | loop fusion | flops 262144 | bytes 3145728 | tf_op jit(solution)/shard_map/add | solution.py:389
  37.0 1.7 %collective-permute-start.4 = (f32[128,1024]{1,0:T(8,128)}, f32[128,1024]{1,0:T(8,128)S(1)}, u32[]{:S(2)}, u32[]{:S(2)}) collective-permute-start(f32[128,1024]{1,0:T(8,128)} %get-tuple-element.25), channel_id=1, source_target_pairs={{0,16},{4,20},{8,24},{12,28},{16,0},{20,4},{24,8},{28,12},{1,17},{... | collective-permute-start | bytes 1572872 | tf_op jit(solution)/shard_map/ppermute | solution.py:355
  38.7 1.5 %collective-permute-start.6 = (f32[128,1024]{1,0:T(8,128)}, f32[128,1024]{1,0:T(8,128)S(1)}, u32[]{:S(2)}, u32[]{:S(2)}) collective-permute-start(f32[128,1024]{1,0:T(8,128)} %get-tuple-element.24), channel_id=1, source_target_pairs={{0,8},{4,12},{8,0},{12,4},{16,24},{20,28},{24,16},{28,20},{1,9},{5... | collective-permute-start | bytes 1572872 | tf_op jit(solution)/shard_map/ppermute | solution.py:355
  40.1 0.6 all-to-all-done
  40.8 13.8 %invert_factors.1 = (f32[256,256]{1,0:T(8,128)S(1)}, f32[256,256]{1,0:T(8,128)S(1)}, f32[256,256]{1,0:T(8,128)S(1)}) custom-call(f32[4]{0:T(128)S(1)} %pad_maximum_fusion.scales, bf16[512,768]{1,0:T(8,128)(2,1)} %bitcast.21.rows_ref), custom_call_target="tpu_custom_call" | custom-call | flops 11475615744 | bytes 2097152 | tf_op jit(solution)/shard_map/invert_factors/pallas_call | solution.py:284
  54.7 3.1 %collective-permute-start.10 = (f32[256,256]{1,0:T(8,128)S(1)}, f32[256,256]{1,0:T(8,128)S(1)}, u32[]{:S(2)}, u32[]{:S(2)}) collective-permute-start(f32[256,256]{1,0:T(8,128)S(1)} %get-tuple-element.18.refs_7_), channel_id=1, source_target_pairs={{0,2},{1,3},{2,0},{3,1},{4,6},{5,7},{6,4},{7,5},{8,10},{9,11},{10,... | collective-permute-start | bytes 786440 | tf_op jit(solution)/shard_map/ppermute | solution.py:358
  57.7 0.0 collective-permute-done.4
  57.7 1.3 collective-permute-start.11
  59.1 0.7 collective-permute-start.12
  59.8 0.0 collective-permute-done.1
  59.8 1.1 collective-permute-start.13
  60.8 2.5 %fusion.3 = (f32[128,1024]{1,0:T(8,128)}, f32[128,1024]{1,0:T(8,128)}) fusion(f32[128,1024]{1,0:T(8,128)S(1)} %collective-permute-done.6, f32[2,256,1024]{2,1,0:T(8,128)} %collective-permute-done.1, f32[2,256,1024]{2,1,0:T(8,128)S(1)} %get-tuple-element.13, f32[128,1024]{1,0:T(8,128)S(1)} %collective-permute-done.4), kind=kLoop, calls=%fused_computation.6 | loop fusion | flops 524288 | bytes 4194304 | tf_op jit(solution)/shard_map/add | solution.py:400
  63.3 17.8 %collective-permute-done.10.refs_9_ = f32[256,256]{1,0:T(8,128)S(1)} collective-permute-done((f32[256,256]{1,0:T(8,128)S(1)}, f32[256,256]{1,0:T(8,128)S(1)}, u32[]{:S(2)}, u32[]{:S(2)}) %collective-permute-start.10) | collective-permute-done | bytes 262176 | tf_op jit(solution)/shard_map/ppermute | solution.py:358
  81.1 0.0 collective-permute-start.14
  81.1 12.1 %collective-permute-start.9 = (f32[256,256]{1,0:T(8,128)S(1)}, f32[256,256]{1,0:T(8,128)S(1)}, u32[]{:S(2)}, u32[]{:S(2)}) collective-permute-start(f32[256,256]{1,0:T(8,128)S(1)} %get-tuple-element.18.refs_7_), channel_id=1, source_target_pairs={{0,1},{1,2},{2,3},{3,0},{4,5},{5,6},{6,7},{7,4},{8,9},{9,10},{10,1... | collective-permute-start | bytes 786440 | tf_op jit(solution)/shard_map/ppermute | solution.py:358
  93.3 2.3 %fusion = (f32[128,1024]{1,0:T(8,128)}, f32[128,1024]{1,0:T(8,128)}) fusion(f32[2,256,1024]{2,1,0:T(8,128)} %collective-permute-done.1, f32[2,256,1024]{2,1,0:T(8,128)S(1)} %get-tuple-element.13), kind=kLoop, calls=%fused_computation.1 | loop fusion | flops 262144 | bytes 3145728 | tf_op jit(solution)/shard_map/add | solution.py:398
  95.6 0.0 collective-permute-done.12.refs_12_
  95.6 0.7 copy-done.14
  96.3 0.0 collective-permute-start.5
  96.3 2.0 %collective-permute-done.13.refs_13_ = f32[256,256]{1,0:T(8,128)S(1)} collective-permute-done((f32[256,256]{1,0:T(8,128)S(1)}, f32[256,256]{1,0:T(8,128)S(1)}, u32[]{:S(2)}, u32[]{:S(2)}) %collective-permute-start.13) | collective-permute-done | bytes 262176 | tf_op jit(solution)/shard_map/ppermute | solution.py:358
  98.3 0.7 copy-done.16
  99.0 0.5 collective-permute-start.7
  99.6 0.7 copy-done.18
  100.3 0.8 collective-permute-start.2
  101.1 0.7 copy-done.20
  101.8 1.4 %collective-permute-start.8 = (f32[128,1024]{1,0:T(8,128)}, f32[128,1024]{1,0:T(8,128)S(1)}, u32[]{:S(2)}, u32[]{:S(2)}) collective-permute-start(f32[128,1024]{1,0:T(8,128)} %get-tuple-element.20), channel_id=1, source_target_pairs={{0,16},{4,20},{8,24},{12,28},{16,0},{20,4},{24,8},{28,12},{1,17},{... | collective-permute-start | bytes 1572872 | tf_op jit(solution)/shard_map/ppermute | solution.py:355
  103.2 0.1 pad_add_fusion.1.order
  103.3 0.0 collective-permute-done.refs_1_
  103.3 7.7 %collective-permute-done.5.refs_3_ = f32[128,1024]{1,0:T(8,128)S(1)} collective-permute-done((f32[128,1024]{1,0:T(8,128)}, f32[128,1024]{1,0:T(8,128)S(1)}, u32[]{:S(2)}, u32[]{:S(2)}) %collective-permute-start.5) | collective-permute-done | bytes 524320 | tf_op jit(solution)/shard_map/ppermute | solution.py:355
  111.0 3.1 %collective-permute-done.7.refs_4_ = f32[128,1024]{1,0:T(8,128)S(1)} collective-permute-done((f32[128,1024]{1,0:T(8,128)}, f32[128,1024]{1,0:T(8,128)S(1)}, u32[]{:S(2)}, u32[]{:S(2)}) %collective-permute-start.7) | collective-permute-done | bytes 524320 | tf_op jit(solution)/shard_map/ppermute | solution.py:355
  114.1 2.8 %collective-permute-done.2.refs_2_ = f32[128,1024]{1,0:T(8,128)S(1)} collective-permute-done((f32[128,1024]{1,0:T(8,128)}, f32[128,1024]{1,0:T(8,128)S(1)}, u32[]{:S(2)}, u32[]{:S(2)}) %collective-permute-start.2) | collective-permute-done | bytes 524320 | tf_op jit(solution)/shard_map/ppermute | solution.py:355
  116.9 5.0 %collective-permute-done.8.refs_5_ = f32[128,1024]{1,0:T(8,128)S(1)} collective-permute-done((f32[128,1024]{1,0:T(8,128)}, f32[128,1024]{1,0:T(8,128)S(1)}, u32[]{:S(2)}, u32[]{:S(2)}) %collective-permute-start.8) | collective-permute-done | bytes 524320 | tf_op jit(solution)/shard_map/ppermute | solution.py:355
  122.0 0.9 copy-done.5
  122.9 0.9 copy-done.7
  123.9 0.9 copy-done.9
  124.8 0.9 copy-done.11
  125.8 0.9 copy-done.13
  126.7 0.9 copy-done.15
  127.7 0.9 copy-done.17
  128.6 0.9 copy-done.19
  129.6 0.9 copy-done.21
  130.5 4.8 %finish.1 = (f32[1024,256]{1,0:T(8,128)}, f32[4,256,256]{2,1,0:T(8,128)}) custom-call(s32[4]{0:T(128)S(1)} %pad_add_fusion.1.order, f32[1,256,1024]{2,1,0:T(8,128)S(1)} %copy-done.3, f32[1,256,1024]{2,1,0:T(8,128)} %collective-permute-done.refs_1_, f32[128,1024]{1,0:T(8,128)S(1)} %collective-permute-done.2.refs_2_, ...), custom_call_target="tpu_custom_call" | custom-call | flops 1610612736 | bytes 9437184 | tf_op jit(solution)/shard_map/finish/pallas_call | solution.py:325
  (42 shorter events, 0.1 us)
Async XLA Ops:
  0.7 1.0 copy-start
  1.7 4.9 %copy-start.1 = (bf16[768,256]{1,0:T(8,128)(2,1)S(1)}, bf16[768,256]{1,0:T(8,128)(2,1)}, u32[]{:S(2)}) copy-start(bf16[768,256]{1,0:T(8,128)(2,1)} %cot_ref.7) | copy-start | bytes 1179652
  6.1 28.6 %collective-permute-start.3 = (f32[1,256,1024]{2,1,0:T(8,128)}, f32[1,256,1024]{2,1,0:T(8,128)}, u32[]{:S(2)}, u32[]{:S(2)}) collective-permute-start(f32[1,256,1024]{2,1,0:T(8,128)} %get-tuple-element.16), channel_id=1, source_target_pairs={{0,4},{4,0},{8,12},{12,8},{16,20},{20,16},{24,28},{28,24},{1,5},{5... | collective-permute-start | bytes 3145736 | tf_op jit(solution)/shard_map/ppermute | solution.py:355
  6.6 7.0 %copy-start.24 = (s32[32]{0:T(128)S(1)}, s32[32]{0:T(128)}, u32[]{:S(2)}) copy-start(s32[32]{0:T(128)} %param.7) | copy-start | bytes 388
  6.6 8.2 %copy-start.23 = (s32[64]{0:T(128)S(1)}, s32[64]{0:T(128)}, u32[]{:S(2)}) copy-start(s32[64]{0:T(128)} %param.6) | copy-start | bytes 772
  13.5 46.2 %collective-permute-start.1 = (f32[2,256,1024]{2,1,0:T(8,128)}, f32[2,256,1024]{2,1,0:T(8,128)}, u32[]{:S(2)}, u32[]{:S(2)}) collective-permute-start(f32[2,256,1024]{2,1,0:T(8,128)} %get-tuple-element.14), channel_id=1, source_target_pairs={{0,4},{4,0},{8,12},{12,8},{16,20},{20,16},{24,28},{28,24},{1,5},{5... | collective-permute-start | bytes 6291464 | tf_op jit(solution)/shard_map/ppermute | solution.py:355
  15.5 0.8 copy-start.22
  22.8 17.9 %all-to-all-start = ((bf16[8,64,768]{2,1,0:T(8,128)(2,1)}), bf16[8,64,768]{2,1,0:T(8,128)(2,1)}, u32[]{:S(2)}, u32[]{:S(2)}) async-start(bf16[8,64,768]{2,1,0:T(8,128)(2,1)} %pick_rows.1), calls=%async_computation | async-start | bytes 1572864 | tf_op jit(solution)/shard_map/all_to_all | solution.py:387
  32.5 1.0 copy-start.2
  33.5 69.8 %collective-permute-start = (f32[1,256,1024]{2,1,0:T(8,128)}, f32[1,256,1024]{2,1,0:T(8,128)}, u32[]{:S(2)}, u32[]{:S(2)}) collective-permute-start(f32[1,256,1024]{2,1,0:T(8,128)} %get-tuple-element.12), channel_id=1, source_target_pairs={{0,4},{4,0},{8,12},{12,8},{16,20},{20,16},{24,28},{28,24},{1,5},{5... | collective-permute-start | bytes 3145736 | tf_op jit(solution)/shard_map/ppermute | solution.py:355
  37.0 20.7 %collective-permute-start.4 = (f32[128,1024]{1,0:T(8,128)}, f32[128,1024]{1,0:T(8,128)S(1)}, u32[]{:S(2)}, u32[]{:S(2)}) collective-permute-start(f32[128,1024]{1,0:T(8,128)} %get-tuple-element.25), channel_id=1, source_target_pairs={{0,16},{4,20},{8,24},{12,28},{16,0},{20,4},{24,8},{28,12},{1,17},{... | collective-permute-start | bytes 1572872 | tf_op jit(solution)/shard_map/ppermute | solution.py:355
  38.7 20.4 %collective-permute-start.6 = (f32[128,1024]{1,0:T(8,128)}, f32[128,1024]{1,0:T(8,128)S(1)}, u32[]{:S(2)}, u32[]{:S(2)}) collective-permute-start(f32[128,1024]{1,0:T(8,128)} %get-tuple-element.24), channel_id=1, source_target_pairs={{0,8},{4,12},{8,0},{12,4},{16,24},{20,28},{24,16},{28,20},{1,9},{5... | collective-permute-start | bytes 1572872 | tf_op jit(solution)/shard_map/ppermute | solution.py:355
  54.6 8.7 %copy-start.8 = (f32[256,256]{1,0:T(8,128)}, f32[256,256]{1,0:T(8,128)S(1)}, u32[]{:S(2)}) copy-start(f32[256,256]{1,0:T(8,128)S(1)} %get-tuple-element.17.refs_6_) | copy-start | bytes 786436
  54.6 26.4 %copy-start.6 = (f32[256,256]{1,0:T(8,128)}, f32[256,256]{1,0:T(8,128)S(1)}, u32[]{:S(2)}) copy-start(f32[256,256]{1,0:T(8,128)S(1)} %get-tuple-element.19.refs_11_) | copy-start | bytes 786436
  54.7 26.5 %copy-start.4 = (f32[256,256]{1,0:T(8,128)}, f32[256,256]{1,0:T(8,128)S(1)}, u32[]{:S(2)}) copy-start(f32[256,256]{1,0:T(8,128)S(1)} %get-tuple-element.18.refs_7_) | copy-start | bytes 786436
  54.7 26.4 %collective-permute-start.10 = (f32[256,256]{1,0:T(8,128)S(1)}, f32[256,256]{1,0:T(8,128)S(1)}, u32[]{:S(2)}, u32[]{:S(2)}) collective-permute-start(f32[256,256]{1,0:T(8,128)S(1)} %get-tuple-element.18.refs_7_), channel_id=1, source_target_pairs={{0,2},{1,3},{2,0},{3,1},{4,6},{5,7},{6,4},{7,5},{8,10},{9,11},{10,... | collective-permute-start | bytes 786440 | tf_op jit(solution)/shard_map/ppermute | solution.py:358
  57.7 23.4 %collective-permute-start.11 = (f32[256,256]{1,0:T(8,128)S(1)}, f32[256,256]{1,0:T(8,128)S(1)}, u32[]{:S(2)}, u32[]{:S(2)}) collective-permute-start(f32[256,256]{1,0:T(8,128)S(1)} %get-tuple-element.18.refs_7_), channel_id=1, source_target_pairs={{0,3},{1,0},{2,1},{3,2},{4,7},{5,4},{6,5},{7,6},{8,11},{9,8},{10,9... | collective-permute-start | bytes 786440 | tf_op jit(solution)/shard_map/ppermute | solution.py:358
  59.1 36.5 %collective-permute-start.12 = (f32[256,256]{1,0:T(8,128)S(1)}, f32[256,256]{1,0:T(8,128)S(1)}, u32[]{:S(2)}, u32[]{:S(2)}) collective-permute-start(f32[256,256]{1,0:T(8,128)S(1)} %get-tuple-element.19.refs_11_), channel_id=1, source_target_pairs={{0,1},{1,2},{2,3},{3,0},{4,5},{5,6},{6,7},{7,4},{8,9},{9,10},{10,1... | collective-permute-start | bytes 786440 | tf_op jit(solution)/shard_map/ppermute | solution.py:358
  59.8 38.6 %collective-permute-start.13 = (f32[256,256]{1,0:T(8,128)S(1)}, f32[256,256]{1,0:T(8,128)S(1)}, u32[]{:S(2)}, u32[]{:S(2)}) collective-permute-start(f32[256,256]{1,0:T(8,128)S(1)} %get-tuple-element.19.refs_11_), channel_id=1, source_target_pairs={{0,2},{1,3},{2,0},{3,1},{4,6},{5,7},{6,4},{7,5},{8,10},{9,11},{10,... | collective-permute-start | bytes 786440 | tf_op jit(solution)/shard_map/ppermute | solution.py:358
  63.3 58.7 %copy-start.3 = (f32[1,256,1024]{2,1,0:T(8,128)S(1)}, f32[1,256,1024]{2,1,0:T(8,128)}, u32[]{:S(2)}) copy-start(f32[1,256,1024]{2,1,0:T(8,128)} %copy-done.2) | copy-start | bytes 3145732
  81.1 20.0 %copy-start.10 = (f32[256,256]{1,0:T(8,128)}, f32[256,256]{1,0:T(8,128)S(1)}, u32[]{:S(2)}) copy-start(f32[256,256]{1,0:T(8,128)S(1)} %collective-permute-done.10.refs_9_) | copy-start | bytes 786436
  81.1 18.5 %collective-permute-start.14 = (f32[256,256]{1,0:T(8,128)S(1)}, f32[256,256]{1,0:T(8,128)S(1)}, u32[]{:S(2)}, u32[]{:S(2)}) collective-permute-start(f32[256,256]{1,0:T(8,128)S(1)} %get-tuple-element.19.refs_11_), channel_id=1, source_target_pairs={{0,3},{1,0},{2,1},{3,2},{4,7},{5,4},{6,5},{7,6},{8,11},{9,8},{10,9... | collective-permute-start | bytes 786440 | tf_op jit(solution)/shard_map/ppermute | solution.py:358
  81.1 20.7 %copy-start.12 = (f32[256,256]{1,0:T(8,128)}, f32[256,256]{1,0:T(8,128)S(1)}, u32[]{:S(2)}) copy-start(f32[256,256]{1,0:T(8,128)S(1)} %collective-permute-done.11.refs_10_) | copy-start | bytes 786436
  81.1 20.0 %collective-permute-start.9 = (f32[256,256]{1,0:T(8,128)S(1)}, f32[256,256]{1,0:T(8,128)S(1)}, u32[]{:S(2)}, u32[]{:S(2)}) collective-permute-start(f32[256,256]{1,0:T(8,128)S(1)} %get-tuple-element.18.refs_7_), channel_id=1, source_target_pairs={{0,1},{1,2},{2,3},{3,0},{4,5},{5,6},{6,7},{7,4},{8,9},{9,10},{10,1... | collective-permute-start | bytes 786440 | tf_op jit(solution)/shard_map/ppermute | solution.py:358
  95.6 0.7 copy-start.14
  96.3 14.7 %collective-permute-start.5 = (f32[128,1024]{1,0:T(8,128)}, f32[128,1024]{1,0:T(8,128)S(1)}, u32[]{:S(2)}, u32[]{:S(2)}) collective-permute-start(f32[128,1024]{1,0:T(8,128)} %get-tuple-element.23), channel_id=1, source_target_pairs={{0,8},{4,12},{8,0},{12,4},{16,24},{20,28},{24,16},{28,20},{1,9},{5... | collective-permute-start | bytes 1572872 | tf_op jit(solution)/shard_map/ppermute | solution.py:355
  98.3 0.7 copy-start.16
  99.0 15.1 %collective-permute-start.7 = (f32[128,1024]{1,0:T(8,128)}, f32[128,1024]{1,0:T(8,128)S(1)}, u32[]{:S(2)}, u32[]{:S(2)}) collective-permute-start(f32[128,1024]{1,0:T(8,128)} %get-tuple-element.22), channel_id=1, source_target_pairs={{0,16},{4,20},{8,24},{12,28},{16,0},{20,4},{24,8},{28,12},{1,17},{... | collective-permute-start | bytes 1572872 | tf_op jit(solution)/shard_map/ppermute | solution.py:355
  99.6 0.7 copy-start.18
  100.3 16.7 %collective-permute-start.2 = (f32[128,1024]{1,0:T(8,128)}, f32[128,1024]{1,0:T(8,128)S(1)}, u32[]{:S(2)}, u32[]{:S(2)}) collective-permute-start(f32[128,1024]{1,0:T(8,128)} %get-tuple-element.21), channel_id=1, source_target_pairs={{0,8},{4,12},{8,0},{12,4},{16,24},{20,28},{24,16},{28,20},{1,9},{5... | collective-permute-start | bytes 1572872 | tf_op jit(solution)/shard_map/ppermute | solution.py:355
  101.1 0.7 copy-start.20
  101.8 20.1 %collective-permute-start.8 = (f32[128,1024]{1,0:T(8,128)}, f32[128,1024]{1,0:T(8,128)S(1)}, u32[]{:S(2)}, u32[]{:S(2)}) collective-permute-start(f32[128,1024]{1,0:T(8,128)} %get-tuple-element.20), channel_id=1, source_target_pairs={{0,16},{4,20},{8,24},{12,28},{16,0},{20,4},{24,8},{28,12},{1,17},{... | collective-permute-start | bytes 1572872 | tf_op jit(solution)/shard_map/ppermute | solution.py:355
  122.0 1.0 copy-start.5
  122.9 0.9 copy-start.7
  123.9 0.9 copy-start.9
  124.8 0.9 copy-start.11
  125.8 0.9 copy-start.13
  126.7 0.9 copy-start.15
  127.7 0.9 copy-start.17
  128.6 0.9 copy-start.19
  129.6 0.9 copy-start.21

commit v2 on v0

--- a/solution.py
+++ b/solution.py
@@ -1,6 +1,10 @@
+import functools
+
 import jax
 import jax.numpy as jnp
 from jax import lax
+from jax.experimental import pallas as pl
+from jax.experimental.pallas import tpu as pltpu
 from jax.sharding import PartitionSpec as P
 
 S_DEV = 64
@@ -10,6 +14,16 @@
 
 DAMPING = 0.05
 precise_mode = lax.Precision.HIGHEST
+f32 = jnp.float32
+bf16 = jnp.bfloat16
+
+
+def block_rank(block_owner):
+    block_total = block_owner.shape[0]
+    same_owner = block_owner[:, None] == block_owner[None, :]
+    positions = jnp.arange(block_total, dtype=jnp.int32)
+    before = positions[None, :] < positions[:, None]
+    return jnp.sum((same_owner & before).astype(jnp.int32), axis=1)
 
 
 def from_partner(block, axis, apart):
@@ -37,19 +51,11 @@
     return lax.fori_loop(0, ITERS, advance, initial)
 
 
-def block_rank(block_owner):
-    block_total = block_owner.shape[0]
-    same_owner = block_owner[:, None] == block_owner[None, :]
-    positions = jnp.arange(block_total, dtype=jnp.int32)
-    before = positions[None, :] < positions[:, None]
-    return jnp.sum((same_owner & before).astype(jnp.int32), axis=1)
-
-
 def owner_grams(received):
     return jnp.einsum("pcsk,pcsl->ckl", received, received, preferred_element_type=jnp.float32)
 
 
-def per_device(activations, cotangent, sampled_rows, block_owner):
+def general_device(activations, cotangent, sampled_rows, block_owner):
     tok_local = activations.shape[0]
     model_width = activations.shape[1]
     group_w = cotangent.shape[1]
@@ -122,7 +128,481 @@
     return (natural_step.reshape(row_share, group_w), owned_out)
 
 
+MIB = 1 << 20
+VMEM_MIB = 63
+AHEAD = 3
+PREPARE_FLOPS = 20_000_000_000
+ANY = pl.BlockSpec(memory_space=pl.ANY)
+VMEM = pl.BlockSpec(memory_space=pltpu.VMEM)
+SMEM = pl.BlockSpec(memory_space=pltpu.SMEM)
+CORE, NEAR_X, NEAR_Y, FAR = 1, 2, 4, 6
+MASKS = (FAR, NEAR_X, NEAR_Y, 0)
+
+
+def shaped(shape, dtype=f32):
+    return jax.ShapeDtypeStruct(shape, dtype)
+
+
+def call(body, name, out_shape, in_specs, out_specs, scratch=(), flops=0, moved=0):
+    return pl.pallas_call(
+        body,
+        out_shape=out_shape,
+        in_specs=in_specs,
+        out_specs=out_specs,
+        scratch_shapes=scratch,
+        compiler_params=pltpu.CompilerParams(vmem_limit_bytes=VMEM_MIB * MIB),
+        cost_estimate=pl.CostEstimate(flops=flops, bytes_accessed=moved, transcendentals=0),
+        name=name,
+    )
+
+
+def start_all(sources, targets, sems, first=0):
+    copies = [
+        pltpu.make_async_copy(source, target, sems.at[first + i])
+        for i, (source, target) in enumerate(zip(sources, targets))
+    ]
+    for copy in copies:
+        copy.start()
+    return copies
+
+
+def fold_rows(rows):
+    return rows + rows // 2
+
+
+def encode(x, into):
+    rows = x.shape[0]
+    high = x.astype(bf16)
+    into[:rows] = high
+    base = high.astype(f32)
+    left = (x - base) * pl.reciprocal(base, approx=True) * 256.0
+    left = jnp.where(jnp.abs(base) < 1e-30, 0.0, jnp.clip(left, -1.0, 1.0))
+    digit = jnp.floor(left * 63.5 + 64.0)
+    first, second = digit[: rows // 2], digit[rows // 2 :]
+    negative = second >= 64.0
+    power = jnp.exp2(jnp.where(negative, second - 96.0, second - 32.0))
+    packed = (first + 128.0) * power
+    into[rows:] = jnp.where(negative, -packed, packed).astype(bf16)
+
+
+def decode(ref):
+    rows = ref.shape[0] * 2 // 3
+    packed = ref[rows:].astype(f32)
+    size = jnp.abs(packed)
+    power = jnp.floor(jnp.log2(size) + 1e-3)
+    first = jnp.floor(size * jnp.exp2(7.0 - power) + 0.5) - 128.0
+    second = power + jnp.where(packed < 0.0, 89.0, 25.0)
+    digit = jnp.concatenate([first, second], axis=0)
+    base = ref[:rows].astype(f32)
+    return base + base * ((digit - 63.5) * (1.0 / (63.5 * 256.0)))
+
+
+def project_body(
+    owner, rows_ref, cot_ref, act_ref, theirs, own_theirs, out_ref,
+    held, cot, rows, left, grads, picks, slots, sems, out_sems, small_sems,
+):
+    count, tokens, share = held.shape
+    group_w = cot.shape[1]
+    samples = rows.shape[1]
+    per_tile = share // FACTOR_BLOCK
+    me = lax.axis_index("dp")
+    z = lax.axis_index("tensor")
+    half = count // 2
+    tiles = [me ^ m ^ CORE for m in MASKS] + [me ^ m for m in MASKS]
+    targets = [theirs.at[i] for i in range(half - 1)] + [own_theirs.at[0]]
+
+    small = start_all([cot_ref, rows_ref], [cot, rows], small_sems)
+    starts = [pl.multiple_of(t * share, share) for t in tiles]
+    loads = [
+        pltpu.make_async_copy(act_ref.at[:, pl.ds(start, share)], held.at[i], sems.at[i])
+        for i, start in enumerate(starts)
+    ]
+    for load in loads[:AHEAD]:
+        load.start()
+
+    for d in range(count):
+        slots[0, d] = 0
+        slots[1, d] = 0
+    for b in range(owner.shape[0]):
+        holder = owner[b]
+        rank = slots[0, holder]
+        slots[0, holder] = rank + 1
+        slots[1, holder] = jnp.where(rank == z, b, slots[1, holder])
+
+    for copy in small:
+        copy.wait()
+    left[:group_w] = cot[...].astype(f32).T.astype(bf16)
+    places = lax.broadcasted_iota(jnp.int32, (tokens, samples), 0)
+    left[group_w:] = (places == rows[...]).astype(f32).T.astype(bf16)
+
+    stores = []
+    for i in range(count):
+        loads[i].wait()
+        if i + AHEAD < count:
+            loads[i + AHEAD].start()
+        if i < half:
+            product = jnp.dot(left[...], held[i], preferred_element_type=f32)
+            grads[i] = product[:group_w]
+            stores += start_all([grads.at[i]], [targets[i]], out_sems, i)
+            picked = product[group_w:]
+        else:
+            picked = jnp.dot(left[group_w:], held[i], preferred_element_type=f32)
+        for j in range(per_tile):
+            picks[tiles[i] * per_tile + j] = picked[
+                :, j * FACTOR_BLOCK : (j + 1) * FACTOR_BLOCK
+            ].astype(bf16)
+    picked_cot = jnp.dot(left[group_w:], cot[...], preferred_element_type=f32).astype(bf16)
+    for d in range(count):
+        first = d * per_tile + 2 * (z % 2)
+        for j, block in enumerate((first, first + 1, slots[1, d])):
+            out_ref[d, :, j * FACTOR_BLOCK : (j + 1) * FACTOR_BLOCK] = picks[block]
+        out_ref[d, :, 3 * FACTOR_BLOCK :] = picked_cot
+    for store in stores:
+        store.wait()
+
+
+def project(block_owner, sampled_rows, cotangent, activations, count):
+    samples = sampled_rows.shape[0]
+    tokens, group_w = cotangent.shape
+    model_width = activations.shape[1]
+    share = model_width // count
+    one = shaped((1, group_w, share))
+    rest = shaped((count // 2 - 1, group_w, share))
+    return call(
+        project_body,
+        "project",
+        (rest, one, shaped((count, samples, 3 * FACTOR_BLOCK + group_w), bf16)),
+        [SMEM, ANY, ANY, ANY],
+        (ANY, ANY, VMEM),
+        [
+            pltpu.VMEM((count, tokens, share), bf16),
+            pltpu.VMEM((tokens, group_w), bf16),
+            pltpu.VMEM((1, samples), jnp.int32),
+            pltpu.VMEM((group_w + samples, tokens), bf16),
+            pltpu.VMEM((count // 2, group_w, share), f32),
+            pltpu.VMEM((model_width // FACTOR_BLOCK, samples, FACTOR_BLOCK), bf16),
+            pltpu.SMEM((2, count), jnp.int32),
+            pltpu.SemaphoreType.DMA((count,)),
+            pltpu.SemaphoreType.DMA((count // 2,)),
+            pltpu.SemaphoreType.DMA((2,)),
+        ],
+        flops=2 * tokens * (group_w + samples) * model_width,
+        moved=2 * tokens * model_width + 2 * group_w * model_width,
+    )(block_owner, sampled_rows[None, :], cotangent, activations)
+
+
+def sum_body(cot_ref, act_ref, got_ref, x_ref, y_ref, x_b, y_a, cot, held, got, left, wire, plain, sems, got_sems, out_sems):
+    share = held.shape[2]
+    half = cot.shape[1] // 2
+    me = lax.axis_index("dp")
+    starts = [pl.multiple_of((me ^ m) * share, share) for m in MASKS[:3]]
+    loads = start_all(
+        [cot_ref] + [act_ref.at[:, pl.ds(start, share)] for start in starts],
+        [cot] + [held.at[i] for i in range(3)],
+        sems,
+    )
+    more = start_all([got_ref.at[i] for i in range(3)], [got.at[i] for i in range(3)], got_sems)
+    loads[0].wait()
+    left[...] = cot[...].astype(f32).T.astype(bf16)
+    targets = [(x_ref.at[0], y_ref.at[0]), (x_ref.at[1], x_b), (y_a, y_ref.at[1])]
+    stores = []
+    for i in range(3):
+        loads[i + 1].wait()
+        product = jnp.dot(left[...], held[i], preferred_element_type=f32)
+        more[i].wait()
+        got[i] += product
+        for k in range(2):
+            part = got[i, k * half : (k + 1) * half]
+            n = 2 * i + k
+            if n in (3, 4):
+                plain[n - 3] = part
+                source = plain.at[n - 3]
+            else:
+                encode(part, wire.at[n])
+                source = wire.at[n]
+            stores += start_all([source], [targets[i][k]], out_sems, n)
+    for store in stores:
+        store.wait()
+
+
+def hop_body(x_b, y_a, x_got, y_got, _, x_ref, y_ref, x_own, y_own, x_in, y_in, x_out, y_out, sems, out_sems):
+    loads = start_all(
+        [x_b, y_got.at[0], y_a, x_got.at[0]], [x_own, y_in, y_own, x_in], sems
+    )
+    stores = []
+    for n, (own, come, out, ref) in enumerate(((x_own, y_in, x_out, x_ref), (y_own, x_in, y_out, y_ref))):
+        loads[2 * n].wait()
+        loads[2 * n + 1].wait()
+        encode(own[...] + decode(come), out)
+        stores += start_all([out], [ref], out_sems, n)
+    for store in stores:
+        store.wait()
+
+
+def two(x):
+    high = x.astype(bf16)
+    return high, (x - high.astype(f32)).astype(bf16)
+
+
+def wide_dot(left, right, dims=(((1,), (0,)), ((), ()))):
+    left_high, left_low = two(left)
+    right_high, right_low = two(right)
+
+    def dot(a, b):
+        return lax.dot_general(a, b, dims, preferred_element_type=f32)
+
+    return dot(left_high, right_high) + (dot(left_high, right_low) + dot(left_low, right_high))
+
+
+def places(extent):
+    return (
+        lax.broadcasted_iota(jnp.int32, (extent, extent), 0),
+        lax.broadcasted_iota(jnp.int32, (extent, extent), 1),
+    )
+
+
+FOLD_ROWS = 8
+
+
+def fold(matrix, into, at=()):
+    half = matrix.shape[0] // 2
+    row, column = places(half)
+    low = matrix[half:, half:]
+    into[(*at, slice(0, half), slice(0, half))] = jnp.where(row <= column, matrix[:half, :half], low)
+    into[(*at, slice(0, half), slice(half, 2 * half))] = matrix[:half, half:]
+    diagonal = jnp.sum(jnp.where(row == column, low, 0.0), axis=0, keepdims=True)
+    wide = jnp.concatenate([diagonal, diagonal], axis=1)
+    into[(*at, slice(half, half + FOLD_ROWS))] = jnp.broadcast_to(wide, (FOLD_ROWS, 2 * half))
+
+
+def unfold(packed):
+    half = packed.shape[1] // 2
+    row, column = places(half)
+    both, corner = packed[:half, :half], packed[:half, half:]
+    turned = both.T
+    top = jnp.where(row <= column, both, turned)
+    low = jnp.where(row == column, packed[half : half + 1, :half], jnp.where(row > column, both, turned))
+    return jnp.concatenate(
+        [jnp.concatenate([top, corner], axis=1), jnp.concatenate([corner.T, low], axis=1)], axis=0
+    )
+
+
+def invert_body(scales, owner, rows_ref, _, __, all_ref, own_ref, out_ref):
+    width = FACTOR_BLOCK
+    me = lax.axis_index("dp")
+    owned = jnp.int32(0)
+    for b in range(owner.shape[0]):
+        owned = owned + jnp.where(owner[b] == me, 1, 0)
+    used = jnp.where(lax.axis_index("tensor") < owned, 1.0, 0.0).astype(f32)
+    row, column = places(width)
+    eye = (row == column).astype(f32)
+    states = []
+    for m in range(4):
+        rows = rows_ref[:, m * width : (m + 1) * width]
+        gram = lax.dot_general(
+            rows, rows, (((0,), (0,)), ((), ())), preferred_element_type=f32
+        )
+        matrix = gram * scales[1 if m == 3 else 0] + DAMPING * eye
+        bound = jnp.max(jnp.sum(jnp.abs(matrix), axis=1, keepdims=True), axis=0, keepdims=True)
+        inverse_bound = 1.0 / bound
+        low = matrix * inverse_bound
+        states.append((low, (2.0 * eye - low) * inverse_bound))
+    lows = [2.0 * low - wide_dot(low, low) for low, _ in states]
+    currents = [current for _, current in states]
+    for turn in range(1, ITERS):
+        if turn < ITERS - 1:
+            both = [
+                wide_dot(jnp.concatenate([current, low], axis=0), low)
+                for current, low in zip(currents, lows)
+            ]
+            currents = [2.0 * current - b[:width] for current, b in zip(currents, both)]
+            lows = [2.0 * low - b[width:] for low, b in zip(lows, both)]
+        else:
+            currents = [
+                2.0 * current - wide_dot(current, low) for current, low in zip(currents, lows)
+            ]
+    fold(currents[0], all_ref, (0,))
+    fold(currents[1], all_ref, (1,))
+    fold(currents[2] * used, all_ref, (2,))
+    own_ref[...] = all_ref[2]
+    out_ref[...] = currents[3]
+
+
+def owned_body(here, beside, two_off, three_off, _, out_ref, held, sems):
+    loads = start_all([here.at[2], beside.at[2], two_off, three_off], [held.at[k] for k in range(4)], sems)
+    z = lax.axis_index("tensor")
+    for k, load in enumerate(loads):
+        load.wait()
+        out_ref[z ^ k] = unfold(held[k])
+
+
+def prepare_body(cot_ref, act_ref, got_ref, x_got, y_got, _, sum_ref, cot, held, got, x_in, y_in, sems):
+    half = cot.shape[1] // 2
+    share = held.shape[1]
+    start = pl.multiple_of(lax.axis_index("dp") * share, share)
+    loads = start_all(
+        [cot_ref, act_ref.at[:, pl.ds(start, share)], got_ref.at[0], x_got.at[1], y_got.at[1]],
+        [cot, held, got, x_in, y_in],
+        sems,
+    )
+    loads[0].wait()
+    left = cot[...].astype(f32).T.astype(bf16)
+    loads[1].wait()
+    product = jnp.dot(left, held[...], preferred_element_type=f32)
+    for load in loads[2:]:
+        load.wait()
+    total = product + got[...]
+    sum_ref[:half] = total[:half] + decode(x_in)
+    sum_ref[half:] = total[half:] + decode(y_in)
+
+
+def finish_body(*refs):
+    sources, step_out = refs[:6], refs[6]
+    held, (step, sems, out_sems) = refs[7:13], refs[13:]
+    loads = start_all([source.at[pl.ds(0, 2)] for source in sources[:2]] + list(sources[2:]), held, sems)
+    near, far, g_inverse, total, x_in, y_in = held
+    half = total.shape[0] // 2
+    odd = lax.axis_index("tensor") % 2
+    width = FACTOR_BLOCK
+    for load in loads[:2]:
+        load.wait()
+    inverses = [[unfold(part[p]) for part in (near, far)] for p in range(2)]
+    for load in loads[2:]:
+        load.wait()
+    total[:half] += decode(y_in)
+    total[half:] += decode(x_in)
+    right = wide_dot(g_inverse[...], total[...], (((0,), (0,)), ((), ())))
+    stores = []
+    for p in range(2):
+        block = right[:, p * width : (p + 1) * width], right[:, (p + 2) * width : (p + 3) * width]
+        for k in range(2):
+            at = odd if k == 0 else 1 - odd
+            chosen = jnp.where(at == 0, block[0], block[1])
+            step[2 * p + k] = wide_dot(inverses[p][k], chosen, (((1,), (1,)), ((), ())))
+            start = pl.multiple_of((2 * at + p) * width, width)
+            stores += start_all([step.at[2 * p + k]], [step_out.at[pl.ds(start, width), :]], out_sems, 2 * p + k)
+    for store in stores:
+        store.wait()
+
+
+def square_device(activations, cotangent, sampled_rows, block_owner):
+    tok_local, model_width = activations.shape
+    group_w = cotangent.shape[1]
+    dp_count = lax.axis_size("dp")
+    depth = lax.axis_size("tensor")
+    samples = sampled_rows.shape[0]
+    row_share = model_width // dp_count
+    half = group_w // 2
+
+    def swap(block, bit, axis="dp"):
+        count = lax.axis_size(axis)
+        return lax.ppermute(block, axis, [(i, i ^ bit) for i in range(count)])
+
+    theirs, own_theirs, picked = project(
+        block_owner, sampled_rows, cotangent, activations, dp_count
+    )
+    got = swap(theirs, CORE)
+    rows = lax.all_to_all(picked, "dp", split_axis=0, concat_axis=0, tiled=True)
+    own_got = swap(own_theirs, CORE)
+
+    def dma(count):
+        return pltpu.SemaphoreType.DMA((count,))
+
+    cot_vmem = pltpu.VMEM(cotangent.shape, bf16)
+    three = len(MASKS) - 1
+    wired = (fold_rows(half), row_share)
+    piece = shaped((half, row_share))
+    x_first, y_first, x_b, y_a = call(
+        sum_body,
+        "sum_cores",
+        (shaped((2, *wired), bf16),) * 2 + (piece,) * 2,
+        [ANY] * 3,
+        (ANY,) * 4,
+        [
+            cot_vmem,
+            pltpu.VMEM((three, tok_local, row_share), bf16),
+            pltpu.VMEM((three, group_w, row_share), f32),
+            pltpu.VMEM((group_w, tok_local), bf16),
+            pltpu.VMEM((2 * three, *wired), bf16),
+            pltpu.VMEM((2, half, row_share), f32),
+            dma(1 + three),
+            dma(three),
+            dma(2 * three),
+        ],
+        moved=9 * MIB,
+    )(cotangent, activations, got)
+    x_got, y_got = swap(x_first, NEAR_X), swap(y_first, NEAR_Y)
+
+    scales = (1.0 / (samples * dp_count), tok_local / samples)
+    packed = (FACTOR_BLOCK // 2 + FOLD_ROWS, FACTOR_BLOCK)
+    inverses, own, g_inverse = call(
+        functools.partial(invert_body, scales),
+        "invert_factors",
+        (shaped((3, *packed)), shaped(packed), shaped((FACTOR_BLOCK, FACTOR_BLOCK))),
+        [SMEM, VMEM, ANY, ANY],
+        (VMEM,) * 3,
+        flops=2 * 3 * 4 * 18 * FACTOR_BLOCK**3,
+        moved=2 * MIB,
+    )(block_owner, rows.reshape(-1, rows.shape[-1]), x_b, own_got)
+    beside = swap(inverses, 1, "tensor")
+    two_off, three_off = swap(own, 2, "tensor"), swap(own, 3, "tensor")
+
+    piece_vmem = pltpu.VMEM((half, row_share), f32)
+    wired_vmem = pltpu.VMEM(wired, bf16)
+    x_last, y_last = call(
+        hop_body,
+        "hop",
+        (shaped(wired, bf16),) * 2,
+        [ANY] * 5,
+        (ANY,) * 2,
+        [piece_vmem] * 2 + [wired_vmem] * 4 + [dma(4), dma(2)],
+    )(x_b, y_a, x_got, y_got, inverses)
+    hopped = x_last
+    x_last, y_last = swap(x_last, NEAR_X), swap(y_last, NEAR_Y)
+
+    total = pltpu.VMEM((group_w, row_share), f32)
+    square = (depth, FACTOR_BLOCK, FACTOR_BLOCK)
+    owned = call(
+        owned_body, "owned", shaped(square), [ANY] * 5, VMEM, [pltpu.VMEM((4, *packed), f32), dma(4)]
+    )(inverses, beside, two_off, three_off, hopped)
+    so_far = call(
+        prepare_body,
+        "prepare",
+        shaped((group_w, row_share)),
+        [ANY] * 6,
+        VMEM,
+        [cot_vmem, pltpu.VMEM((tok_local, row_share), bf16), total, wired_vmem, wired_vmem, dma(5)],
+        flops=PREPARE_FLOPS,
+    )(cotangent, activations, own_got, x_got, y_got, owned)
+    step = call(
+        finish_body,
+        "finish",
+        shaped((row_share, group_w)),
+        [ANY] * 6,
+        ANY,
+        [pltpu.VMEM((2, *packed), f32)] * 2
+        + [pltpu.VMEM((FACTOR_BLOCK, FACTOR_BLOCK), f32), total, wired_vmem, wired_vmem]
+        + [pltpu.VMEM(square, f32), dma(6), dma(depth)],
+        moved=6 * MIB,
+    )(inverses, beside, g_inverse, so_far, x_last, y_last)
+    return step, owned
+
+
 def solution(mesh):
+    def per_device(activations, cotangent, sampled_rows, block_owner):
+        block_total = activations.shape[1] // FACTOR_BLOCK
+        dp_count, depth = mesh.shape["dp"], mesh.shape["tensor"]
+        fits = (
+            dp_count == 8
+            and depth == 4
+            and block_total == dp_count * depth
+            and cotangent.shape[1] == FACTOR_BLOCK
+            and sampled_rows.shape[0] % 16 == 0
+            and activations.shape[0] % 128 == 0
+        )
+        run = square_device if fits else general_device
+        return run(activations, cotangent, sampled_rows, block_owner)
+
     return jax.shard_map(
         per_device,
         mesh=mesh,

time: 220 us -> 71.1 us (0.32)
  waiting for transfers between devices: 108 us -> 10.6 us
  matrix products: 68.9 us -> 0 us
  Pallas kernels: 0 us -> 40.4 us
  between operations: 14.6 us -> 0.89 us
  local copies, waits for them, and re-layouts: 14.1 us -> 2.14 us
  starting transfers between devices: 5.49 us -> 16.1 us
  other arithmetic: 7.31 us -> 0 us
    dot_general x47 -> x0, matrix products: 68.9 us -> none  [the longest x20 25 us: advance(): jnp.einsum('nij,njk->nik', current, 2.0 * identity[None, :, :] - product,...]
    all_gather x1 -> x0, waiting for transfers between devices: 54.6 us -> none  [per_device(): shard_piece = lax.all_gather(owned_out, 'dp', axis=0, tiled=True)]
    pallas_call x0 -> x7, Pallas kernels: none -> 40.4 us  [the longest x1 10.7 us: square_device(): call(functools.partial(invert_body, scales), 'invert_factors', (shaped((3...]
    reduce_scatter x1 -> x0, waiting for transfers between devices: 39.6 us -> none  [per_device(): lax.psum_scatter(lax.dot_general(activations, cotangent, (((0,), (0,)), (...]
    ppermute x0 -> x9, starting transfers between devices: none -> 11 us  [swap(): return lax.ppermute(block, axis, [(i, i ^ bit) for i in range(count)])]
    gather x3 -> x0, local copies, waits for them, and re-layouts: 9.72 us -> none  [the longest x1 8.38 us: per_device(): picked_acts = jnp.take(activations, sampled_rows, axis=0)]
    all_to_all x1, waiting for transfers between devices: 13.9 us -> 4.32 us  [square_device(): rows = lax.all_to_all(picked, 'dp', split_axis=0, concat_axis=0, tiled=True)]
    ppermute x0 -> x9, waiting for transfers between devices: none -> 6.25 us  [swap(): return lax.ppermute(block, axis, [(i, i ^ bit) for i in range(count)])]
  transfers between devices with their start and end apart: 4 -> 10, of which waited for: 3 -> 5; matrix products, arithmetic and copies ran while one was open for 34% -> 0% of each run, Pallas kernels for 0% -> 38%
where the time goes in v2:
time: 71.1 us; the launch traced here: 70.1 us
  Pallas kernels  40.4 us (57%)
  starting transfers between devices  16.1 us (23%)
  waiting for transfers between devices  10.6 us (15%)
  local copies, waits for them, and re-layouts  2.14 us (3%)
  between operations  0.89 us (1%)
    ppermute x9, starting transfers between devices, swap(): return lax.ppermute(block, axis, [(i, i ^ bit) for i in range(count)])  11 us
    pallas_call x1, Pallas kernels, square_device(): call(functools.partial(invert_body, scales), 'invert_factors', (shaped((3...  10.7 us
    pallas_call x1, Pallas kernels, project(): call(project_body, 'project', (rest, one, shaped((count, samples, 3 * FAC...  9.25 us
    pallas_call x1, Pallas kernels, square_device(): call(sum_body, 'sum_cores', (shaped((2, *wired), bf16),) * 2 + (piece,) *...  6.86 us
    ppermute x9, waiting for transfers between devices, swap(): return lax.ppermute(block, axis, [(i, i ^ bit) for i in range(count)])  6.25 us
    all_to_all x1, starting transfers between devices, square_device(): rows = lax.all_to_all(picked, 'dp', split_axis=0, concat_axis=0, tiled=True)  5.15 us
    all_to_all x1, waiting for transfers between devices, square_device(): rows = lax.all_to_all(picked, 'dp', split_axis=0, concat_axis=0, tiled=True)  4.32 us
    pallas_call x1, Pallas kernels, square_device(): call(finish_body, 'finish', shaped((row_share, group_w)), [ANY] * 6, ANY,...  4.16 us
  transfers between devices with their start and end apart: 10, of which 5 were waited for; matrix products, arithmetic and copies ran while one was open for 0% of the time, Pallas kernels for 38%

profile of v2, /device:TPU:0, one launch (start us, length us, event | category | flops | bytes accessed | tf_op | source)
XLA Modules:
  0.0 70.1 jit_solution(8669167980438255414)
XLA Ops:
  0.6 9.3 %project.1 = (f32[3,256,1024]{2,1,0:T(8,128)}, f32[1,256,1024]{2,1,0:T(8,128)}, bf16[8,64,1024]{2,1,0:T(8,128)(2,1)}) custom-call(s32[32]{0:T(128)} %owner.3, s32[1,64]{1,0:T(1,128)} %bitcast.2, bf16[768,256]{1,0:T(8,128)(2,1)} %cot_ref.5, bf16[768,8192]{1,0:T(8,128)(2,1)} %act_ref.5), custom_call_target="tpu_custom_call" | custom-call | flops 4026531840 | bytes 16777216 | tf_op jit(solution)/shard_map/project/pallas_call | solution.py:271
  9.9 0.5 collective-permute-start
  10.4 0.1 collective-permute-start.1
  10.5 5.2 %all-to-all-start = ((bf16[8,64,1024]{2,1,0:T(8,128)(2,1)}), bf16[8,64,1024]{2,1,0:T(8,128)(2,1)}, u32[]{:S(2)}, u32[]{:S(2)}) async-start(bf16[8,64,1024]{2,1,0:T(8,128)(2,1)} %get-tuple-element.14), calls=%async_computation | async-start | bytes 2097152 | tf_op jit(solution)/shard_map/all_to_all | solution.py:505
  15.6 0.4 collective-permute-done.got_ref
  16.0 6.9 %sum_cores.1 = (bf16[2,192,1024]{2,1,0:T(8,128)(2,1)}, bf16[2,192,1024]{2,1,0:T(8,128)(2,1)}, f32[128,1024]{1,0:T(8,128)}, f32[128,1024]{1,0:T(8,128)}) custom-call(bf16[768,256]{1,0:T(8,128)(2,1)} %cot_ref.5, bf16[768,8192]{1,0:T(8,128)(2,1)} %act_ref.5, f32[3,256,1024]{2,1,0:T(8,128)} %collective-permute-done.got_ref), custom_call_target="tpu_custom_call" | custom-call | bytes 9437184 | tf_op jit(solution)/shard_map/sum_cores/pallas_call | solution.py:515
  22.9 2.9 %collective-permute-start.3 = (bf16[2,192,1024]{2,1,0:T(8,128)(2,1)}, bf16[2,192,1024]{2,1,0:T(8,128)(2,1)}, u32[]{:S(2)}, u32[]{:S(2)}) collective-permute-start(bf16[2,192,1024]{2,1,0:T(8,128)(2,1)} %get-tuple-element.20), channel_id=1, source_target_pairs={{0,8},{4,12},{8,0},{12,4},{16,24},{20,28},{24,16},{28,20},{1,9},{5... | collective-permute-start | bytes 2359304 | tf_op jit(solution)/shard_map/ppermute | solution.py:499
  25.8 1.5 %collective-permute-start.4 = (bf16[2,192,1024]{2,1,0:T(8,128)(2,1)}, bf16[2,192,1024]{2,1,0:T(8,128)(2,1)}, u32[]{:S(2)}, u32[]{:S(2)}) collective-permute-start(bf16[2,192,1024]{2,1,0:T(8,128)(2,1)} %get-tuple-element.21), channel_id=1, source_target_pairs={{0,16},{4,20},{8,24},{12,28},{16,0},{20,4},{24,8},{28,12},{1,17},{... | collective-permute-start | bytes 2359304 | tf_op jit(solution)/shard_map/ppermute | solution.py:499
  27.4 4.3 %all-to-all-done = bf16[8,64,1024]{2,1,0:T(8,128)(2,1)} async-done(((bf16[8,64,1024]{2,1,0:T(8,128)(2,1)}), bf16[8,64,1024]{2,1,0:T(8,128)(2,1)}, u32[]{:S(2)}, u32[]{:S(2)}) %all-to-all-start) | async-done | bytes 1048608 | tf_op jit(solution)/shard_map/all_to_all | solution.py:505
  31.7 0.0 collective-permute-done.1.__.got_ref
  31.7 10.7 %invert_factors.1 = (f32[3,136,256]{2,1,0:T(8,128)}, f32[136,256]{1,0:T(8,128)}, f32[256,256]{1,0:T(8,128)}) custom-call(s32[32]{0:T(128)} %owner.3, bf16[512,1024]{1,0:T(8,128)(2,1)} %bitcast.1.rows_ref, f32[128,1024]{1,0:T(8,128)} %get-tuple-element.16._.x_b, f32[1,256,1024]{2,1,0:T(8,128)} %collective-permute-done.1.__.got_ref), custom_call_target="tpu_custom_call" | custom-call | flops 7247757312 | bytes 2097152 | tf_op jit(solution)/shard_map/invert_factors/pallas_call | solution.py:538
  42.3 2.0 %collective-permute-start.2 = (f32[3,136,256]{2,1,0:T(8,128)}, f32[3,136,256]{2,1,0:T(8,128)S(1)}, u32[]{:S(2)}, u32[]{:S(2)}) collective-permute-start(f32[3,136,256]{2,1,0:T(8,128)} %get-tuple-element.18._.here.refs_0_), channel_id=1, source_target_pairs={{0,1},{1,0},{2,3},{3,2},{4,5},{5,4},{6,7},{7,6},{8,9},{9,8},{10,11... | collective-permute-start | bytes 1253384 | tf_op jit(solution)/shard_map/ppermute | solution.py:499
  44.4 2.5 %collective-permute-start.6 = (f32[136,256]{1,0:T(8,128)}, f32[136,256]{1,0:T(8,128)S(1)}, u32[]{:S(2)}, u32[]{:S(2)}) collective-permute-start(f32[136,256]{1,0:T(8,128)} %get-tuple-element.22), channel_id=1, source_target_pairs={{0,3},{1,2},{2,1},{3,0},{4,7},{5,6},{6,5},{7,4},{8,11},{9,10},{10,... | collective-permute-start | bytes 417800 | tf_op jit(solution)/shard_map/ppermute | solution.py:499
  46.8 0.1 collective-permute-start.5
  46.9 0.2 collective-permute-done.3.x_got
  47.1 0.8 %collective-permute-done.4.y_got = bf16[2,192,1024]{2,1,0:T(8,128)(2,1)} collective-permute-done((bf16[2,192,1024]{2,1,0:T(8,128)(2,1)}, bf16[2,192,1024]{2,1,0:T(8,128)(2,1)}, u32[]{:S(2)}, u32[]{:S(2)}) %collective-permute-start.4) | collective-permute-done | bytes 786464 | tf_op jit(solution)/shard_map/ppermute | solution.py:499
  47.9 3.2 %hop.1 = (bf16[192,1024]{1,0:T(8,128)(2,1)}, bf16[192,1024]{1,0:T(8,128)(2,1)}) custom-call(f32[128,1024]{1,0:T(8,128)} %get-tuple-element.16._.x_b, f32[128,1024]{1,0:T(8,128)} %get-tuple-element.23.y_a, bf16[2,192,1024]{2,1,0:T(8,128)(2,1)} %collective-permute-done.3.x_got, bf16[2,192,1024]{2,1,0:T(8,128)(2,1)} %collective-permute-done.4.y_got, ...), custom_call_target="tpu_custom_call" | custom-call | tf_op jit(solution)/shard_map/hop/pallas_call | solution.py:552
  51.1 0.8 %collective-permute-start.8 = (bf16[192,1024]{1,0:T(8,128)(2,1)}, bf16[192,1024]{1,0:T(8,128)(2,1)S(1)}, u32[]{:S(2)}, u32[]{:S(2)}) collective-permute-start(bf16[192,1024]{1,0:T(8,128)(2,1)} %get-tuple-element.25), channel_id=1, source_target_pairs={{0,16},{4,20},{8,24},{12,28},{16,0},{20,4},{24,8},{28,12},{1,17},{... | collective-permute-start | bytes 1179656 | tf_op jit(solution)/shard_map/ppermute | solution.py:499
  51.9 0.6 collective-permute-start.7
  52.5 4.9 %collective-permute-done.6.three_off = f32[136,256]{1,0:T(8,128)S(1)} collective-permute-done((f32[136,256]{1,0:T(8,128)}, f32[136,256]{1,0:T(8,128)S(1)}, u32[]{:S(2)}, u32[]{:S(2)}) %collective-permute-start.6) | collective-permute-done | bytes 139296 | tf_op jit(solution)/shard_map/ppermute | solution.py:499
  57.4 0.0 copy-start.2
  57.4 0.0 collective-permute-done.5.two_off
  57.4 0.0 collective-permute-done.2.beside.refs_1_
  57.4 0.6 copy-done.2
  58.0 0.0 copy-start
  58.0 0.7 %copy-done = f32[3,136,256]{2,1,0:T(8,128)} copy-done((f32[3,136,256]{2,1,0:T(8,128)}, f32[3,136,256]{2,1,0:T(8,128)S(1)}, u32[]{:S(2)}) %copy-start) | copy-done | bytes 417816
  58.8 2.3 %owned.1._ = f32[4,256,256]{2,1,0:T(8,128)} custom-call(f32[3,136,256]{2,1,0:T(8,128)} %get-tuple-element.18._.here.refs_0_, f32[3,136,256]{2,1,0:T(8,128)} %copy-done, f32[136,256]{1,0:T(8,128)} %collective-permute-done.5.two_off, f32[136,256]{1,0:T(8,128)} %copy-done.2, bf16[192,1024]{1,0:T(8,128)(2,1)} %get-tuple-element.24._), custom_call_target="tpu_custom_call" | custom-call | tf_op jit(solution)/shard_map/owned/pallas_call | solution.py:565
  61.1 3.9 %prepare.1.refs_3_ = f32[256,1024]{1,0:T(8,128)} custom-call(bf16[768,256]{1,0:T(8,128)(2,1)} %cot_ref.5, bf16[768,8192]{1,0:T(8,128)(2,1)} %act_ref.5, f32[1,256,1024]{2,1,0:T(8,128)} %collective-permute-done.1.__.got_ref, bf16[2,192,1024]{2,1,0:T(8,128)(2,1)} %collective-permute-done.3.x_got, bf16[2,192,1024]{2,1,0:T(8,128)(2,1)} %collective-permute-done.4.y_got, ...), custom_call_target="tpu_custom_call" | custom-call | flops 20000000000 | tf_op jit(solution)/shard_map/prepare/pallas_call | solution.py:568
  65.0 0.0 collective-permute-done.8.refs_5_
  65.0 0.0 copy-start.1
  65.0 0.0 collective-permute-done.7.refs_4_
  65.0 0.7 %copy-done.1 = bf16[192,1024]{1,0:T(8,128)(2,1)} copy-done((bf16[192,1024]{1,0:T(8,128)(2,1)}, bf16[192,1024]{1,0:T(8,128)(2,1)S(1)}, u32[]{:S(2)}) %copy-start.1) | copy-done | bytes 393240
  65.8 4.2 %finish.1 = f32[1024,256]{1,0:T(8,128)} custom-call(f32[3,136,256]{2,1,0:T(8,128)} %get-tuple-element.18._.here.refs_0_, f32[3,136,256]{2,1,0:T(8,128)} %copy-done, f32[256,256]{1,0:T(8,128)} %get-tuple-element.19.refs_2_, f32[256,1024]{1,0:T(8,128)} %prepare.1.refs_3_, bf16[192,1024]{1,0:T(8,128)(2,1)} %collective-permute-done.7.refs_4_, ...), custom_call_target="tpu_custom_call" | custom-call | bytes 6291456 | tf_op jit(solution)/shard_map/finish/pallas_call | solution.py:577
Async XLA Ops:
  9.9 6.1 %collective-permute-start = (f32[3,256,1024]{2,1,0:T(8,128)}, f32[3,256,1024]{2,1,0:T(8,128)}, u32[]{:S(2)}, u32[]{:S(2)}) collective-permute-start(f32[3,256,1024]{2,1,0:T(8,128)} %get-tuple-element.15), channel_id=1, source_target_pairs={{0,4},{4,0},{8,12},{12,8},{16,20},{20,16},{24,28},{28,24},{1,5},{5... | collective-permute-start | bytes 9437192 | tf_op jit(solution)/shard_map/ppermute | solution.py:499
  10.4 21.3 %collective-permute-start.1 = (f32[1,256,1024]{2,1,0:T(8,128)}, f32[1,256,1024]{2,1,0:T(8,128)}, u32[]{:S(2)}, u32[]{:S(2)}) collective-permute-start(f32[1,256,1024]{2,1,0:T(8,128)} %get-tuple-element.17), channel_id=1, source_target_pairs={{0,4},{4,0},{8,12},{12,8},{16,20},{20,16},{24,28},{28,24},{1,5},{5... | collective-permute-start | bytes 3145736 | tf_op jit(solution)/shard_map/ppermute | solution.py:499
  10.5 21.2 %all-to-all-start = ((bf16[8,64,1024]{2,1,0:T(8,128)(2,1)}), bf16[8,64,1024]{2,1,0:T(8,128)(2,1)}, u32[]{:S(2)}, u32[]{:S(2)}) async-start(bf16[8,64,1024]{2,1,0:T(8,128)(2,1)} %get-tuple-element.14), calls=%async_computation | async-start | bytes 2097152 | tf_op jit(solution)/shard_map/all_to_all | solution.py:505
  22.9 24.2 %collective-permute-start.3 = (bf16[2,192,1024]{2,1,0:T(8,128)(2,1)}, bf16[2,192,1024]{2,1,0:T(8,128)(2,1)}, u32[]{:S(2)}, u32[]{:S(2)}) collective-permute-start(bf16[2,192,1024]{2,1,0:T(8,128)(2,1)} %get-tuple-element.20), channel_id=1, source_target_pairs={{0,8},{4,12},{8,0},{12,4},{16,24},{20,28},{24,16},{28,20},{1,9},{5... | collective-permute-start | bytes 2359304 | tf_op jit(solution)/shard_map/ppermute | solution.py:499
  25.8 22.1 %collective-permute-start.4 = (bf16[2,192,1024]{2,1,0:T(8,128)(2,1)}, bf16[2,192,1024]{2,1,0:T(8,128)(2,1)}, u32[]{:S(2)}, u32[]{:S(2)}) collective-permute-start(bf16[2,192,1024]{2,1,0:T(8,128)(2,1)} %get-tuple-element.21), channel_id=1, source_target_pairs={{0,16},{4,20},{8,24},{12,28},{16,0},{20,4},{24,8},{28,12},{1,17},{... | collective-permute-start | bytes 2359304 | tf_op jit(solution)/shard_map/ppermute | solution.py:499
  42.3 15.0 %collective-permute-start.2 = (f32[3,136,256]{2,1,0:T(8,128)}, f32[3,136,256]{2,1,0:T(8,128)S(1)}, u32[]{:S(2)}, u32[]{:S(2)}) collective-permute-start(f32[3,136,256]{2,1,0:T(8,128)} %get-tuple-element.18._.here.refs_0_), channel_id=1, source_target_pairs={{0,1},{1,0},{2,3},{3,2},{4,5},{5,4},{6,7},{7,6},{8,9},{9,8},{10,11... | collective-permute-start | bytes 1253384 | tf_op jit(solution)/shard_map/ppermute | solution.py:499
  44.4 13.0 %collective-permute-start.6 = (f32[136,256]{1,0:T(8,128)}, f32[136,256]{1,0:T(8,128)S(1)}, u32[]{:S(2)}, u32[]{:S(2)}) collective-permute-start(f32[136,256]{1,0:T(8,128)} %get-tuple-element.22), channel_id=1, source_target_pairs={{0,3},{1,2},{2,1},{3,0},{4,7},{5,6},{6,5},{7,4},{8,11},{9,10},{10,... | collective-permute-start | bytes 417800 | tf_op jit(solution)/shard_map/ppermute | solution.py:499
  46.8 10.6 %collective-permute-start.5 = (f32[136,256]{1,0:T(8,128)}, f32[136,256]{1,0:T(8,128)}, u32[]{:S(2)}, u32[]{:S(2)}) collective-permute-start(f32[136,256]{1,0:T(8,128)} %get-tuple-element.22), channel_id=1, source_target_pairs={{0,2},{1,3},{2,0},{3,1},{4,6},{5,7},{6,4},{7,5},{8,10},{9,11},{10,... | collective-permute-start | bytes 417800 | tf_op jit(solution)/shard_map/ppermute | solution.py:499
  51.1 13.8 %collective-permute-start.8 = (bf16[192,1024]{1,0:T(8,128)(2,1)}, bf16[192,1024]{1,0:T(8,128)(2,1)S(1)}, u32[]{:S(2)}, u32[]{:S(2)}) collective-permute-start(bf16[192,1024]{1,0:T(8,128)(2,1)} %get-tuple-element.25), channel_id=1, source_target_pairs={{0,16},{4,20},{8,24},{12,28},{16,0},{20,4},{24,8},{28,12},{1,17},{... | collective-permute-start | bytes 1179656 | tf_op jit(solution)/shard_map/ppermute | solution.py:499
  51.9 13.1 %collective-permute-start.7 = (bf16[192,1024]{1,0:T(8,128)(2,1)}, bf16[192,1024]{1,0:T(8,128)(2,1)}, u32[]{:S(2)}, u32[]{:S(2)}) collective-permute-start(bf16[192,1024]{1,0:T(8,128)(2,1)} %get-tuple-element.24._), channel_id=1, source_target_pairs={{0,8},{4,12},{8,0},{12,4},{16,24},{20,28},{24,16},{28,20},{1,9},{5... | collective-permute-start | bytes 1179656 | tf_op jit(solution)/shard_map/ppermute | solution.py:499
  57.4 0.7 copy-start.2
  58.0 0.7 %copy-start = (f32[3,136,256]{2,1,0:T(8,128)}, f32[3,136,256]{2,1,0:T(8,128)S(1)}, u32[]{:S(2)}) copy-start(f32[3,136,256]{2,1,0:T(8,128)S(1)} %collective-permute-done.2.beside.refs_1_) | copy-start | bytes 1253380
  65.0 0.8 %copy-start.1 = (bf16[192,1024]{1,0:T(8,128)(2,1)}, bf16[192,1024]{1,0:T(8,128)(2,1)S(1)}, u32[]{:S(2)}) copy-start(bf16[192,1024]{1,0:T(8,128)(2,1)S(1)} %collective-permute-done.8.refs_5_) | copy-start | bytes 1179652

commit v3 on v2

v3 whole, which is shorter than its diff:
```python
import functools

import jax
import jax.numpy as jnp
from jax import lax
from jax.experimental import pallas as pl
from jax.experimental.pallas import tpu as pltpu
from jax.sharding import PartitionSpec as P

S_DEV = 64
FACTOR_BLOCK = 256
ITERS = 10


DAMPING = 0.05
precise_mode = lax.Precision.HIGHEST
f32 = jnp.float32
bf16 = jnp.bfloat16


def block_rank(block_owner):
    block_total = block_owner.shape[0]
    same_owner = block_owner[:, None] == block_owner[None, :]
    positions = jnp.arange(block_total, dtype=jnp.int32)
    before = positions[None, :] < positions[:, None]
    return jnp.sum((same_owner & before).astype(jnp.int32), axis=1)


def from_partner(block, axis, apart):
    count = lax.axis_size(axis)
    route = []
    for low in range(count):
        high = low | 1 << apart
        if high != low and high < count:
            route += [(low, high), (high, low)]
    return lax.ppermute(block, axis, route)


def newton_inverse(matrix):
    extent = matrix.shape[-1]
    identity = jnp.eye(extent, dtype=jnp.float32)
    row_bound = jnp.max(jnp.sum(jnp.abs(matrix), axis=2), axis=1)
    initial = identity[None, :, :] / row_bound[:, None, None]

    def advance(turn_index, current):
        product = jnp.einsum("nij,njk->nik", matrix, current, precision=precise_mode)
        return jnp.einsum(
            "nij,njk->nik", current, 2.0 * identity[None, :, :] - product, precision=precise_mode
        )

    return lax.fori_loop(0, ITERS, advance, initial)


def owner_grams(received):
    return jnp.einsum("pcsk,pcsl->ckl", received, received, preferred_element_type=jnp.float32)


def general_device(activations, cotangent, sampled_rows, block_owner):
    tok_local = activations.shape[0]
    model_width = activations.shape[1]
    group_w = cotangent.shape[1]
    dp_count = lax.axis_size("dp")
    my_dp = lax.axis_index("dp")
    block_total = model_width // FACTOR_BLOCK
    capacity = max(1, block_total // dp_count)
    row_share = model_width // dp_count
    samples_all = S_DEV * dp_count
    grad_rows = lax.psum_scatter(
        lax.dot_general(
            activations, cotangent, (((0,), (0,)), ((), ())), preferred_element_type=jnp.float32
        ),
        "dp",
        scatter_dimension=0,
        tiled=True,
    )
    picked_acts = jnp.take(activations, sampled_rows, axis=0)
    picked_grads = jnp.take(cotangent, sampled_rows, axis=0)
    g_partial = lax.dot_general(
        picked_grads, picked_grads, (((0,), (0,)), ((), ())), preferred_element_type=jnp.float32
    )
    g_total = lax.psum(g_partial, "dp")
    g_factor = g_total * (tok_local / S_DEV) + DAMPING * jnp.eye(group_w, dtype=jnp.float32)
    slot_of = block_owner * capacity + block_rank(block_owner)
    dest_ids = jnp.arange(dp_count * capacity, dtype=jnp.int32)
    chooser = (slot_of[None, :] == dest_ids[:, None]).astype(jnp.bfloat16)
    row_blocks = picked_acts.reshape(S_DEV, block_total, FACTOR_BLOCK)
    outgoing = lax.dot_general(
        chooser, row_blocks, (((1,), (1,)), ((), ())), preferred_element_type=jnp.float32
    )
    outgoing = outgoing.astype(jnp.bfloat16).reshape(dp_count, capacity, S_DEV, FACTOR_BLOCK)
    gram_slots = owner_grams(
        lax.all_to_all(outgoing, "dp", split_axis=0, concat_axis=0, tiled=True)
    )
    a_factor = (
        gram_slots / samples_all + DAMPING * jnp.eye(FACTOR_BLOCK, dtype=jnp.float32)[None, :, :]
    )
    input_factor_inverse = newton_inverse(a_factor)
    owned_count = jnp.sum((block_owner == my_dp).astype(jnp.int32))
    slot_used = jnp.arange(capacity, dtype=jnp.int32) < owned_count
    owned_out = jnp.where(slot_used[:, None, None], input_factor_inverse, 0.0)
    g_inverse = newton_inverse(g_factor[None, :, :])[0]
    per_dev = max(1, row_share // FACTOR_BLOCK)
    rows_each = min(row_share, FACTOR_BLOCK)
    first_block = my_dp * row_share // FACTOR_BLOCK
    need_ids = first_block + jnp.arange(per_dev, dtype=jnp.int32)
    need_slots = jnp.take(slot_of, need_ids)
    row_offset = my_dp * row_share % FACTOR_BLOCK
    shard_piece = lax.all_gather(owned_out, "dp", axis=0, tiled=True)
    rows_part = lax.dynamic_slice_in_dim(shard_piece, row_offset, rows_each, 1)
    slot_ids = jnp.arange(shard_piece.shape[0], dtype=jnp.int32)
    selector = (need_slots[:, None] == slot_ids[None, :]).astype(jnp.float32)
    inverse_rows = jnp.einsum("jm,mkl->jkl", selector, rows_part, precision=precise_mode)
    grad_right = jnp.dot(
        grad_rows, g_inverse, precision=precise_mode, preferred_element_type=jnp.float32
    )
    if row_share < FACTOR_BLOCK:
        partner = from_partner(grad_right, "dp", 0)
        is_lower = my_dp % 2 == 0
        joined = jnp.where(
            is_lower,
            jnp.concatenate([grad_right, partner], 0),
            jnp.concatenate([partner, grad_right], 0),
        )
        complete_rows = joined[None, :, :]
    else:
        complete_rows = grad_right.reshape(per_dev, FACTOR_BLOCK, group_w)
    natural_step = jnp.einsum("jrk,jkl->jrl", inverse_rows, complete_rows, precision=precise_mode)
    return (natural_step.reshape(row_share, group_w), owned_out)


MIB = 1 << 20
VMEM_MIB = 64
AHEAD = 3
PROJECT_AHEAD = 6
HOP_PARTS = 2
SUM_PARTS = 2
OWNED_FLOPS = 20_000_000_000
ANY = pl.BlockSpec(memory_space=pl.ANY)
VMEM = pl.BlockSpec(memory_space=pltpu.VMEM)
SMEM = pl.BlockSpec(memory_space=pltpu.SMEM)
CORE, NEAR_X, NEAR_Y, FAR = 1, 2, 4, 6


def routes(me):
    first = jnp.where(me % 2 == 0, NEAR_X, NEAR_Y)
    return FAR, first, FAR - first, 0


def shaped(shape, dtype=f32):
    return jax.ShapeDtypeStruct(shape, dtype)


def call(body, name, out_shape, in_specs, out_specs, scratch=(), flops=0, moved=0):
    return pl.pallas_call(
        body,
        out_shape=out_shape,
        in_specs=in_specs,
        out_specs=out_specs,
        scratch_shapes=scratch,
        compiler_params=pltpu.CompilerParams(vmem_limit_bytes=VMEM_MIB * MIB),
        cost_estimate=pl.CostEstimate(flops=flops, bytes_accessed=moved, transcendentals=0),
        name=name,
    )


def start_all(sources, targets, sems, first=0):
    copies = [
        pltpu.make_async_copy(source, target, sems.at[first + i])
        for i, (source, target) in enumerate(zip(sources, targets))
    ]
    for copy in copies:
        copy.start()
    return copies


def fold_rows(rows):
    return rows + rows // 2


def encode(x, into):
    rows = x.shape[0]
    high = x.astype(bf16)
    into[:rows] = high
    base = high.astype(f32)
    left = (x - base) * pl.reciprocal(base, approx=True) * 256.0
    left = jnp.where(jnp.abs(base) < 1e-30, 0.0, jnp.clip(left, -1.0, 1.0))
    digit = jnp.floor(left * 63.5 + 64.0)
    first, second = digit[: rows // 2], digit[rows // 2 :]
    negative = second >= 64.0
    power = jnp.exp2(jnp.where(negative, second - 96.0, second - 32.0))
    packed = (first + 128.0) * power
    into[rows:] = jnp.where(negative, -packed, packed).astype(bf16)


def decode(ref):
    rows = ref.shape[0] * 2 // 3
    packed = ref[rows:].astype(f32)
    size = jnp.abs(packed)
    power = jnp.floor(jnp.log2(size) + 1e-3)
    first = jnp.floor(size * jnp.exp2(7.0 - power) + 0.5) - 128.0
    second = power + jnp.where(packed < 0.0, 89.0, 25.0)
    digit = jnp.concatenate([first, second], axis=0)
    base = ref[:rows].astype(f32)
    return base + base * ((digit - 63.5) * (1.0 / (63.5 * 256.0)))


def project_body(
    owner, rows_ref, cot_ref, act_ref, theirs, own_theirs, out_ref,
    held, cot, rows, left, grads, picks, slots, sems, out_sems, small_sems, pick_sems,
):
    count, tokens, share = held.shape
    group_w = cot.shape[1]
    samples = rows.shape[1]
    per_tile = share // FACTOR_BLOCK
    me = lax.axis_index("dp")
    z = lax.axis_index("tensor")
    half = count // 2
    tiles = [me ^ m ^ CORE for m in routes(me ^ CORE)] + [me ^ m for m in routes(me)]
    targets = [theirs.at[i] for i in range(half - 1)] + [own_theirs.at[0]]

    small = start_all([cot_ref, rows_ref], [cot, rows], small_sems)
    starts = [pl.multiple_of(t * share, share) for t in tiles]
    loads = [
        pltpu.make_async_copy(act_ref.at[:, pl.ds(start, share)], held.at[i], sems.at[i])
        for i, start in enumerate(starts)
    ]
    for load in loads[:PROJECT_AHEAD]:
        load.start()

    for d in range(count):
        slots[0, d] = 0
        slots[1, d] = 0
    for b in range(owner.shape[0]):
        holder = owner[b]
        rank = slots[0, holder]
        slots[0, holder] = rank + 1
        slots[1, holder] = jnp.where(rank == z, b, slots[1, holder])

    for copy in small:
        copy.wait()
    left[:group_w] = cot[...].astype(f32).T.astype(bf16)
    places = lax.broadcasted_iota(jnp.int32, (tokens, samples), 0)
    left[group_w:] = (places == rows[...]).astype(f32).T.astype(bf16)

    blocks = count * per_tile
    picks[blocks] = jnp.dot(left[group_w:], cot[...], preferred_element_type=f32).astype(bf16)
    stores = []

    def pass_on(block, many, dest, place, n):
        return start_all([picks.at[pl.ds(block, many)]], [out_ref.at[dest, pl.ds(place, many)]], pick_sems, n)

    for d in range(count):
        stores += pass_on(blocks, 1, d, 3, 3 * d + 2)
    for i in range(count):
        if i % 2 == 0:
            loads[i].wait()
            loads[i + 1].wait()
            for load in loads[i + PROJECT_AHEAD : i + PROJECT_AHEAD + 2]:
                load.start()
        if i < half:
            product = jnp.dot(left[...], held[i], preferred_element_type=f32)
            grads[i] = product[:group_w]
            stores += start_all([grads.at[i]], [targets[i]], out_sems, i)
            picked = product[group_w:]
        else:
            picked = jnp.dot(left[group_w:], held[i], preferred_element_type=f32)
        for j in range(per_tile):
            picks[tiles[i] * per_tile + j] = picked[
                :, j * FACTOR_BLOCK : (j + 1) * FACTOR_BLOCK
            ].astype(bf16)
        stores += pass_on(tiles[i] * per_tile + 2 * (z % 2), 2, tiles[i], 0, 3 * i)
    for d in range(count):
        stores += pass_on(slots[1, d], 1, d, 2, 3 * d + 1)
    for store in stores:
        store.wait()


def project(block_owner, sampled_rows, cotangent, activations, count):
    samples = sampled_rows.shape[0]
    tokens, group_w = cotangent.shape
    model_width = activations.shape[1]
    share = model_width // count
    one = shaped((1, group_w, share))
    rest = shaped((count // 2 - 1, group_w, share))
    return call(
        project_body,
        "project",
        (rest, one, shaped((count, 4, samples, FACTOR_BLOCK), bf16)),
        [SMEM, ANY, ANY, ANY],
        (ANY,) * 3,
        [
            pltpu.VMEM((count, tokens, share), bf16),
            pltpu.VMEM((tokens, group_w), bf16),
            pltpu.VMEM((1, samples), jnp.int32),
            pltpu.VMEM((group_w + samples, tokens), bf16),
            pltpu.VMEM((count // 2, group_w, share), f32),
            pltpu.VMEM((model_width // FACTOR_BLOCK + 1, samples, FACTOR_BLOCK), bf16),
            pltpu.SMEM((2, count), jnp.int32),
            pltpu.SemaphoreType.DMA((count,)),
            pltpu.SemaphoreType.DMA((count // 2,)),
            pltpu.SemaphoreType.DMA((2,)),
            pltpu.SemaphoreType.DMA((3 * count,)),
        ],
        flops=2 * tokens * (group_w + samples) * model_width,
        moved=2 * tokens * model_width + 2 * group_w * model_width,
    )(block_owner, sampled_rows[None, :], cotangent, activations)


def sum_body(which, cot_ref, act_ref, got_ref, *refs):
    count = len(which)
    outs, (cot, held, got, left, wire, plain, sems, got_sems, out_sems) = refs[-9 - count : -9], refs[-9:]
    width = held.shape[2]
    share = got_ref.shape[2]
    parts = share // width
    me = lax.axis_index("dp")
    starts = [pl.multiple_of((me ^ routes(me)[i]) * share, share) for i in which]
    work = [(i, p) for i in range(count) for p in range(parts)]
    first = start_all([cot_ref], [cot], sems)[0]

    def fetch(n):
        i, p = work[n]
        tile = act_ref.at[:, pl.ds(starts[i] + p * width, width)]
        come = got_ref.at[which[i], :, pl.ds(p * width, width)]
        return start_all([tile], [held.at[n]], sems, 1 + n) + start_all([come], [got.at[n]], got_sems, n)

    loads = [fetch(n) for n in range(min(AHEAD, len(work)))]
    first.wait()
    left[...] = cot[...].astype(f32).T.astype(bf16)
    stores = []
    for n, (i, p) in enumerate(work):
        loads[n][0].wait()
        if n + AHEAD < len(work):
            loads.append(fetch(n + AHEAD))
        product = jnp.dot(left[...], held[n], preferred_element_type=f32)
        loads[n][1].wait()
        if which[i] < 2:
            encode(product + got[n], wire.at[n])
            source = wire.at[n]
        else:
            plain[p] = product + got[n]
            source = plain.at[p]
        stores += start_all([source], [outs[i].at[:, pl.ds(p * width, width)]], out_sems, n)
    for store in stores:
        store.wait()


def hop_body(rest, come, _, out_ref, rest_in, come_in, out, sems, out_sems):
    parts = rest_in.shape[0]
    width = rest_in.shape[2]
    loads, stores = [], []
    for p in range(parts):
        columns = pl.ds(p * width, width)
        loads.append(start_all([rest.at[:, columns], come.at[:, columns]], [rest_in.at[p], come_in.at[p]], sems, 2 * p))
    for p in range(parts):
        for load in loads[p]:
            load.wait()
        encode(rest_in[p] + decode(come_in.at[p]), out.at[p])
        stores += start_all([out.at[p]], [out_ref.at[:, pl.ds(p * width, width)]], out_sems, p)
    for store in stores:
        store.wait()


def two(x):
    high = x.astype(bf16)
    return high, (x - high.astype(f32)).astype(bf16)


def newton_step(low, current, last):
    width = low.shape[0]
    high_part, low_part = two(low)

    def dot(a, b):
        return jnp.dot(a, b, preferred_element_type=f32)

    if current is None:
        mixed = dot(high_part, low_part)
        return 2.0 * low - (dot(high_part, high_part) + (mixed + mixed.T)), None
    current_high, current_low = two(current)
    if last:
        both = dot(jnp.concatenate([current_high, current_low], axis=0), high_part)
        return None, 2.0 * current - (both[:width] + (both[width:] + dot(current_high, low_part)))
    both = dot(jnp.concatenate([current_high, high_part, current_low], axis=0), high_part)
    mixed = dot(jnp.concatenate([current_high, high_part], axis=0), low_part)
    square = both[width : 2 * width] + (mixed[width:] + mixed[width:].T)
    return 2.0 * low - square, 2.0 * current - (both[:width] + (both[2 * width :] + mixed[:width]))


def places(extent):
    return (
        lax.broadcasted_iota(jnp.int32, (extent, extent), 0),
        lax.broadcasted_iota(jnp.int32, (extent, extent), 1),
    )


FOLD_ROWS = 16


def fold(matrix, into):
    half = matrix.shape[0] // 2
    row, column = places(half)
    low = matrix[half:, half:]
    both = jnp.where(row <= column, matrix[:half, :half], low)
    coded = fold_rows(half)
    encode(jnp.concatenate([both, matrix[:half, half:]], axis=1), into.at[:coded])
    left = jnp.sum(jnp.where(row == column, low, 0.0), axis=0, keepdims=True)
    line = lax.broadcasted_iota(jnp.int32, (FOLD_ROWS, 2 * half), 0)
    diagonal = jnp.zeros((FOLD_ROWS, 2 * half), f32)
    for part in range(3):
        high = left.astype(bf16).astype(f32)
        diagonal = jnp.where(line == part, jnp.concatenate([high, high], axis=1), diagonal)
        left = left - high
    into[coded:] = diagonal.astype(bf16)


def unfold(packed):
    half = packed.shape[1] // 2
    coded = fold_rows(half)
    row, column = places(half)
    values = decode(packed.at[:coded])
    diagonal = jnp.sum(packed[coded:].astype(f32), axis=0, keepdims=True)[:, :half]
    both, corner = values[:, :half], values[:, half:]
    turned = both.T
    top = jnp.where(row <= column, both, turned)
    low = jnp.where(row == column, diagonal, jnp.where(row > column, both, turned))
    return jnp.concatenate(
        [jnp.concatenate([top, corner], axis=1), jnp.concatenate([corner.T, low], axis=1)], axis=0
    )


def invert_body(scales, owner, rows_ref, _, all_ref, own_ref, out_ref):
    width = FACTOR_BLOCK
    me = lax.axis_index("dp")
    owned = jnp.int32(0)
    for b in range(owner.shape[0]):
        owned = owned + jnp.where(owner[b] == me, 1, 0)
    used = jnp.where(lax.axis_index("tensor") < owned, 1.0, 0.0).astype(f32)
    row, column = places(width)
    eye = (row == column).astype(f32)
    states = []
    for m in range(4):
        rows = rows_ref[:, m].reshape(-1, width)
        gram = lax.dot_general(
            rows, rows, (((0,), (0,)), ((), ())), preferred_element_type=f32
        )
        matrix = gram * scales[1 if m == 3 else 0] + DAMPING * eye
        bound = jnp.max(jnp.sum(jnp.abs(matrix), axis=1, keepdims=True), axis=0, keepdims=True)
        inverse_bound = 1.0 / bound
        low = matrix * inverse_bound
        states.append((low, (2.0 * eye - low) * inverse_bound))
    lows = [newton_step(low, None, False)[0] for low, _ in states]
    currents = [current for _, current in states]
    for turn in range(1, ITERS):
        stepped = [newton_step(low, current, turn == ITERS - 1) for low, current in zip(lows, currents)]
        lows, currents = [pair[0] for pair in stepped], [pair[1] for pair in stepped]
    fold(currents[0], all_ref.at[0])
    fold(currents[1], all_ref.at[1])
    fold(currents[2] * used, all_ref.at[2])
    own_ref[...] = all_ref[2]
    out_ref[...] = currents[3]


def owned_body(here, beside, two_off, three_off, _, out_ref, split, held, need, sems, need_sems):
    needs = start_all([here.at[pl.ds(0, 2)], beside.at[pl.ds(0, 2)]], [need.at[pl.ds(0, 2)], need.at[pl.ds(2, 2)]], need_sems)
    loads = start_all([here.at[2], beside.at[2], two_off, three_off], [held.at[k] for k in range(4)], sems)
    z = lax.axis_index("tensor")
    odd = z % 2
    for k in range(2):
        needs[k].wait()
        for p in range(2):
            high, low = two(unfold(need.at[2 * k + p]))
            at = 2 * (odd if k == 0 else 1 - odd) + p
            split[0, at] = high
            split[1, at] = low
    for k, load in enumerate(loads):
        load.wait()
        out_ref[z ^ k] = unfold(held.at[k])


def own_body(cot_ref, act_ref, got_ref, _, sum_ref, cot, held, got, sems):
    share = held.shape[1]
    start = pl.multiple_of(lax.axis_index("dp") * share, share)
    loads = start_all([cot_ref, act_ref.at[:, pl.ds(start, share)], got_ref.at[0]], [cot, held, got], sems)
    loads[0].wait()
    left = cot[...].astype(f32).T.astype(bf16)
    loads[1].wait()
    product = jnp.dot(left, held[...], preferred_element_type=f32)
    loads[2].wait()
    sum_ref[...] = product + got[...]


def near_body(own_ref, come, _, sum_ref, own, come_in, sems):
    loads = start_all([own_ref, come], [own, come_in], sems)
    for load in loads:
        load.wait()
    sum_ref[...] = own[...] + decode(come_in)


def finish_body(split_ref, g_ref, sum_ref, come, step_out, split, g_in, total, come_in, step, sems, out_sems):
    width = FACTOR_BLOCK
    loads = start_all([g_ref, come, sum_ref, split_ref], [g_in, come_in, total, split], sems)

    def dot(a, c, dims):
        return lax.dot_general(a, c, (dims, ((), ())), preferred_element_type=f32)

    loads[0].wait()
    left = jnp.concatenate([part.astype(f32).T for part in two(g_in[...])], axis=0).astype(bf16)
    for load in loads[1:3]:
        load.wait()
    sum_high, sum_low = two(total[...] + decode(come_in))
    both = dot(left, sum_high, ((1,), (0,)))
    right_high, right_low = two(both[:width] + (both[width:] + dot(left[:width], sum_low, ((1,), (0,)))))
    loads[3].wait()
    stores = []
    for b in range(split.shape[1]):
        part = slice(b * width, (b + 1) * width)
        both = dot(split[:, b].reshape(2 * width, width), right_high[:, part], ((1,), (1,)))
        step[b] = both[:width] + (both[width:] + dot(split[0, b], right_low[:, part], ((1,), (1,))))
        stores += start_all([step.at[b]], [step_out.at[part, :]], out_sems, b)
    for store in stores:
        store.wait()


def dma(count):
    return pltpu.SemaphoreType.DMA((count,))


def sum_cores(name, which, cotangent, activations, got, *after):
    tokens, group_w = cotangent.shape
    share = got.shape[2]
    wired = (fold_rows(group_w), share)
    steps, width = len(which) * SUM_PARTS, share // SUM_PARTS
    return call(
        functools.partial(sum_body, which),
        name,
        tuple(shaped(wired, bf16) if i < 2 else shaped((group_w, share)) for i in which),
        [ANY] * (3 + len(after)),
        (ANY,) * len(which),
        [
            pltpu.VMEM(cotangent.shape, bf16),
            pltpu.VMEM((steps, tokens, width), bf16),
            pltpu.VMEM((steps, group_w, width), f32),
            pltpu.VMEM((group_w, tokens), bf16),
            pltpu.VMEM((steps, wired[0], width), bf16),
            pltpu.VMEM((SUM_PARTS, group_w, width), f32),
            dma(1 + steps),
            dma(steps),
            dma(steps),
        ],
        moved=4 * MIB * len(which),
    )(cotangent, activations, got, *after)


def invert(block_owner, rows, after, scales):
    packed = shaped((fold_rows(FACTOR_BLOCK // 2) + FOLD_ROWS, FACTOR_BLOCK), bf16)
    return call(
        functools.partial(invert_body, scales),
        "invert_factors",
        (shaped((3, *packed.shape), bf16), packed, shaped((FACTOR_BLOCK, FACTOR_BLOCK))),
        [SMEM, VMEM, ANY],
        (VMEM,) * 3,
        flops=2 * 3 * 4 * 18 * FACTOR_BLOCK**3,
        moved=2 * MIB,
    )(block_owner, rows, after)


def hop(rest, come, after):
    group_w, share = rest.shape
    wired = come.shape
    width = share // HOP_PARTS
    return call(
        hop_body,
        "hop",
        shaped(wired, bf16),
        [ANY] * 3,
        ANY,
        [pltpu.VMEM((HOP_PARTS, group_w, width), f32)]
        + [pltpu.VMEM((HOP_PARTS, wired[0], width), bf16)] * 2
        + [dma(2 * HOP_PARTS), dma(HOP_PARTS)],
    )(rest, come, after)


def sum_own(cotangent, activations, own_got, after):
    tokens = cotangent.shape[0]
    _, group_w, share = own_got.shape
    return call(
        own_body,
        "sum_own",
        shaped((group_w, share)),
        [ANY] * 4,
        VMEM,
        [
            pltpu.VMEM(cotangent.shape, bf16),
            pltpu.VMEM((tokens, share), bf16),
            pltpu.VMEM((group_w, share), f32),
            dma(3),
        ],
    )(cotangent, activations, own_got, after)


def add_near(own, come, after):
    return call(
        near_body,
        "add_near",
        shaped(own.shape),
        [ANY] * 3,
        VMEM,
        [pltpu.VMEM(own.shape, f32), pltpu.VMEM(come.shape, bf16), dma(2)],
    )(own, come, after)


def owned_blocks(inverses, beside, two_off, three_off, after):
    square = (4, FACTOR_BLOCK, FACTOR_BLOCK)
    held = pltpu.VMEM((4, *two_off.shape), bf16)
    return call(
        owned_body,
        "owned",
        (shaped(square), shaped((2, *square), bf16)),
        [ANY] * 5,
        (VMEM,) * 2,
        [held, held, dma(4), dma(2)],
        flops=OWNED_FLOPS,
    )(inverses, beside, two_off, three_off, after)


def finish(split, g_inverse, so_far, come):
    group_w, share = so_far.shape
    blocks = share // FACTOR_BLOCK
    return call(
        finish_body,
        "finish",
        shaped((share, group_w)),
        [ANY] * 4,
        ANY,
        [
            pltpu.VMEM(split.shape, bf16),
            pltpu.VMEM(g_inverse.shape, f32),
            pltpu.VMEM(so_far.shape, f32),
            pltpu.VMEM(come.shape, bf16),
            pltpu.VMEM((blocks, FACTOR_BLOCK, group_w), f32),
            dma(4),
            dma(blocks),
        ],
        moved=6 * MIB,
    )(split, g_inverse, so_far, come)


def square_device(activations, cotangent, sampled_rows, block_owner):
    dp_count = lax.axis_size("dp")
    samples = sampled_rows.shape[0]

    def swap(block, bit, axis="dp"):
        count = lax.axis_size(axis)
        return lax.ppermute(block, axis, [(i, i ^ bit) for i in range(count)])

    def travel(block, even, odd):
        return lax.ppermute(block, "dp", [(i, i ^ (odd if i % 2 else even)) for i in range(dp_count)])

    theirs, own_theirs, picked = project(
        block_owner, sampled_rows, cotangent, activations, dp_count
    )
    got = swap(theirs, CORE)
    rows = lax.all_to_all(picked, "dp", split_axis=0, concat_axis=0, tiled=True)
    own_got = swap(own_theirs, CORE)

    (far,) = sum_cores("sum_far", (0,), cotangent, activations, got)
    far_come = travel(far, NEAR_X, NEAR_Y)
    near, rest = sum_cores("sum_near", (1, 2), cotangent, activations, got, far)
    near_come = travel(near, NEAR_X, NEAR_Y)
    own_sum = sum_own(cotangent, activations, own_got, rest)

    scales = (1.0 / (samples * dp_count), activations.shape[0] / samples)
    inverses, own, g_inverse = invert(block_owner, rows, own_sum, scales)
    beside = swap(inverses, 1, "tensor")
    two_off, three_off = swap(own, 2, "tensor"), swap(own, 3, "tensor")

    hopped = hop(rest, far_come, inverses)
    come_last = travel(hopped, NEAR_Y, NEAR_X)

    so_far = add_near(own_sum, near_come, hopped)
    owned, split = owned_blocks(inverses, beside, two_off, three_off, so_far)
    step = finish(split, g_inverse, so_far, come_last)
    return step, owned


def solution(mesh):
    def per_device(activations, cotangent, sampled_rows, block_owner):
        block_total = activations.shape[1] // FACTOR_BLOCK
        dp_count, depth = mesh.shape["dp"], mesh.shape["tensor"]
        fits = (
            dp_count == 8
            and depth == 4
            and block_total == dp_count * depth
            and cotangent.shape[1] == FACTOR_BLOCK
            and sampled_rows.shape[0] % 16 == 0
            and activations.shape[0] % 128 == 0
        )
        run = square_device if fits else general_device
        return run(activations, cotangent, sampled_rows, block_owner)

    return jax.shard_map(
        per_device,
        mesh=mesh,
        in_specs=(P("dp", None), P("dp", "tensor"), P("dp"), P()),
        out_specs=(P("dp", "tensor"), P("dp", None, None)),
        check_vma=False,
    )
```

time: 71.1 us -> 65.6 us (0.923)
  waiting for transfers between devices: 10.6 us -> 5.47 us
  Pallas kernels: 40.4 us -> 44.1 us
  local copies, waits for them, and re-layouts: 2.14 us -> 0 us
  starting transfers between devices: 16.1 us -> 14.8 us
    ppermute x9 -> x5, starting transfers between devices: 11 us -> 5.18 us  [swap(): return lax.ppermute(block, axis, [(i, i ^ bit) for i in range(count)])]
    ppermute x0 -> x3, starting transfers between devices: none -> 4.45 us  [travel(): lax.ppermute(block, 'dp', [(i, i ^ (odd if i % 2 else even)) for i in ran...]
    all_to_all x1, waiting for transfers between devices: 4.32 us -> 0.25 us  [square_device(): rows = lax.all_to_all(picked, 'dp', split_axis=0, concat_axis=0, tiled=True)]
    pallas_call x7 -> x9, Pallas kernels: 40.4 us -> 44.1 us  [the longest x1 9.91 us: invert(): call(functools.partial(invert_body, scales), 'invert_factors', (shaped((3...]
    ppermute x9 -> x5, waiting for transfers between devices: 6.25 us -> 3.23 us  [swap(): return lax.ppermute(block, axis, [(i, i ^ bit) for i in range(count)])]
    unnamed x6 -> x0, local copies, waits for them, and re-layouts: 2.14 us -> none
    ppermute x0 -> x3, waiting for transfers between devices: none -> 1.99 us  [travel(): lax.ppermute(block, 'dp', [(i, i ^ (odd if i % 2 else even)) for i in ran...]
  transfers between devices with their start and end apart: 10 -> 9, of which waited for: 5 -> 4; matrix products, arithmetic and copies ran while one was open for 0% -> 0% of each run, Pallas kernels for 38% -> 48%
where the time goes in v3:
time: 65.6 us; the launch traced here: 65.2 us
  Pallas kernels  44.1 us (67%)
  starting transfers between devices  14.8 us (23%)
  waiting for transfers between devices  5.47 us (8%)
  between operations  0.88 us (1%)
    pallas_call x1, Pallas kernels, invert(): call(functools.partial(invert_body, scales), 'invert_factors', (shaped((3...  9.91 us
    pallas_call x1, Pallas kernels, project(): call(project_body, 'project', (rest, one, shaped((count, 4, samples, FACT...  8.92 us
    pallas_call x2, Pallas kernels, sum_cores(): call(functools.partial(sum_body, which), name, tuple((shaped(wired, bf16)...  8.53 us
    ppermute x5, starting transfers between devices, swap(): return lax.ppermute(block, axis, [(i, i ^ bit) for i in range(count)])  5.18 us
    all_to_all x1, starting transfers between devices, square_device(): rows = lax.all_to_all(picked, 'dp', split_axis=0, concat_axis=0, tiled=True)  5.15 us
    ppermute x3, starting transfers between devices, travel(): lax.ppermute(block, 'dp', [(i, i ^ (odd if i % 2 else even)) for i in ran...  4.45 us
    pallas_call x1, Pallas kernels, finish(): call(finish_body, 'finish', shaped((share, group_w)), [ANY] * 4, ANY, [pl...  3.94 us
    pallas_call x1, Pallas kernels, sum_own(): call(own_body, 'sum_own', shaped((group_w, share)), [ANY] * 4, VMEM, [plt...  3.4 us
  transfers between devices with their start and end apart: 9, of which 4 were waited for; matrix products, arithmetic and copies ran while one was open for 0% of the time, Pallas kernels for 48%

profile of v3, /device:TPU:0, one launch (start us, length us, event | category | flops | bytes accessed | tf_op | source)
XLA Modules:
  0.0 65.2 jit_solution(2860476546022463734)
XLA Ops:
  0.6 8.9 %project.1 = (f32[3,256,1024]{2,1,0:T(8,128)}, f32[1,256,1024]{2,1,0:T(8,128)}, bf16[8,4,64,256]{3,2,1,0:T(8,128)(2,1)}) custom-call(s32[32]{0:T(128)} %owner.3, s32[1,64]{1,0:T(1,128)} %bitcast.1, bf16[768,256]{1,0:T(8,128)(2,1)} %cot_ref.7, bf16[768,8192]{1,0:T(8,128)(2,1)} %act_ref.7), custom_call_target="tpu_custom_call" | custom-call | flops 4026531840 | bytes 16777216 | tf_op jit(solution)/shard_map/project/pallas_call | solution.py:285
  9.6 0.5 collective-permute-start.1
  10.1 0.1 collective-permute-start
  10.2 5.2 %all-to-all-start = ((bf16[8,4,64,256]{3,2,1,0:T(8,128)(2,1)}), bf16[8,4,64,256]{3,2,1,0:T(8,128)(2,1)}, u32[]{:S(2)}, u32[]{:S(2)}) async-start(bf16[8,4,64,256]{3,2,1,0:T(8,128)(2,1)} %get-tuple-element.12), calls=%async_computation | async-start | bytes 2097152 | tf_op jit(solution)/shard_map/all_to_all | solution.py:662
  15.3 0.4 collective-permute-done.1.got_ref
  15.7 3.6 %sum_far.1.refs_0_ = bf16[384,1024]{1,0:T(8,128)(2,1)} custom-call(bf16[768,256]{1,0:T(8,128)(2,1)} %cot_ref.7, bf16[768,8192]{1,0:T(8,128)(2,1)} %act_ref.7, f32[3,256,1024]{2,1,0:T(8,128)} %collective-permute-done.1.got_ref), custom_call_target="tpu_custom_call" | custom-call | bytes 4194304 | tf_op jit(solution)/shard_map/sum_far/pallas_call | solution.py:532
  19.4 2.9 %collective-permute-start.6 = (bf16[384,1024]{1,0:T(8,128)(2,1)}, bf16[384,1024]{1,0:T(8,128)(2,1)}, u32[]{:S(2)}, u32[]{:S(2)}) collective-permute-start(bf16[384,1024]{1,0:T(8,128)(2,1)} %sum_far.1.refs_0_), channel_id=1, source_target_pairs={{0,8},{4,20},{8,0},{12,28},{16,24},{20,4},{24,16},{28,12},{1,9},{5... | collective-permute-start | bytes 2359304 | tf_op jit(solution)/shard_map/ppermute | solution.py:656
  22.3 4.9 %sum_near.1 = (bf16[384,1024]{1,0:T(8,128)(2,1)}, f32[256,1024]{1,0:T(8,128)}) custom-call(bf16[768,256]{1,0:T(8,128)(2,1)} %cot_ref.7, bf16[768,8192]{1,0:T(8,128)(2,1)} %act_ref.7, f32[3,256,1024]{2,1,0:T(8,128)} %collective-permute-done.1.got_ref, bf16[384,1024]{1,0:T(8,128)(2,1)} %sum_far.1.refs_0_), custom_call_target="tpu_custom_call" | custom-call | bytes 8388608 | tf_op jit(solution)/shard_map/sum_near/pallas_call | solution.py:532
  27.2 0.1 collective-permute-start.5
  27.3 0.0 collective-permute-done.got_ref
  27.3 3.4 %sum_own.1._.own_ref = f32[256,1024]{1,0:T(8,128)} custom-call(bf16[768,256]{1,0:T(8,128)(2,1)} %cot_ref.7, bf16[768,8192]{1,0:T(8,128)(2,1)} %act_ref.7, f32[1,256,1024]{2,1,0:T(8,128)} %collective-permute-done.got_ref, f32[256,1024]{1,0:T(8,128)} %get-tuple-element.15._.rest), custom_call_target="tpu_custom_call" | custom-call | tf_op jit(solution)/shard_map/sum_own/pallas_call | solution.py:585
  30.7 0.2 all-to-all-done.rows_ref
  30.9 9.9 %invert_factors.1 = (bf16[3,208,256]{2,1,0:T(8,128)(2,1)}, bf16[208,256]{1,0:T(8,128)(2,1)}, f32[256,256]{1,0:T(8,128)}) custom-call(s32[32]{0:T(128)} %owner.3, bf16[8,4,64,256]{3,2,1,0:T(8,128)(2,1)} %all-to-all-done.rows_ref, f32[256,1024]{1,0:T(8,128)} %sum_own.1._.own_ref), custom_call_target="tpu_custom_call" | custom-call | flops 7247757312 | bytes 2097152 | tf_op jit(solution)/shard_map/invert_factors/pallas_call | solution.py:555
  40.8 2.0 %collective-permute-start.2 = (bf16[3,208,256]{2,1,0:T(8,128)(2,1)}, bf16[3,208,256]{2,1,0:T(8,128)(2,1)}, u32[]{:S(2)}, u32[]{:S(2)}) collective-permute-start(bf16[3,208,256]{2,1,0:T(8,128)(2,1)} %get-tuple-element.16._.here), channel_id=1, source_target_pairs={{0,1},{1,0},{2,3},{3,2},{4,5},{5,4},{6,7},{7,6},{8,9},{9,8},{10,11... | collective-permute-start | bytes 958472 | tf_op jit(solution)/shard_map/ppermute | solution.py:653
  42.8 2.5 %collective-permute-start.4 = (bf16[208,256]{1,0:T(8,128)(2,1)}, bf16[208,256]{1,0:T(8,128)(2,1)}, u32[]{:S(2)}, u32[]{:S(2)}) collective-permute-start(bf16[208,256]{1,0:T(8,128)(2,1)} %get-tuple-element.17), channel_id=1, source_target_pairs={{0,3},{1,2},{2,1},{3,0},{4,7},{5,6},{6,5},{7,4},{8,11},{9,10},{10,... | collective-permute-start | bytes 319496 | tf_op jit(solution)/shard_map/ppermute | solution.py:653
  45.3 0.1 collective-permute-start.3
  45.4 0.0 collective-permute-done.6.come
  45.4 3.3 %hop.1._ = bf16[384,1024]{1,0:T(8,128)(2,1)} custom-call(f32[256,1024]{1,0:T(8,128)} %get-tuple-element.15._.rest, bf16[384,1024]{1,0:T(8,128)(2,1)} %collective-permute-done.6.come, bf16[3,208,256]{2,1,0:T(8,128)(2,1)} %get-tuple-element.16._.here), custom_call_target="tpu_custom_call" | custom-call | tf_op jit(solution)/shard_map/hop/pallas_call | solution.py:570
  48.7 1.4 %collective-permute-start.7 = (bf16[384,1024]{1,0:T(8,128)(2,1)}, bf16[384,1024]{1,0:T(8,128)(2,1)}, u32[]{:S(2)}, u32[]{:S(2)}) collective-permute-start(bf16[384,1024]{1,0:T(8,128)(2,1)} %hop.1._), channel_id=1, source_target_pairs={{0,16},{4,12},{8,24},{12,4},{16,0},{20,28},{24,8},{28,20},{1,17},{... | collective-permute-start | bytes 2359304 | tf_op jit(solution)/shard_map/ppermute | solution.py:656
  50.2 0.0 collective-permute-done.5.come
  50.2 2.9 %add_near.1._.sum_ref = f32[256,1024]{1,0:T(8,128)} custom-call(f32[256,1024]{1,0:T(8,128)} %sum_own.1._.own_ref, bf16[384,1024]{1,0:T(8,128)(2,1)} %collective-permute-done.5.come, bf16[384,1024]{1,0:T(8,128)(2,1)} %hop.1._), custom_call_target="tpu_custom_call" | custom-call | tf_op jit(solution)/shard_map/add_near/pallas_call | solution.py:601
  53.1 2.8 %collective-permute-done.4.three_off = bf16[208,256]{1,0:T(8,128)(2,1)} collective-permute-done((bf16[208,256]{1,0:T(8,128)(2,1)}, bf16[208,256]{1,0:T(8,128)(2,1)}, u32[]{:S(2)}, u32[]{:S(2)}) %collective-permute-start.4) | collective-permute-done | bytes 106528 | tf_op jit(solution)/shard_map/ppermute | solution.py:653
  55.9 0.0 collective-permute-done.3.two_off
  55.9 0.0 collective-permute-done.2.beside
  55.9 3.2 %owned.1 = (f32[4,256,256]{2,1,0:T(8,128)}, bf16[2,4,256,256]{3,2,1,0:T(8,128)(2,1)}) custom-call(bf16[3,208,256]{2,1,0:T(8,128)(2,1)} %get-tuple-element.16._.here, bf16[3,208,256]{2,1,0:T(8,128)(2,1)} %collective-permute-done.2.beside, bf16[208,256]{1,0:T(8,128)(2,1)} %collective-permute-done.3.two_off, bf16[208,256]{1,0:T(8,128)(2,1)} %collective-permute-done.4.three_off, ...), custom_call_target="tpu_custom_call" | custom-call | flops 20000000000 | tf_op jit(solution)/shard_map/owned/pallas_call | solution.py:614
  59.1 2.0 %collective-permute-done.7.come = bf16[384,1024]{1,0:T(8,128)(2,1)} collective-permute-done((bf16[384,1024]{1,0:T(8,128)(2,1)}, bf16[384,1024]{1,0:T(8,128)(2,1)}, u32[]{:S(2)}, u32[]{:S(2)}) %collective-permute-start.7) | collective-permute-done | bytes 786464 | tf_op jit(solution)/shard_map/ppermute | solution.py:656
  61.1 3.9 %finish.1 = f32[1024,256]{1,0:T(8,128)} custom-call(bf16[2,4,256,256]{3,2,1,0:T(8,128)(2,1)} %get-tuple-element.19.split_ref, f32[256,256]{1,0:T(8,128)} %get-tuple-element.20.g_ref, f32[256,1024]{1,0:T(8,128)} %add_near.1._.sum_ref, bf16[384,1024]{1,0:T(8,128)(2,1)} %collective-permute-done.7.come), custom_call_target="tpu_custom_call" | custom-call | bytes 6291456 | tf_op jit(solution)/shard_map/finish/pallas_call | solution.py:628
Async XLA Ops:
  9.6 6.1 %collective-permute-start.1 = (f32[3,256,1024]{2,1,0:T(8,128)}, f32[3,256,1024]{2,1,0:T(8,128)}, u32[]{:S(2)}, u32[]{:S(2)}) collective-permute-start(f32[3,256,1024]{2,1,0:T(8,128)} %get-tuple-element.14), channel_id=1, source_target_pairs={{0,4},{4,0},{8,12},{12,8},{16,20},{20,16},{24,28},{28,24},{1,5},{5... | collective-permute-start | bytes 9437192 | tf_op jit(solution)/shard_map/ppermute | solution.py:653
  10.1 17.2 %collective-permute-start = (f32[1,256,1024]{2,1,0:T(8,128)}, f32[1,256,1024]{2,1,0:T(8,128)}, u32[]{:S(2)}, u32[]{:S(2)}) collective-permute-start(f32[1,256,1024]{2,1,0:T(8,128)} %get-tuple-element.13), channel_id=1, source_target_pairs={{0,4},{4,0},{8,12},{12,8},{16,20},{20,16},{24,28},{28,24},{1,5},{5... | collective-permute-start | bytes 3145736 | tf_op jit(solution)/shard_map/ppermute | solution.py:653
  10.2 20.8 %all-to-all-start = ((bf16[8,4,64,256]{3,2,1,0:T(8,128)(2,1)}), bf16[8,4,64,256]{3,2,1,0:T(8,128)(2,1)}, u32[]{:S(2)}, u32[]{:S(2)}) async-start(bf16[8,4,64,256]{3,2,1,0:T(8,128)(2,1)} %get-tuple-element.12), calls=%async_computation | async-start | bytes 2097152 | tf_op jit(solution)/shard_map/all_to_all | solution.py:662
  19.4 26.1 %collective-permute-start.6 = (bf16[384,1024]{1,0:T(8,128)(2,1)}, bf16[384,1024]{1,0:T(8,128)(2,1)}, u32[]{:S(2)}, u32[]{:S(2)}) collective-permute-start(bf16[384,1024]{1,0:T(8,128)(2,1)} %sum_far.1.refs_0_), channel_id=1, source_target_pairs={{0,8},{4,20},{8,0},{12,28},{16,24},{20,4},{24,16},{28,12},{1,9},{5... | collective-permute-start | bytes 2359304 | tf_op jit(solution)/shard_map/ppermute | solution.py:656
  27.2 23.0 %collective-permute-start.5 = (bf16[384,1024]{1,0:T(8,128)(2,1)}, bf16[384,1024]{1,0:T(8,128)(2,1)}, u32[]{:S(2)}, u32[]{:S(2)}) collective-permute-start(bf16[384,1024]{1,0:T(8,128)(2,1)} %get-tuple-element.18), channel_id=1, source_target_pairs={{0,8},{4,20},{8,0},{12,28},{16,24},{20,4},{24,16},{28,12},{1,9},{5... | collective-permute-start | bytes 2359304 | tf_op jit(solution)/shard_map/ppermute | solution.py:656
  40.8 15.1 %collective-permute-start.2 = (bf16[3,208,256]{2,1,0:T(8,128)(2,1)}, bf16[3,208,256]{2,1,0:T(8,128)(2,1)}, u32[]{:S(2)}, u32[]{:S(2)}) collective-permute-start(bf16[3,208,256]{2,1,0:T(8,128)(2,1)} %get-tuple-element.16._.here), channel_id=1, source_target_pairs={{0,1},{1,0},{2,3},{3,2},{4,5},{5,4},{6,7},{7,6},{8,9},{9,8},{10,11... | collective-permute-start | bytes 958472 | tf_op jit(solution)/shard_map/ppermute | solution.py:653
  42.8 13.1 %collective-permute-start.4 = (bf16[208,256]{1,0:T(8,128)(2,1)}, bf16[208,256]{1,0:T(8,128)(2,1)}, u32[]{:S(2)}, u32[]{:S(2)}) collective-permute-start(bf16[208,256]{1,0:T(8,128)(2,1)} %get-tuple-element.17), channel_id=1, source_target_pairs={{0,3},{1,2},{2,1},{3,0},{4,7},{5,6},{6,5},{7,4},{8,11},{9,10},{10,... | collective-permute-start | bytes 319496 | tf_op jit(solution)/shard_map/ppermute | solution.py:653
  45.3 10.6 %collective-permute-start.3 = (bf16[208,256]{1,0:T(8,128)(2,1)}, bf16[208,256]{1,0:T(8,128)(2,1)}, u32[]{:S(2)}, u32[]{:S(2)}) collective-permute-start(bf16[208,256]{1,0:T(8,128)(2,1)} %get-tuple-element.17), channel_id=1, source_target_pairs={{0,2},{1,3},{2,0},{3,1},{4,6},{5,7},{6,4},{7,5},{8,10},{9,11},{10,... | collective-permute-start | bytes 319496 | tf_op jit(solution)/shard_map/ppermute | solution.py:653
  48.7 12.4 %collective-permute-start.7 = (bf16[384,1024]{1,0:T(8,128)(2,1)}, bf16[384,1024]{1,0:T(8,128)(2,1)}, u32[]{:S(2)}, u32[]{:S(2)}) collective-permute-start(bf16[384,1024]{1,0:T(8,128)(2,1)} %hop.1._), channel_id=1, source_target_pairs={{0,16},{4,12},{8,24},{12,4},{16,0},{20,28},{24,8},{28,20},{1,17},{... | collective-permute-start | bytes 2359304 | tf_op jit(solution)/shard_map/ppermute | solution.py:656

commit v4 on v3

--- a/solution.py
+++ b/solution.py
@@ -365,24 +365,24 @@
     return high, (x - high.astype(f32)).astype(bf16)
 
 
-def newton_step(low, current, last):
-    width = low.shape[0]
-    high_part, low_part = two(low)
-
+def newton_step(lows, currents, last):
     def dot(a, b):
         return jnp.dot(a, b, preferred_element_type=f32)
 
-    if current is None:
-        mixed = dot(high_part, low_part)
-        return 2.0 * low - (dot(high_part, high_part) + (mixed + mixed.T)), None
-    current_high, current_low = two(current)
-    if last:
-        both = dot(jnp.concatenate([current_high, current_low], axis=0), high_part)
-        return None, 2.0 * current - (both[:width] + (both[width:] + dot(current_high, low_part)))
-    both = dot(jnp.concatenate([current_high, high_part, current_low], axis=0), high_part)
-    mixed = dot(jnp.concatenate([current_high, high_part], axis=0), low_part)
-    square = both[width : 2 * width] + (mixed[width:] + mixed[width:].T)
-    return 2.0 * low - square, 2.0 * current - (both[:width] + (both[2 * width :] + mixed[:width]))
+    parts = [two(low) for low in lows]
+    next_lows, next_currents = [], []
+    if not last:
+        for low, (high_part, low_part) in zip(lows, parts):
+            mixed = dot(high_part, low_part)
+            next_lows.append(2.0 * low - (dot(high_part, high_part) + (mixed + mixed.T)))
+    for current, (high_part, low_part) in zip(currents, parts):
+        high, rest = two(current)
+        product = dot(
+            jnp.concatenate([high, rest, high], axis=1),
+            jnp.concatenate([high_part, high_part, low_part], axis=0),
+        )
+        next_currents.append(2.0 * current - product)
+    return next_lows, next_currents
 
 
 def places(extent):
@@ -427,39 +427,50 @@
     )
 
 
-def invert_body(scales, owner, rows_ref, _, all_ref, own_ref, out_ref):
-    width = FACTOR_BLOCK
+def inverses_of(samples, scale):
+    row, column = places(FACTOR_BLOCK)
+    eye = (row == column).astype(f32)
+    lows, currents = [], []
+    for rows in samples:
+        gram = lax.dot_general(
+            rows, rows, (((0,), (0,)), ((), ())), preferred_element_type=f32
+        )
+        matrix = gram * scale + DAMPING * eye
+        bound = jnp.max(jnp.sum(jnp.abs(matrix), axis=1, keepdims=True), axis=0, keepdims=True)
+        inverse_bound = 1.0 / bound
+        low = matrix * inverse_bound
+        lows.append(low)
+        currents.append((2.0 * eye - low) * inverse_bound)
+    lows = newton_step(lows, [], False)[0]
+    for turn in range(1, ITERS):
+        lows, currents = newton_step(lows, currents, turn == ITERS - 1)
+    return currents
+
+
+def invert_body(scale, owner, rows_ref, _, all_ref, own_ref, rows, sem):
+    load = start_all([rows_ref.at[:, pl.ds(0, 3)]], [rows], sem)[0]
     me = lax.axis_index("dp")
     owned = jnp.int32(0)
     for b in range(owner.shape[0]):
         owned = owned + jnp.where(owner[b] == me, 1, 0)
     used = jnp.where(lax.axis_index("tensor") < owned, 1.0, 0.0).astype(f32)
-    row, column = places(width)
-    eye = (row == column).astype(f32)
-    states = []
-    for m in range(4):
-        rows = rows_ref[:, m].reshape(-1, width)
-        gram = lax.dot_general(
-            rows, rows, (((0,), (0,)), ((), ())), preferred_element_type=f32
-        )
-        matrix = gram * scales[1 if m == 3 else 0] + DAMPING * eye
-        bound = jnp.max(jnp.sum(jnp.abs(matrix), axis=1, keepdims=True), axis=0, keepdims=True)
-        inverse_bound = 1.0 / bound
-        low = matrix * inverse_bound
-        states.append((low, (2.0 * eye - low) * inverse_bound))
-    lows = [newton_step(low, None, False)[0] for low, _ in states]
-    currents = [current for _, current in states]
-    for turn in range(1, ITERS):
-        stepped = [newton_step(low, current, turn == ITERS - 1) for low, current in zip(lows, currents)]
-        lows, currents = [pair[0] for pair in stepped], [pair[1] for pair in stepped]
-    fold(currents[0], all_ref.at[0])
-    fold(currents[1], all_ref.at[1])
-    fold(currents[2] * used, all_ref.at[2])
+    load.wait()
+    first, second, own = inverses_of([rows[:, m].reshape(-1, FACTOR_BLOCK) for m in range(3)], scale)
+    fold(first, all_ref.at[0])
+    fold(second, all_ref.at[1])
+    fold(own * used, all_ref.at[2])
     own_ref[...] = all_ref[2]
-    out_ref[...] = currents[3]
-
-
-def owned_body(here, beside, two_off, three_off, _, out_ref, split, held, need, sems, need_sems):
+
+
+def group_body(scale, rows_ref, _, __, out_ref, rows, sem):
+    load = start_all([rows_ref.at[:, 3]], [rows], sem)[0]
+    load.wait()
+    parts = two(inverses_of([rows[...].reshape(-1, FACTOR_BLOCK)], scale)[0].T)
+    out_ref[...] = jnp.concatenate(parts, axis=0)
+
+
+def owned_body(own_ref, near_ref, here, beside, two_off, three_off, _, sum_ref, out_ref, split, own, near, held, need, sems, need_sems):
+    sums = start_all([own_ref, near_ref], [own, near], need_sems, 2)
     needs = start_all([here.at[pl.ds(0, 2)], beside.at[pl.ds(0, 2)]], [need.at[pl.ds(0, 2)], need.at[pl.ds(2, 2)]], need_sems)
     loads = start_all([here.at[2], beside.at[2], two_off, three_off], [held.at[k] for k in range(4)], sems)
     z = lax.axis_index("tensor")
@@ -471,6 +482,9 @@
             at = 2 * (odd if k == 0 else 1 - odd) + p
             split[0, at] = high
             split[1, at] = low
+    for load in sums:
+        load.wait()
+    sum_ref[...] = own[...] + decode(near)
     for k, load in enumerate(loads):
         load.wait()
         out_ref[z ^ k] = unfold(held.at[k])
@@ -488,26 +502,17 @@
     sum_ref[...] = product + got[...]
 
 
-def near_body(own_ref, come, _, sum_ref, own, come_in, sems):
-    loads = start_all([own_ref, come], [own, come_in], sems)
-    for load in loads:
-        load.wait()
-    sum_ref[...] = own[...] + decode(come_in)
-
-
-def finish_body(split_ref, g_ref, sum_ref, come, step_out, split, g_in, total, come_in, step, sems, out_sems):
+def finish_body(split_ref, g_ref, sum_ref, come, step_out, split, left, total, come_in, step, sems, out_sems):
     width = FACTOR_BLOCK
-    loads = start_all([g_ref, come, sum_ref, split_ref], [g_in, come_in, total, split], sems)
+    loads = start_all([g_ref, sum_ref, come, split_ref], [left, total, come_in, split], sems)
 
     def dot(a, c, dims):
         return lax.dot_general(a, c, (dims, ((), ())), preferred_element_type=f32)
 
-    loads[0].wait()
-    left = jnp.concatenate([part.astype(f32).T for part in two(g_in[...])], axis=0).astype(bf16)
-    for load in loads[1:3]:
+    for load in loads[:3]:
         load.wait()
     sum_high, sum_low = two(total[...] + decode(come_in))
-    both = dot(left, sum_high, ((1,), (0,)))
+    both = dot(left[...], sum_high, ((1,), (0,)))
     right_high, right_low = two(both[:width] + (both[width:] + dot(left[:width], sum_low, ((1,), (0,)))))
     loads[3].wait()
     stores = []
@@ -550,17 +555,31 @@
     )(cotangent, activations, got, *after)
 
 
-def invert(block_owner, rows, after, scales):
+def invert(block_owner, rows, after, scale):
+    _, kinds, samples, _ = rows.shape
     packed = shaped((fold_rows(FACTOR_BLOCK // 2) + FOLD_ROWS, FACTOR_BLOCK), bf16)
     return call(
-        functools.partial(invert_body, scales),
-        "invert_factors",
-        (shaped((3, *packed.shape), bf16), packed, shaped((FACTOR_BLOCK, FACTOR_BLOCK))),
-        [SMEM, VMEM, ANY],
-        (VMEM,) * 3,
+        functools.partial(invert_body, scale),
+        "invert_blocks",
+        (shaped((3, *packed.shape), bf16), packed),
+        [SMEM, ANY, ANY],
+        (VMEM,) * 2,
+        [pltpu.VMEM((rows.shape[0], 3, samples, FACTOR_BLOCK), bf16), dma(1)],
         flops=2 * 3 * 4 * 18 * FACTOR_BLOCK**3,
         moved=2 * MIB,
     )(block_owner, rows, after)
+
+
+def invert_group(rows, after, and_after, scale):
+    samples = rows.shape[2]
+    return call(
+        functools.partial(group_body, scale),
+        "invert_group",
+        shaped((2 * FACTOR_BLOCK, FACTOR_BLOCK), bf16),
+        [ANY] * 3,
+        VMEM,
+        [pltpu.VMEM((rows.shape[0], samples, FACTOR_BLOCK), bf16), dma(1)],
+    )(rows, after, and_after)
 
 
 def hop(rest, come, after):
@@ -597,32 +616,21 @@
     )(cotangent, activations, own_got, after)
 
 
-def add_near(own, come, after):
-    return call(
-        near_body,
-        "add_near",
-        shaped(own.shape),
-        [ANY] * 3,
-        VMEM,
-        [pltpu.VMEM(own.shape, f32), pltpu.VMEM(come.shape, bf16), dma(2)],
-    )(own, come, after)
-
-
-def owned_blocks(inverses, beside, two_off, three_off, after):
+def owned_blocks(own_sum, near, inverses, beside, two_off, three_off, after):
     square = (4, FACTOR_BLOCK, FACTOR_BLOCK)
     held = pltpu.VMEM((4, *two_off.shape), bf16)
     return call(
         owned_body,
         "owned",
-        (shaped(square), shaped((2, *square), bf16)),
-        [ANY] * 5,
-        (VMEM,) * 2,
-        [held, held, dma(4), dma(2)],
+        (shaped(own_sum.shape), shaped(square), shaped((2, *square), bf16)),
+        [ANY] * 7,
+        (VMEM,) * 3,
+        [pltpu.VMEM(own_sum.shape, f32), pltpu.VMEM(near.shape, bf16), held, held, dma(4), dma(4)],
         flops=OWNED_FLOPS,
-    )(inverses, beside, two_off, three_off, after)
-
-
-def finish(split, g_inverse, so_far, come):
+    )(own_sum, near, inverses, beside, two_off, three_off, after)
+
+
+def finish(split, g_parts, so_far, come):
     group_w, share = so_far.shape
     blocks = share // FACTOR_BLOCK
     return call(
@@ -633,7 +641,7 @@
         ANY,
         [
             pltpu.VMEM(split.shape, bf16),
-            pltpu.VMEM(g_inverse.shape, f32),
+            pltpu.VMEM(g_parts.shape, bf16),
             pltpu.VMEM(so_far.shape, f32),
             pltpu.VMEM(come.shape, bf16),
             pltpu.VMEM((blocks, FACTOR_BLOCK, group_w), f32),
@@ -641,7 +649,7 @@
             dma(blocks),
         ],
         moved=6 * MIB,
-    )(split, g_inverse, so_far, come)
+    )(split, g_parts, so_far, come)
 
 
 def square_device(activations, cotangent, sampled_rows, block_owner):
@@ -668,17 +676,16 @@
     near_come = travel(near, NEAR_X, NEAR_Y)
     own_sum = sum_own(cotangent, activations, own_got, rest)
 
-    scales = (1.0 / (samples * dp_count), activations.shape[0] / samples)
-    inverses, own, g_inverse = invert(block_owner, rows, own_sum, scales)
+    inverses, own = invert(block_owner, rows, own_sum, 1.0 / (samples * dp_count))
     beside = swap(inverses, 1, "tensor")
     two_off, three_off = swap(own, 2, "tensor"), swap(own, 3, "tensor")
 
     hopped = hop(rest, far_come, inverses)
     come_last = travel(hopped, NEAR_Y, NEAR_X)
 
-    so_far = add_near(own_sum, near_come, hopped)
-    owned, split = owned_blocks(inverses, beside, two_off, three_off, so_far)
-    step = finish(split, g_inverse, so_far, come_last)
+    g_parts = invert_group(rows, near_come, hopped, activations.shape[0] / samples)
+    so_far, owned, split = owned_blocks(own_sum, near_come, inverses, beside, two_off, three_off, g_parts)
+    step = finish(split, g_parts, so_far, come_last)
     return step, owned
 
 

time: 65.6 us -> 64.1 us (0.977)
  waiting for transfers between devices: 5.47 us -> 1.5 us
  Pallas kernels: 44.1 us -> 46.4 us
    pallas_call x3, Pallas kernels: 16 us -> 18.5 us  [the longest x1 8.5 us: invert(): call(functools.partial(invert_body, scale), 'invert_blocks', (shaped((3,...]
    ppermute x5, waiting for transfers between devices: 3.23 us -> 0.84 us  [swap(): return lax.ppermute(block, axis, [(i, i ^ bit) for i in range(count)])]
    ppermute x3, waiting for transfers between devices: 1.99 us -> 0.43 us  [travel(): lax.ppermute(block, 'dp', [(i, i ^ (odd if i % 2 else even)) for i in ran...]
  transfers between devices with their start and end apart: 9 -> 9, of which waited for: 4 -> 4; matrix products, arithmetic and copies ran while one was open for 0% -> 0% of each run, Pallas kernels for 48% -> 53%
where the time goes in v4:
time: 64.1 us; the launch traced here: 63.7 us
  Pallas kernels  46.4 us (72%)
  starting transfers between devices  14.9 us (23%)
  waiting for transfers between devices  1.5 us (2%)
  between operations  0.88 us (1%)
    pallas_call x1, Pallas kernels, project(): call(project_body, 'project', (rest, one, shaped((count, 4, samples, FACT...  8.92 us
    pallas_call x2, Pallas kernels, sum_cores(): call(functools.partial(sum_body, which), name, tuple((shaped(wired, bf16)...  8.54 us
    pallas_call x1, Pallas kernels, invert(): call(functools.partial(invert_body, scale), 'invert_blocks', (shaped((3,...  8.5 us
    pallas_call x1, Pallas kernels, invert_group(): call(functools.partial(group_body, scale), 'invert_group', shaped((2 * FA...  5.47 us
    ppermute x5, starting transfers between devices, swap(): return lax.ppermute(block, axis, [(i, i ^ bit) for i in range(count)])  5.25 us
    all_to_all x1, starting transfers between devices, square_device(): rows = lax.all_to_all(picked, 'dp', split_axis=0, concat_axis=0, tiled=True)  5.15 us
    pallas_call x1, Pallas kernels, owned_blocks(): call(owned_body, 'owned', (shaped(own_sum.shape), shaped(square), shaped(...  4.57 us
    ppermute x3, starting transfers between devices, travel(): lax.ppermute(block, 'dp', [(i, i ^ (odd if i % 2 else even)) for i in ran...  4.46 us
  transfers between devices with their start and end apart: 9, of which 4 were waited for; matrix products, arithmetic and copies ran while one was open for 0% of the time, Pallas kernels for 53%

profile of v4, /device:TPU:0, one launch (start us, length us, event | category | flops | bytes accessed | tf_op | source)
XLA Modules:
  0.0 63.7 jit_solution(11777553360019662314)
XLA Ops:
  0.6 8.9 %project.1 = (f32[3,256,1024]{2,1,0:T(8,128)}, f32[1,256,1024]{2,1,0:T(8,128)}, bf16[8,4,64,256]{3,2,1,0:T(8,128)(2,1)}) custom-call(s32[32]{0:T(128)} %owner.3, s32[1,64]{1,0:T(1,128)} %bitcast.1, bf16[768,256]{1,0:T(8,128)(2,1)} %cot_ref.7, bf16[768,8192]{1,0:T(8,128)(2,1)} %act_ref.7), custom_call_target="tpu_custom_call" | custom-call | flops 4026531840 | bytes 16777216 | tf_op jit(solution)/shard_map/project/pallas_call | solution.py:285
  9.6 0.5 collective-permute-start.1
  10.1 0.1 collective-permute-start
  10.2 5.2 %all-to-all-start = ((bf16[8,4,64,256]{3,2,1,0:T(8,128)(2,1)}), bf16[8,4,64,256]{3,2,1,0:T(8,128)(2,1)}, u32[]{:S(2)}, u32[]{:S(2)}) async-start(bf16[8,4,64,256]{3,2,1,0:T(8,128)(2,1)} %get-tuple-element.16), calls=%async_computation | async-start | bytes 2097152 | tf_op jit(solution)/shard_map/all_to_all | solution.py:670
  15.3 0.4 collective-permute-done.1.got_ref
  15.7 3.7 %sum_far.1.refs_0_ = bf16[384,1024]{1,0:T(8,128)(2,1)} custom-call(bf16[768,256]{1,0:T(8,128)(2,1)} %cot_ref.7, bf16[768,8192]{1,0:T(8,128)(2,1)} %act_ref.7, f32[3,256,1024]{2,1,0:T(8,128)} %collective-permute-done.1.got_ref), custom_call_target="tpu_custom_call" | custom-call | bytes 4194304 | tf_op jit(solution)/shard_map/sum_far/pallas_call | solution.py:537
  19.4 2.9 %collective-permute-start.6 = (bf16[384,1024]{1,0:T(8,128)(2,1)}, bf16[384,1024]{1,0:T(8,128)(2,1)}, u32[]{:S(2)}, u32[]{:S(2)}) collective-permute-start(bf16[384,1024]{1,0:T(8,128)(2,1)} %sum_far.1.refs_0_), channel_id=1, source_target_pairs={{0,8},{4,20},{8,0},{12,28},{16,24},{20,4},{24,16},{28,12},{1,9},{5... | collective-permute-start | bytes 2359304 | tf_op jit(solution)/shard_map/ppermute | solution.py:664
  22.3 4.9 %sum_near.1 = (bf16[384,1024]{1,0:T(8,128)(2,1)}, f32[256,1024]{1,0:T(8,128)}) custom-call(bf16[768,256]{1,0:T(8,128)(2,1)} %cot_ref.7, bf16[768,8192]{1,0:T(8,128)(2,1)} %act_ref.7, f32[3,256,1024]{2,1,0:T(8,128)} %collective-permute-done.1.got_ref, bf16[384,1024]{1,0:T(8,128)(2,1)} %sum_far.1.refs_0_), custom_call_target="tpu_custom_call" | custom-call | bytes 8388608 | tf_op jit(solution)/shard_map/sum_near/pallas_call | solution.py:537
  27.2 0.1 collective-permute-start.2
  27.3 0.0 collective-permute-done.got_ref
  27.3 3.4 %sum_own.1._.own_ref = f32[256,1024]{1,0:T(8,128)} custom-call(bf16[768,256]{1,0:T(8,128)(2,1)} %cot_ref.7, bf16[768,8192]{1,0:T(8,128)(2,1)} %act_ref.7, f32[1,256,1024]{2,1,0:T(8,128)} %collective-permute-done.got_ref, f32[256,1024]{1,0:T(8,128)} %get-tuple-element.14._.rest), custom_call_target="tpu_custom_call" | custom-call | tf_op jit(solution)/shard_map/sum_own/pallas_call | solution.py:604
  30.7 0.2 all-to-all-done.rows_ref
  30.9 8.5 %invert_blocks.1 = (bf16[3,208,256]{2,1,0:T(8,128)(2,1)}, bf16[208,256]{1,0:T(8,128)(2,1)}) custom-call(s32[32]{0:T(128)} %owner.3, bf16[8,4,64,256]{3,2,1,0:T(8,128)(2,1)} %all-to-all-done.rows_ref, f32[256,1024]{1,0:T(8,128)} %sum_own.1._.own_ref), custom_call_target="tpu_custom_call" | custom-call | flops 7247757312 | bytes 2097152 | tf_op jit(solution)/shard_map/invert_blocks/pallas_call | solution.py:561
  39.4 2.1 %collective-permute-start.3 = (bf16[3,208,256]{2,1,0:T(8,128)(2,1)}, bf16[3,208,256]{2,1,0:T(8,128)(2,1)}, u32[]{:S(2)}, u32[]{:S(2)}) collective-permute-start(bf16[3,208,256]{2,1,0:T(8,128)(2,1)} %get-tuple-element.17._.here), channel_id=1, source_target_pairs={{0,1},{1,0},{2,3},{3,2},{4,5},{5,4},{6,7},{7,6},{8,9},{9,8},{10,11... | collective-permute-start | bytes 958472 | tf_op jit(solution)/shard_map/ppermute | solution.py:661
  41.5 2.5 %collective-permute-start.5 = (bf16[208,256]{1,0:T(8,128)(2,1)}, bf16[208,256]{1,0:T(8,128)(2,1)}, u32[]{:S(2)}, u32[]{:S(2)}) collective-permute-start(bf16[208,256]{1,0:T(8,128)(2,1)} %get-tuple-element.18), channel_id=1, source_target_pairs={{0,3},{1,2},{2,1},{3,0},{4,7},{5,6},{6,5},{7,4},{8,11},{9,10},{10,... | collective-permute-start | bytes 319496 | tf_op jit(solution)/shard_map/ppermute | solution.py:661
  44.0 0.1 collective-permute-start.4
  44.1 0.0 collective-permute-done.6.come
  44.1 3.1 %hop.1.__ = bf16[384,1024]{1,0:T(8,128)(2,1)} custom-call(f32[256,1024]{1,0:T(8,128)} %get-tuple-element.14._.rest, bf16[384,1024]{1,0:T(8,128)(2,1)} %collective-permute-done.6.come, bf16[3,208,256]{2,1,0:T(8,128)(2,1)} %get-tuple-element.17._.here), custom_call_target="tpu_custom_call" | custom-call | tf_op jit(solution)/shard_map/hop/pallas_call | solution.py:589
  47.2 1.4 %collective-permute-start.7 = (bf16[384,1024]{1,0:T(8,128)(2,1)}, bf16[384,1024]{1,0:T(8,128)(2,1)}, u32[]{:S(2)}, u32[]{:S(2)}) collective-permute-start(bf16[384,1024]{1,0:T(8,128)(2,1)} %hop.1.__), channel_id=1, source_target_pairs={{0,16},{4,12},{8,24},{12,4},{16,0},{20,28},{24,8},{28,20},{1,17},{... | collective-permute-start | bytes 2359304 | tf_op jit(solution)/shard_map/ppermute | solution.py:664
  48.6 0.0 collective-permute-done.2._.near_ref
  48.6 5.5 %invert_group.1._.g_ref = bf16[512,256]{1,0:T(8,128)(2,1)} custom-call(bf16[8,4,64,256]{3,2,1,0:T(8,128)(2,1)} %all-to-all-done.rows_ref, bf16[384,1024]{1,0:T(8,128)(2,1)} %collective-permute-done.2._.near_ref, bf16[384,1024]{1,0:T(8,128)(2,1)} %hop.1.__), custom_call_target="tpu_custom_call" | custom-call | tf_op jit(solution)/shard_map/invert_group/pallas_call | solution.py:575
  54.1 0.4 collective-permute-done.5.three_off
  54.6 0.0 collective-permute-done.4.two_off
  54.6 0.0 collective-permute-done.3.beside
  54.6 4.6 %owned.1 = (f32[256,1024]{1,0:T(8,128)}, f32[4,256,256]{2,1,0:T(8,128)}, bf16[2,4,256,256]{3,2,1,0:T(8,128)(2,1)}) custom-call(f32[256,1024]{1,0:T(8,128)} %sum_own.1._.own_ref, bf16[384,1024]{1,0:T(8,128)(2,1)} %collective-permute-done.2._.near_ref, bf16[3,208,256]{2,1,0:T(8,128)(2,1)} %get-tuple-element.17._.here, ...), custom_call_target="tpu_custom_call" | custom-call | flops 20000000000 | tf_op jit(solution)/shard_map/owned/pallas_call | solution.py:622
  59.1 0.4 collective-permute-done.7.come
  59.6 3.9 %finish.1 = f32[1024,256]{1,0:T(8,128)} custom-call(bf16[2,4,256,256]{3,2,1,0:T(8,128)(2,1)} %get-tuple-element.19.split_ref, bf16[512,256]{1,0:T(8,128)(2,1)} %invert_group.1._.g_ref, f32[256,1024]{1,0:T(8,128)} %get-tuple-element.20.sum_ref, bf16[384,1024]{1,0:T(8,128)(2,1)} %collective-permute-done.7.come), custom_call_target="tpu_custom_call" | custom-call | bytes 6291456 | tf_op jit(solution)/shard_map/finish/pallas_call | solution.py:636
Async XLA Ops:
  9.6 6.1 %collective-permute-start.1 = (f32[3,256,1024]{2,1,0:T(8,128)}, f32[3,256,1024]{2,1,0:T(8,128)}, u32[]{:S(2)}, u32[]{:S(2)}) collective-permute-start(f32[3,256,1024]{2,1,0:T(8,128)} %get-tuple-element.13), channel_id=1, source_target_pairs={{0,4},{4,0},{8,12},{12,8},{16,20},{20,16},{24,28},{28,24},{1,5},{5... | collective-permute-start | bytes 9437192 | tf_op jit(solution)/shard_map/ppermute | solution.py:661
  10.1 17.2 %collective-permute-start = (f32[1,256,1024]{2,1,0:T(8,128)}, f32[1,256,1024]{2,1,0:T(8,128)}, u32[]{:S(2)}, u32[]{:S(2)}) collective-permute-start(f32[1,256,1024]{2,1,0:T(8,128)} %get-tuple-element.12), channel_id=1, source_target_pairs={{0,4},{4,0},{8,12},{12,8},{16,20},{20,16},{24,28},{28,24},{1,5},{5... | collective-permute-start | bytes 3145736 | tf_op jit(solution)/shard_map/ppermute | solution.py:661
  10.2 20.8 %all-to-all-start = ((bf16[8,4,64,256]{3,2,1,0:T(8,128)(2,1)}), bf16[8,4,64,256]{3,2,1,0:T(8,128)(2,1)}, u32[]{:S(2)}, u32[]{:S(2)}) async-start(bf16[8,4,64,256]{3,2,1,0:T(8,128)(2,1)} %get-tuple-element.16), calls=%async_computation | async-start | bytes 2097152 | tf_op jit(solution)/shard_map/all_to_all | solution.py:670
  19.4 24.7 %collective-permute-start.6 = (bf16[384,1024]{1,0:T(8,128)(2,1)}, bf16[384,1024]{1,0:T(8,128)(2,1)}, u32[]{:S(2)}, u32[]{:S(2)}) collective-permute-start(bf16[384,1024]{1,0:T(8,128)(2,1)} %sum_far.1.refs_0_), channel_id=1, source_target_pairs={{0,8},{4,20},{8,0},{12,28},{16,24},{20,4},{24,16},{28,12},{1,9},{5... | collective-permute-start | bytes 2359304 | tf_op jit(solution)/shard_map/ppermute | solution.py:664
  27.2 21.5 %collective-permute-start.2 = (bf16[384,1024]{1,0:T(8,128)(2,1)}, bf16[384,1024]{1,0:T(8,128)(2,1)}, u32[]{:S(2)}, u32[]{:S(2)}) collective-permute-start(bf16[384,1024]{1,0:T(8,128)(2,1)} %get-tuple-element.15), channel_id=1, source_target_pairs={{0,8},{4,20},{8,0},{12,28},{16,24},{20,4},{24,16},{28,12},{1,9},{5... | collective-permute-start | bytes 2359304 | tf_op jit(solution)/shard_map/ppermute | solution.py:664
  39.4 15.1 %collective-permute-start.3 = (bf16[3,208,256]{2,1,0:T(8,128)(2,1)}, bf16[3,208,256]{2,1,0:T(8,128)(2,1)}, u32[]{:S(2)}, u32[]{:S(2)}) collective-permute-start(bf16[3,208,256]{2,1,0:T(8,128)(2,1)} %get-tuple-element.17._.here), channel_id=1, source_target_pairs={{0,1},{1,0},{2,3},{3,2},{4,5},{5,4},{6,7},{7,6},{8,9},{9,8},{10,11... | collective-permute-start | bytes 958472 | tf_op jit(solution)/shard_map/ppermute | solution.py:661
  41.5 13.1 %collective-permute-start.5 = (bf16[208,256]{1,0:T(8,128)(2,1)}, bf16[208,256]{1,0:T(8,128)(2,1)}, u32[]{:S(2)}, u32[]{:S(2)}) collective-permute-start(bf16[208,256]{1,0:T(8,128)(2,1)} %get-tuple-element.18), channel_id=1, source_target_pairs={{0,3},{1,2},{2,1},{3,0},{4,7},{5,6},{6,5},{7,4},{8,11},{9,10},{10,... | collective-permute-start | bytes 319496 | tf_op jit(solution)/shard_map/ppermute | solution.py:661
  44.0 10.6 %collective-permute-start.4 = (bf16[208,256]{1,0:T(8,128)(2,1)}, bf16[208,256]{1,0:T(8,128)(2,1)}, u32[]{:S(2)}, u32[]{:S(2)}) collective-permute-start(bf16[208,256]{1,0:T(8,128)(2,1)} %get-tuple-element.18), channel_id=1, source_target_pairs={{0,2},{1,3},{2,0},{3,1},{4,6},{5,7},{6,4},{7,5},{8,10},{9,11},{10,... | collective-permute-start | bytes 319496 | tf_op jit(solution)/shard_map/ppermute | solution.py:661
  47.2 12.4 %collective-permute-start.7 = (bf16[384,1024]{1,0:T(8,128)(2,1)}, bf16[384,1024]{1,0:T(8,128)(2,1)}, u32[]{:S(2)}, u32[]{:S(2)}) collective-permute-start(bf16[384,1024]{1,0:T(8,128)(2,1)} %hop.1.__), channel_id=1, source_target_pairs={{0,16},{4,12},{8,24},{12,4},{16,0},{20,28},{24,8},{28,20},{1,17},{... | collective-permute-start | bytes 2359304 | tf_op jit(solution)/shard_map/ppermute | solution.py:664

commit v5 on v4

--- a/solution.py
+++ b/solution.py
@@ -129,7 +129,9 @@
 
 
 MIB = 1 << 20
-VMEM_MIB = 64
+VMEM_MIB = 32
+PROJECT_MIB = 64
+SUM_MIB = 64
 AHEAD = 3
 PROJECT_AHEAD = 6
 HOP_PARTS = 2
@@ -150,14 +152,14 @@
     return jax.ShapeDtypeStruct(shape, dtype)
 
 
-def call(body, name, out_shape, in_specs, out_specs, scratch=(), flops=0, moved=0):
+def call(body, name, out_shape, in_specs, out_specs, scratch=(), flops=0, moved=0, mib=VMEM_MIB):
     return pl.pallas_call(
         body,
         out_shape=out_shape,
         in_specs=in_specs,
         out_specs=out_specs,
         scratch_shapes=scratch,
-        compiler_params=pltpu.CompilerParams(vmem_limit_bytes=VMEM_MIB * MIB),
+        compiler_params=pltpu.CompilerParams(vmem_limit_bytes=mib * MIB),
         cost_estimate=pl.CostEstimate(flops=flops, bytes_accessed=moved, transcendentals=0),
         name=name,
     )
@@ -303,6 +305,7 @@
         ],
         flops=2 * tokens * (group_w + samples) * model_width,
         moved=2 * tokens * model_width + 2 * group_w * model_width,
+        mib=PROJECT_MIB,
     )(block_owner, sampled_rows[None, :], cotangent, activations)
 
 
@@ -447,18 +450,13 @@
     return currents
 
 
-def invert_body(scale, owner, rows_ref, _, all_ref, own_ref, rows, sem):
+def invert_body(scale, rows_ref, all_ref, own_ref, rows, sem):
     load = start_all([rows_ref.at[:, pl.ds(0, 3)]], [rows], sem)[0]
-    me = lax.axis_index("dp")
-    owned = jnp.int32(0)
-    for b in range(owner.shape[0]):
-        owned = owned + jnp.where(owner[b] == me, 1, 0)
-    used = jnp.where(lax.axis_index("tensor") < owned, 1.0, 0.0).astype(f32)
     load.wait()
     first, second, own = inverses_of([rows[:, m].reshape(-1, FACTOR_BLOCK) for m in range(3)], scale)
     fold(first, all_ref.at[0])
     fold(second, all_ref.at[1])
-    fold(own * used, all_ref.at[2])
+    fold(own, all_ref.at[2])
     own_ref[...] = all_ref[2]
 
 
@@ -469,25 +467,37 @@
     out_ref[...] = jnp.concatenate(parts, axis=0)
 
 
-def owned_body(own_ref, near_ref, here, beside, two_off, three_off, _, sum_ref, out_ref, split, own, near, held, need, sems, need_sems):
-    sums = start_all([own_ref, near_ref], [own, near], need_sems, 2)
-    needs = start_all([here.at[pl.ds(0, 2)], beside.at[pl.ds(0, 2)]], [need.at[pl.ds(0, 2)], need.at[pl.ds(2, 2)]], need_sems)
-    loads = start_all([here.at[2], beside.at[2], two_off, three_off], [held.at[k] for k in range(4)], sems)
-    z = lax.axis_index("tensor")
-    odd = z % 2
+def ready_body(own_ref, near_ref, here, beside, _, sum_ref, split, own, near, need, sems):
+    loads = start_all(
+        [here.at[pl.ds(0, 2)], beside.at[pl.ds(0, 2)], own_ref, near_ref],
+        [need.at[pl.ds(0, 2)], need.at[pl.ds(2, 2)], own, near],
+        sems,
+    )
+    odd = lax.axis_index("tensor") % 2
     for k in range(2):
-        needs[k].wait()
+        loads[k].wait()
         for p in range(2):
             high, low = two(unfold(need.at[2 * k + p]))
             at = 2 * (odd if k == 0 else 1 - odd) + p
             split[0, at] = high
             split[1, at] = low
-    for load in sums:
+    for load in loads[2:]:
         load.wait()
     sum_ref[...] = own[...] + decode(near)
+
+
+def owned_body(owner, here, beside, two_off, three_off, _, out_ref, done_ref, held, sems):
+    loads = start_all([here.at[2], beside.at[2], two_off, three_off], [held.at[k] for k in range(4)], sems)
+    z = lax.axis_index("tensor")
+    me = lax.axis_index("dp")
+    count = jnp.int32(0)
+    for b in range(owner.shape[0]):
+        count = count + jnp.where(owner[b] == me, 1, 0)
     for k, load in enumerate(loads):
         load.wait()
-        out_ref[z ^ k] = unfold(held.at[k])
+        slot = z ^ k
+        out_ref[slot] = jnp.where(slot < count, unfold(held.at[k]), 0.0)
+    done_ref[...] = jnp.zeros(done_ref.shape, f32)
 
 
 def own_body(cot_ref, act_ref, got_ref, _, sum_ref, cot, held, got, sems):
@@ -502,7 +512,7 @@
     sum_ref[...] = product + got[...]
 
 
-def finish_body(split_ref, g_ref, sum_ref, come, step_out, split, left, total, come_in, step, sems, out_sems):
+def finish_body(split_ref, g_ref, sum_ref, come, _, step_out, split, left, total, come_in, step, sems, out_sems):
     width = FACTOR_BLOCK
     loads = start_all([g_ref, sum_ref, come, split_ref], [left, total, come_in, split], sems)
 
@@ -552,22 +562,23 @@
             dma(steps),
         ],
         moved=4 * MIB * len(which),
+        mib=SUM_MIB,
     )(cotangent, activations, got, *after)
 
 
-def invert(block_owner, rows, after, scale):
+def invert(rows, scale):
     _, kinds, samples, _ = rows.shape
     packed = shaped((fold_rows(FACTOR_BLOCK // 2) + FOLD_ROWS, FACTOR_BLOCK), bf16)
     return call(
         functools.partial(invert_body, scale),
         "invert_blocks",
         (shaped((3, *packed.shape), bf16), packed),
-        [SMEM, ANY, ANY],
+        [ANY],
         (VMEM,) * 2,
         [pltpu.VMEM((rows.shape[0], 3, samples, FACTOR_BLOCK), bf16), dma(1)],
         flops=2 * 3 * 4 * 18 * FACTOR_BLOCK**3,
         moved=2 * MIB,
-    )(block_owner, rows, after)
+    )(rows)
 
 
 def invert_group(rows, after, and_after, scale):
@@ -613,31 +624,43 @@
             pltpu.VMEM((group_w, share), f32),
             dma(3),
         ],
+        mib=SUM_MIB,
     )(cotangent, activations, own_got, after)
 
 
-def owned_blocks(own_sum, near, inverses, beside, two_off, three_off, after):
+def ready(own_sum, near, inverses, beside, after):
     square = (4, FACTOR_BLOCK, FACTOR_BLOCK)
-    held = pltpu.VMEM((4, *two_off.shape), bf16)
+    held = pltpu.VMEM((4, *inverses.shape[1:]), bf16)
+    return call(
+        ready_body,
+        "ready",
+        (shaped(own_sum.shape), shaped((2, *square), bf16)),
+        [ANY] * 5,
+        (VMEM,) * 2,
+        [pltpu.VMEM(own_sum.shape, f32), pltpu.VMEM(near.shape, bf16), held, dma(4)],
+    )(own_sum, near, inverses, beside, after)
+
+
+def owned_blocks(block_owner, inverses, beside, two_off, three_off, after):
     return call(
         owned_body,
         "owned",
-        (shaped(own_sum.shape), shaped(square), shaped((2, *square), bf16)),
-        [ANY] * 7,
-        (VMEM,) * 3,
-        [pltpu.VMEM(own_sum.shape, f32), pltpu.VMEM(near.shape, bf16), held, held, dma(4), dma(4)],
+        (shaped((4, FACTOR_BLOCK, FACTOR_BLOCK)), shaped((8, 128))),
+        [SMEM] + [ANY] * 5,
+        (VMEM,) * 2,
+        [pltpu.VMEM((4, *two_off.shape), bf16), dma(4)],
         flops=OWNED_FLOPS,
-    )(own_sum, near, inverses, beside, two_off, three_off, after)
-
-
-def finish(split, g_parts, so_far, come):
+    )(block_owner, inverses, beside, two_off, three_off, after)
+
+
+def finish(split, g_parts, so_far, come, after):
     group_w, share = so_far.shape
     blocks = share // FACTOR_BLOCK
     return call(
         finish_body,
         "finish",
         shaped((share, group_w)),
-        [ANY] * 4,
+        [ANY] * 5,
         ANY,
         [
             pltpu.VMEM(split.shape, bf16),
@@ -649,7 +672,7 @@
             dma(blocks),
         ],
         moved=6 * MIB,
-    )(split, g_parts, so_far, come)
+    )(split, g_parts, so_far, come, after)
 
 
 def square_device(activations, cotangent, sampled_rows, block_owner):
@@ -672,11 +695,11 @@
 
     (far,) = sum_cores("sum_far", (0,), cotangent, activations, got)
     far_come = travel(far, NEAR_X, NEAR_Y)
-    near, rest = sum_cores("sum_near", (1, 2), cotangent, activations, got, far)
+    own_sum = sum_own(cotangent, activations, own_got, far)
+    near, rest = sum_cores("sum_near", (1, 2), cotangent, activations, got, own_sum)
     near_come = travel(near, NEAR_X, NEAR_Y)
-    own_sum = sum_own(cotangent, activations, own_got, rest)
-
-    inverses, own = invert(block_owner, rows, own_sum, 1.0 / (samples * dp_count))
+
+    inverses, own = invert(rows, 1.0 / (samples * dp_count))
     beside = swap(inverses, 1, "tensor")
     two_off, three_off = swap(own, 2, "tensor"), swap(own, 3, "tensor")
 
@@ -684,8 +707,9 @@
     come_last = travel(hopped, NEAR_Y, NEAR_X)
 
     g_parts = invert_group(rows, near_come, hopped, activations.shape[0] / samples)
-    so_far, owned, split = owned_blocks(own_sum, near_come, inverses, beside, two_off, three_off, g_parts)
-    step = finish(split, g_parts, so_far, come_last)
+    so_far, split = ready(own_sum, near_come, inverses, beside, g_parts)
+    owned, done = owned_blocks(block_owner, inverses, beside, two_off, three_off, so_far)
+    step = finish(split, g_parts, so_far, come_last, done)
     return step, owned
 
 

time: 64.1 us -> 60.4 us (0.942)
  Pallas kernels: 46.4 us -> 41.9 us
    pallas_call x2 -> x3, Pallas kernels: 8.51 us -> 6.89 us  [the longest x1 2.66 us: owned_blocks(): call(owned_body, 'owned', (shaped((4, FACTOR_BLOCK, FACTOR_BLOCK)), shape...]
    pallas_call x1, Pallas kernels: 8.5 us -> 7.08 us  [invert(): call(functools.partial(invert_body, scale), 'invert_blocks', (shaped((3,...]
    pallas_call x1, Pallas kernels: 5.47 us -> 4.54 us  [invert_group(): call(functools.partial(group_body, scale), 'invert_group', shaped((2 * FA...]
  transfers between devices with their start and end apart: 9 -> 9, of which waited for: 4 -> 4; matrix products, arithmetic and copies ran while one was open for 0% -> 0% of each run, Pallas kernels for 53% -> 51%
where the time goes in v5:
time: 60.4 us; the launch traced here: 60 us
  Pallas kernels  41.9 us (69%)
  starting transfers between devices  15.1 us (25%)
  waiting for transfers between devices  2.13 us (4%)
  between operations  0.94 us (2%)
    pallas_call x1, Pallas kernels, project(): call(project_body, 'project', (rest, one, shaped((count, 4, samples, FACT...  8.92 us
    pallas_call x2, Pallas kernels, sum_cores(): call(functools.partial(sum_body, which), name, tuple((shaped(wired, bf16)...  8.58 us
    pallas_call x1, Pallas kernels, invert(): call(functools.partial(invert_body, scale), 'invert_blocks', (shaped((3,...  7.08 us
    ppermute x5, starting transfers between devices, swap(): return lax.ppermute(block, axis, [(i, i ^ bit) for i in range(count)])  5.21 us
    all_to_all x1, starting transfers between devices, square_device(): rows = lax.all_to_all(picked, 'dp', split_axis=0, concat_axis=0, tiled=True)  5.15 us
    ppermute x3, starting transfers between devices, travel(): lax.ppermute(block, 'dp', [(i, i ^ (odd if i % 2 else even)) for i in ran...  4.72 us
    pallas_call x1, Pallas kernels, invert_group(): call(functools.partial(group_body, scale), 'invert_group', shaped((2 * FA...  4.54 us
    pallas_call x1, Pallas kernels, sum_own(): call(own_body, 'sum_own', shaped((group_w, share)), [ANY] * 4, VMEM, [plt...  3.4 us
  transfers between devices with their start and end apart: 9, of which 4 were waited for; matrix products, arithmetic and copies ran while one was open for 0% of the time, Pallas kernels for 51%

profile of v5, /device:TPU:0, one launch (start us, length us, event | category | flops | bytes accessed | tf_op | source)
XLA Modules:
  0.0 60.0 jit_solution(527142269573918161)
XLA Ops:
  0.6 8.9 %project.1 = (f32[3,256,1024]{2,1,0:T(8,128)}, f32[1,256,1024]{2,1,0:T(8,128)}, bf16[8,4,64,256]{3,2,1,0:T(8,128)(2,1)}) custom-call(s32[32]{0:T(128)} %owner.3, s32[1,64]{1,0:T(1,128)} %bitcast.1, bf16[768,256]{1,0:T(8,128)(2,1)} %cot_ref.7, bf16[768,8192]{1,0:T(8,128)(2,1)} %act_ref.7), custom_call_target="tpu_custom_call" | custom-call | flops 4026531840 | bytes 16777216 | tf_op jit(solution)/shard_map/project/pallas_call | solution.py:287
  9.6 0.5 collective-permute-start.1
  10.1 0.1 collective-permute-start
  10.2 5.2 %all-to-all-start = ((bf16[8,4,64,256]{3,2,1,0:T(8,128)(2,1)}), bf16[8,4,64,256]{3,2,1,0:T(8,128)(2,1)}, u32[]{:S(2)}, u32[]{:S(2)}) async-start(bf16[8,4,64,256]{3,2,1,0:T(8,128)(2,1)} %get-tuple-element.16), calls=%async_computation | async-start | bytes 2097152 | tf_op jit(solution)/shard_map/all_to_all | solution.py:693
  15.3 0.4 collective-permute-done.1.got_ref
  15.7 3.7 %sum_far.1._ = bf16[384,1024]{1,0:T(8,128)(2,1)} custom-call(bf16[768,256]{1,0:T(8,128)(2,1)} %cot_ref.7, bf16[768,8192]{1,0:T(8,128)(2,1)} %act_ref.7, f32[3,256,1024]{2,1,0:T(8,128)} %collective-permute-done.1.got_ref), custom_call_target="tpu_custom_call" | custom-call | bytes 4194304 | tf_op jit(solution)/shard_map/sum_far/pallas_call | solution.py:547
  19.4 2.9 %collective-permute-start.4 = (bf16[384,1024]{1,0:T(8,128)(2,1)}, bf16[384,1024]{1,0:T(8,128)(2,1)}, u32[]{:S(2)}, u32[]{:S(2)}) collective-permute-start(bf16[384,1024]{1,0:T(8,128)(2,1)} %sum_far.1._), channel_id=1, source_target_pairs={{0,8},{4,20},{8,0},{12,28},{16,24},{20,4},{24,16},{28,12},{1,9},{5... | collective-permute-start | bytes 2359304 | tf_op jit(solution)/shard_map/ppermute | solution.py:687
  22.3 0.0 collective-permute-done.got_ref
  22.3 3.4 %sum_own.1.refs_0_.own_ref = f32[256,1024]{1,0:T(8,128)} custom-call(bf16[768,256]{1,0:T(8,128)(2,1)} %cot_ref.7, bf16[768,8192]{1,0:T(8,128)(2,1)} %act_ref.7, f32[1,256,1024]{2,1,0:T(8,128)} %collective-permute-done.got_ref, bf16[384,1024]{1,0:T(8,128)(2,1)} %sum_far.1._), custom_call_target="tpu_custom_call" | custom-call | tf_op jit(solution)/shard_map/sum_own/pallas_call | solution.py:615
  25.7 4.9 %sum_near.1 = (bf16[384,1024]{1,0:T(8,128)(2,1)}, f32[256,1024]{1,0:T(8,128)}) custom-call(bf16[768,256]{1,0:T(8,128)(2,1)} %cot_ref.7, bf16[768,8192]{1,0:T(8,128)(2,1)} %act_ref.7, f32[3,256,1024]{2,1,0:T(8,128)} %collective-permute-done.1.got_ref, f32[256,1024]{1,0:T(8,128)} %sum_own.1.refs_0_.own_ref), custom_call_target="tpu_custom_call" | custom-call | bytes 8388608 | tf_op jit(solution)/shard_map/sum_near/pallas_call | solution.py:547
  30.6 0.0 copy-start.1
  30.6 0.1 collective-permute-start.2
  30.7 0.2 all-to-all-done.rows_ref
  31.0 7.1 %invert_blocks.1 = (bf16[3,208,256]{2,1,0:T(8,128)(2,1)S(1)}, bf16[208,256]{1,0:T(8,128)(2,1)S(1)}) custom-call(bf16[8,4,64,256]{3,2,1,0:T(8,128)(2,1)} %all-to-all-done.rows_ref), custom_call_target="tpu_custom_call" | custom-call | flops 7247757312 | bytes 2097152 | tf_op jit(solution)/shard_map/invert_blocks/pallas_call | solution.py:572
  38.1 0.0 copy-start
  38.1 2.0 %collective-permute-start.3 = (bf16[3,208,256]{2,1,0:T(8,128)(2,1)S(1)}, bf16[3,208,256]{2,1,0:T(8,128)(2,1)S(1)}, u32[]{:S(2)}, u32[]{:S(2)}) collective-permute-start(bf16[3,208,256]{2,1,0:T(8,128)(2,1)S(1)} %get-tuple-element.17._.here), channel_id=1, source_target_pairs={{0,1},{1,0},{2,3},{3,2},{4,5},{5,4},{6,7},{7,6},{8,9},{9,8},{10,11... | collective-permute-start | bytes 958472 | tf_op jit(solution)/shard_map/ppermute | solution.py:684
  40.1 2.6 %collective-permute-start.6 = (bf16[208,256]{1,0:T(8,128)(2,1)S(1)}, bf16[208,256]{1,0:T(8,128)(2,1)S(1)}, u32[]{:S(2)}, u32[]{:S(2)}) collective-permute-start(bf16[208,256]{1,0:T(8,128)(2,1)S(1)} %get-tuple-element.21), channel_id=1, source_target_pairs={{0,2},{1,3},{2,0},{3,1},{4,6},{5,7},{6,4},{7,5},{8,10},{9,11},{10,... | collective-permute-start | bytes 319496 | tf_op jit(solution)/shard_map/ppermute | solution.py:684
  42.7 0.0 collective-permute-start.7
  42.7 0.0 collective-permute-done.4.come
  42.7 0.0 copy-done.1
  42.7 2.5 %hop.1.__ = bf16[384,1024]{1,0:T(8,128)(2,1)S(1)} custom-call(f32[256,1024]{1,0:T(8,128)S(1)} %copy-done.1, bf16[384,1024]{1,0:T(8,128)(2,1)} %collective-permute-done.4.come, bf16[3,208,256]{2,1,0:T(8,128)(2,1)S(1)} %get-tuple-element.17._.here), custom_call_target="tpu_custom_call" | custom-call | tf_op jit(solution)/shard_map/hop/pallas_call | solution.py:600
  45.2 0.0 copy-start.2
  45.2 1.7 %collective-permute-start.5 = (bf16[384,1024]{1,0:T(8,128)(2,1)S(1)}, bf16[384,1024]{1,0:T(8,128)(2,1)S(1)}, u32[]{:S(2)}, u32[]{:S(2)}) collective-permute-start(bf16[384,1024]{1,0:T(8,128)(2,1)S(1)} %hop.1.__), channel_id=1, source_target_pairs={{0,16},{4,12},{8,24},{12,4},{16,0},{20,28},{24,8},{28,20},{1,17},{... | collective-permute-start | bytes 2359304 | tf_op jit(solution)/shard_map/ppermute | solution.py:687
  46.9 0.0 collective-permute-done.2._.near_ref
  46.9 4.5 %invert_group.1._.g_ref = bf16[512,256]{1,0:T(8,128)(2,1)S(1)} custom-call(bf16[8,4,64,256]{3,2,1,0:T(8,128)(2,1)} %all-to-all-done.rows_ref, bf16[384,1024]{1,0:T(8,128)(2,1)S(1)} %collective-permute-done.2._.near_ref, bf16[384,1024]{1,0:T(8,128)(2,1)S(1)} %hop.1.__), custom_call_target="tpu_custom_call" | custom-call | tf_op jit(solution)/shard_map/invert_group/pallas_call | solution.py:586
  51.4 0.0 collective-permute-done.3.beside
  51.4 0.0 copy-done
  51.4 1.6 %ready.1 = (f32[256,1024]{1,0:T(8,128)S(1)}, bf16[2,4,256,256]{3,2,1,0:T(8,128)(2,1)S(1)}) custom-call(f32[256,1024]{1,0:T(8,128)S(1)} %copy-done, bf16[384,1024]{1,0:T(8,128)(2,1)S(1)} %collective-permute-done.2._.near_ref, bf16[3,208,256]{2,1,0:T(8,128)(2,1)S(1)} %get-tuple-element.17._.here, bf16[3,208,256]{2,1,0:T(8,128)(2,1)S(1)} %collective-permute-done.3.beside, ...), custom_call_target="tpu_custom_call" | custom-call | tf_op jit(solution)/shard_map/ready/pallas_call | solution.py:634
  53.0 0.0 collective-permute-done.6.two_off
  53.1 1.0 %collective-permute-done.7.three_off = bf16[208,256]{1,0:T(8,128)(2,1)S(1)} collective-permute-done((bf16[208,256]{1,0:T(8,128)(2,1)S(1)}, bf16[208,256]{1,0:T(8,128)(2,1)S(1)}, u32[]{:S(2)}, u32[]{:S(2)}) %collective-permute-start.7) | collective-permute-done | bytes 106528 | tf_op jit(solution)/shard_map/ppermute | solution.py:684
  54.1 0.0 copy-done.2
  54.1 2.7 %owned.1 = (f32[4,256,256]{2,1,0:T(8,128)}, f32[8,128]{1,0:T(8,128)S(1)}) custom-call(s32[32]{0:T(128)S(1)} %copy-done.2, bf16[3,208,256]{2,1,0:T(8,128)(2,1)S(1)} %get-tuple-element.17._.here, bf16[3,208,256]{2,1,0:T(8,128)(2,1)S(1)} %collective-permute-done.3.beside, bf16[208,256]{1,0:T(8,128)(2,1)S(1)} %collective-permute-done.6.two_off, ...), custom_call_target="tpu_custom_call" | custom-call | flops 20000000000 | tf_op jit(solution)/shard_map/owned/pallas_call | solution.py:645
  56.7 0.5 collective-permute-done.5.come
  57.2 2.6 %finish.1 = f32[1024,256]{1,0:T(8,128)} custom-call(bf16[2,4,256,256]{3,2,1,0:T(8,128)(2,1)S(1)} %get-tuple-element.19.split_ref, bf16[512,256]{1,0:T(8,128)(2,1)S(1)} %invert_group.1._.g_ref, f32[256,1024]{1,0:T(8,128)S(1)} %get-tuple-element.20._.sum_ref, bf16[384,1024]{1,0:T(8,128)(2,1)S(1)} %collective-permute-done.5.come, f32[8,128]{1,0:T(8,128)S(1)} %get-tuple-element.22._), custom_call_target="tpu_custom_call" | custom-call | bytes 6291456 | tf_op jit(solution)/shard_map/finish/pallas_call | solution.py:659
Async XLA Ops:
  9.6 6.1 %collective-permute-start.1 = (f32[3,256,1024]{2,1,0:T(8,128)}, f32[3,256,1024]{2,1,0:T(8,128)}, u32[]{:S(2)}, u32[]{:S(2)}) collective-permute-start(f32[3,256,1024]{2,1,0:T(8,128)} %get-tuple-element.14), channel_id=1, source_target_pairs={{0,4},{4,0},{8,12},{12,8},{16,20},{20,16},{24,28},{28,24},{1,5},{5... | collective-permute-start | bytes 9437192 | tf_op jit(solution)/shard_map/ppermute | solution.py:684
  10.1 12.2 %collective-permute-start = (f32[1,256,1024]{2,1,0:T(8,128)}, f32[1,256,1024]{2,1,0:T(8,128)}, u32[]{:S(2)}, u32[]{:S(2)}) collective-permute-start(f32[1,256,1024]{2,1,0:T(8,128)} %get-tuple-element.13), channel_id=1, source_target_pairs={{0,4},{4,0},{8,12},{12,8},{16,20},{20,16},{24,28},{28,24},{1,5},{5... | collective-permute-start | bytes 3145736 | tf_op jit(solution)/shard_map/ppermute | solution.py:684
  10.2 20.8 %all-to-all-start = ((bf16[8,4,64,256]{3,2,1,0:T(8,128)(2,1)}), bf16[8,4,64,256]{3,2,1,0:T(8,128)(2,1)}, u32[]{:S(2)}, u32[]{:S(2)}) async-start(bf16[8,4,64,256]{3,2,1,0:T(8,128)(2,1)} %get-tuple-element.16), calls=%async_computation | async-start | bytes 2097152 | tf_op jit(solution)/shard_map/all_to_all | solution.py:693
  19.4 23.3 %collective-permute-start.4 = (bf16[384,1024]{1,0:T(8,128)(2,1)}, bf16[384,1024]{1,0:T(8,128)(2,1)}, u32[]{:S(2)}, u32[]{:S(2)}) collective-permute-start(bf16[384,1024]{1,0:T(8,128)(2,1)} %sum_far.1._), channel_id=1, source_target_pairs={{0,8},{4,20},{8,0},{12,28},{16,24},{20,4},{24,16},{28,12},{1,9},{5... | collective-permute-start | bytes 2359304 | tf_op jit(solution)/shard_map/ppermute | solution.py:687
  30.6 12.0 %copy-start.1 = (f32[256,1024]{1,0:T(8,128)S(1)}, f32[256,1024]{1,0:T(8,128)}, u32[]{:S(2)}) copy-start(f32[256,1024]{1,0:T(8,128)} %get-tuple-element.18.rest) | copy-start | bytes 3145732
  30.6 16.2 %collective-permute-start.2 = (bf16[384,1024]{1,0:T(8,128)(2,1)}, bf16[384,1024]{1,0:T(8,128)(2,1)S(1)}, u32[]{:S(2)}, u32[]{:S(2)}) collective-permute-start(bf16[384,1024]{1,0:T(8,128)(2,1)} %get-tuple-element.15), channel_id=1, source_target_pairs={{0,8},{4,20},{8,0},{12,28},{16,24},{20,4},{24,16},{28,12},{1,9},{5... | collective-permute-start | bytes 2359304 | tf_op jit(solution)/shard_map/ppermute | solution.py:687
  38.1 13.4 %copy-start = (f32[256,1024]{1,0:T(8,128)S(1)}, f32[256,1024]{1,0:T(8,128)}, u32[]{:S(2)}) copy-start(f32[256,1024]{1,0:T(8,128)} %sum_own.1.refs_0_.own_ref) | copy-start | bytes 3145732
  38.1 13.3 %collective-permute-start.3 = (bf16[3,208,256]{2,1,0:T(8,128)(2,1)S(1)}, bf16[3,208,256]{2,1,0:T(8,128)(2,1)S(1)}, u32[]{:S(2)}, u32[]{:S(2)}) collective-permute-start(bf16[3,208,256]{2,1,0:T(8,128)(2,1)S(1)} %get-tuple-element.17._.here), channel_id=1, source_target_pairs={{0,1},{1,0},{2,3},{3,2},{4,5},{5,4},{6,7},{7,6},{8,9},{9,8},{10,11... | collective-permute-start | bytes 958472 | tf_op jit(solution)/shard_map/ppermute | solution.py:684
  40.1 13.0 %collective-permute-start.6 = (bf16[208,256]{1,0:T(8,128)(2,1)S(1)}, bf16[208,256]{1,0:T(8,128)(2,1)S(1)}, u32[]{:S(2)}, u32[]{:S(2)}) collective-permute-start(bf16[208,256]{1,0:T(8,128)(2,1)S(1)} %get-tuple-element.21), channel_id=1, source_target_pairs={{0,2},{1,3},{2,0},{3,1},{4,6},{5,7},{6,4},{7,5},{8,10},{9,11},{10,... | collective-permute-start | bytes 319496 | tf_op jit(solution)/shard_map/ppermute | solution.py:684
  42.7 11.4 %collective-permute-start.7 = (bf16[208,256]{1,0:T(8,128)(2,1)S(1)}, bf16[208,256]{1,0:T(8,128)(2,1)S(1)}, u32[]{:S(2)}, u32[]{:S(2)}) collective-permute-start(bf16[208,256]{1,0:T(8,128)(2,1)S(1)} %get-tuple-element.21), channel_id=1, source_target_pairs={{0,3},{1,2},{2,1},{3,0},{4,7},{5,6},{6,5},{7,4},{8,11},{9,10},{10,... | collective-permute-start | bytes 319496 | tf_op jit(solution)/shard_map/ppermute | solution.py:684
  45.2 8.9 %copy-start.2 = (s32[32]{0:T(128)S(1)}, s32[32]{0:T(128)}, u32[]{:S(2)}) copy-start(s32[32]{0:T(128)} %owner.3) | copy-start | bytes 388
  45.2 12.1 %collective-permute-start.5 = (bf16[384,1024]{1,0:T(8,128)(2,1)S(1)}, bf16[384,1024]{1,0:T(8,128)(2,1)S(1)}, u32[]{:S(2)}, u32[]{:S(2)}) collective-permute-start(bf16[384,1024]{1,0:T(8,128)(2,1)S(1)} %hop.1.__), channel_id=1, source_target_pairs={{0,16},{4,12},{8,24},{12,4},{16,0},{20,28},{24,8},{28,20},{1,17},{... | collective-permute-start | bytes 2359304 | tf_op jit(solution)/shard_map/ppermute | solution.py:687

commit v6 on v5

--- a/solution.py
+++ b/solution.py
@@ -245,14 +245,18 @@
     left[group_w:] = (places == rows[...]).astype(f32).T.astype(bf16)
 
     blocks = count * per_tile
-    picks[blocks] = jnp.dot(left[group_w:], cot[...], preferred_element_type=f32).astype(bf16)
     stores = []
 
-    def pass_on(block, many, dest, place, n):
-        return start_all([picks.at[pl.ds(block, many)]], [out_ref.at[dest, pl.ds(place, many)]], pick_sems, n)
-
+    def keep(block, values):
+        for k in range(2):
+            picks[2 * block + k] = values[k * samples // 2 : (k + 1) * samples // 2].astype(bf16)
+
+    def pass_on(half_block, many, dest, place, n):
+        return start_all([picks.at[pl.ds(half_block, many)]], [out_ref.at[dest, pl.ds(place, many)]], pick_sems, n)
+
+    keep(blocks, jnp.dot(left[group_w:], cot[...], preferred_element_type=f32))
     for d in range(count):
-        stores += pass_on(blocks, 1, d, 3, 3 * d + 2)
+        stores += pass_on(2 * blocks + d % 2, 1, d, 6, 3 * d + 2)
     for i in range(count):
         if i % 2 == 0:
             loads[i].wait()
@@ -267,12 +271,10 @@
         else:
             picked = jnp.dot(left[group_w:], held[i], preferred_element_type=f32)
         for j in range(per_tile):
-            picks[tiles[i] * per_tile + j] = picked[
-                :, j * FACTOR_BLOCK : (j + 1) * FACTOR_BLOCK
-            ].astype(bf16)
-        stores += pass_on(tiles[i] * per_tile + 2 * (z % 2), 2, tiles[i], 0, 3 * i)
+            keep(tiles[i] * per_tile + j, picked[:, j * FACTOR_BLOCK : (j + 1) * FACTOR_BLOCK])
+        stores += pass_on(2 * (tiles[i] * per_tile + 2 * (z % 2)), 4, tiles[i], 0, 3 * i)
     for d in range(count):
-        stores += pass_on(slots[1, d], 1, d, 2, 3 * d + 1)
+        stores += pass_on(2 * slots[1, d], 2, d, 4, 3 * d + 1)
     for store in stores:
         store.wait()
 
@@ -287,7 +289,7 @@
     return call(
         project_body,
         "project",
-        (rest, one, shaped((count, 4, samples, FACTOR_BLOCK), bf16)),
+        (rest, one, shaped((count, 7, samples // 2, FACTOR_BLOCK), bf16)),
         [SMEM, ANY, ANY, ANY],
         (ANY,) * 3,
         [
@@ -296,7 +298,7 @@
             pltpu.VMEM((1, samples), jnp.int32),
             pltpu.VMEM((group_w + samples, tokens), bf16),
             pltpu.VMEM((count // 2, group_w, share), f32),
-            pltpu.VMEM((model_width // FACTOR_BLOCK + 1, samples, FACTOR_BLOCK), bf16),
+            pltpu.VMEM((2 * (model_width // FACTOR_BLOCK + 1), samples // 2, FACTOR_BLOCK), bf16),
             pltpu.SMEM((2, count), jnp.int32),
             pltpu.SemaphoreType.DMA((count,)),
             pltpu.SemaphoreType.DMA((count // 2,)),
@@ -309,7 +311,7 @@
     )(block_owner, sampled_rows[None, :], cotangent, activations)
 
 
-def sum_body(which, cot_ref, act_ref, got_ref, *refs):
+def sum_body(which, cot_ref, act_ref, got_ref, own_got_ref, *refs):
     count = len(which)
     outs, (cot, held, got, left, wire, plain, sems, got_sems, out_sems) = refs[-9 - count : -9], refs[-9:]
     width = held.shape[2]
@@ -323,7 +325,8 @@
     def fetch(n):
         i, p = work[n]
         tile = act_ref.at[:, pl.ds(starts[i] + p * width, width)]
-        come = got_ref.at[which[i], :, pl.ds(p * width, width)]
+        source, at = (own_got_ref, 0) if which[i] == 3 else (got_ref, which[i])
+        come = source.at[at, :, pl.ds(p * width, width)]
         return start_all([tile], [held.at[n]], sems, 1 + n) + start_all([come], [got.at[n]], got_sems, n)
 
     loads = [fetch(n) for n in range(min(AHEAD, len(work)))]
@@ -340,8 +343,8 @@
             encode(product + got[n], wire.at[n])
             source = wire.at[n]
         else:
-            plain[p] = product + got[n]
-            source = plain.at[p]
+            plain[n] = product + got[n]
+            source = plain.at[n]
         stores += start_all([source], [outs[i].at[:, pl.ds(p * width, width)]], out_sems, n)
     for store in stores:
         store.wait()
@@ -450,19 +453,23 @@
     return currents
 
 
-def invert_body(scale, rows_ref, all_ref, own_ref, rows, sem):
-    load = start_all([rows_ref.at[:, pl.ds(0, 3)]], [rows], sem)[0]
+def invert_body(scale, rows_ref, all_ref, own_ref, cot_ref, rows, sems):
+    load, copy = start_all([rows_ref.at[:, pl.ds(0, 6)], rows_ref.at[:, 6]], [rows, cot_ref], sems)
     load.wait()
-    first, second, own = inverses_of([rows[:, m].reshape(-1, FACTOR_BLOCK) for m in range(3)], scale)
+    first, second, own = inverses_of(
+        [rows[:, 2 * m : 2 * m + 2].reshape(-1, FACTOR_BLOCK) for m in range(3)], scale
+    )
     fold(first, all_ref.at[0])
     fold(second, all_ref.at[1])
     fold(own, all_ref.at[2])
     own_ref[...] = all_ref[2]
-
-
-def group_body(scale, rows_ref, _, __, out_ref, rows, sem):
-    load = start_all([rows_ref.at[:, 3]], [rows], sem)[0]
-    load.wait()
+    copy.wait()
+
+
+def group_body(scale, half_ref, other_ref, _, __, out_ref, rows, sems):
+    loads = start_all([half_ref, other_ref], [rows.at[0], rows.at[1]], sems)
+    for load in loads:
+        load.wait()
     parts = two(inverses_of([rows[...].reshape(-1, FACTOR_BLOCK)], scale)[0].T)
     out_ref[...] = jnp.concatenate(parts, axis=0)
 
@@ -498,18 +505,6 @@
         slot = z ^ k
         out_ref[slot] = jnp.where(slot < count, unfold(held.at[k]), 0.0)
     done_ref[...] = jnp.zeros(done_ref.shape, f32)
-
-
-def own_body(cot_ref, act_ref, got_ref, _, sum_ref, cot, held, got, sems):
-    share = held.shape[1]
-    start = pl.multiple_of(lax.axis_index("dp") * share, share)
-    loads = start_all([cot_ref, act_ref.at[:, pl.ds(start, share)], got_ref.at[0]], [cot, held, got], sems)
-    loads[0].wait()
-    left = cot[...].astype(f32).T.astype(bf16)
-    loads[1].wait()
-    product = jnp.dot(left, held[...], preferred_element_type=f32)
-    loads[2].wait()
-    sum_ref[...] = product + got[...]
 
 
 def finish_body(split_ref, g_ref, sum_ref, come, _, step_out, split, left, total, come_in, step, sems, out_sems):
@@ -539,7 +534,7 @@
     return pltpu.SemaphoreType.DMA((count,))
 
 
-def sum_cores(name, which, cotangent, activations, got, *after):
+def sum_cores(name, which, cotangent, activations, got, own_got, *after):
     tokens, group_w = cotangent.shape
     share = got.shape[2]
     wired = (fold_rows(group_w), share)
@@ -548,7 +543,7 @@
         functools.partial(sum_body, which),
         name,
         tuple(shaped(wired, bf16) if i < 2 else shaped((group_w, share)) for i in which),
-        [ANY] * (3 + len(after)),
+        [ANY] * (4 + len(after)),
         (ANY,) * len(which),
         [
             pltpu.VMEM(cotangent.shape, bf16),
@@ -556,41 +551,40 @@
             pltpu.VMEM((steps, group_w, width), f32),
             pltpu.VMEM((group_w, tokens), bf16),
             pltpu.VMEM((steps, wired[0], width), bf16),
-            pltpu.VMEM((SUM_PARTS, group_w, width), f32),
+            pltpu.VMEM((steps, group_w, width), f32),
             dma(1 + steps),
             dma(steps),
             dma(steps),
         ],
         moved=4 * MIB * len(which),
         mib=SUM_MIB,
-    )(cotangent, activations, got, *after)
+    )(cotangent, activations, got, own_got, *after)
 
 
 def invert(rows, scale):
-    _, kinds, samples, _ = rows.shape
+    count, _, samples, _ = rows.shape
     packed = shaped((fold_rows(FACTOR_BLOCK // 2) + FOLD_ROWS, FACTOR_BLOCK), bf16)
     return call(
         functools.partial(invert_body, scale),
         "invert_blocks",
-        (shaped((3, *packed.shape), bf16), packed),
+        (shaped((3, *packed.shape), bf16), packed, shaped((count, samples, FACTOR_BLOCK), bf16)),
         [ANY],
-        (VMEM,) * 2,
-        [pltpu.VMEM((rows.shape[0], 3, samples, FACTOR_BLOCK), bf16), dma(1)],
+        (VMEM, VMEM, ANY),
+        [pltpu.VMEM((count, 6, samples, FACTOR_BLOCK), bf16), dma(2)],
         flops=2 * 3 * 4 * 18 * FACTOR_BLOCK**3,
         moved=2 * MIB,
     )(rows)
 
 
-def invert_group(rows, after, and_after, scale):
-    samples = rows.shape[2]
+def invert_group(half, other, after, and_after, scale):
     return call(
         functools.partial(group_body, scale),
         "invert_group",
         shaped((2 * FACTOR_BLOCK, FACTOR_BLOCK), bf16),
-        [ANY] * 3,
+        [ANY] * 4,
         VMEM,
-        [pltpu.VMEM((rows.shape[0], samples, FACTOR_BLOCK), bf16), dma(1)],
-    )(rows, after, and_after)
+        [pltpu.VMEM((2, *half.shape), bf16), dma(2)],
+    )(half, other, after, and_after)
 
 
 def hop(rest, come, after):
@@ -607,25 +601,6 @@
         + [pltpu.VMEM((HOP_PARTS, wired[0], width), bf16)] * 2
         + [dma(2 * HOP_PARTS), dma(HOP_PARTS)],
     )(rest, come, after)
-
-
-def sum_own(cotangent, activations, own_got, after):
-    tokens = cotangent.shape[0]
-    _, group_w, share = own_got.shape
-    return call(
-        own_body,
-        "sum_own",
-        shaped((group_w, share)),
-        [ANY] * 4,
-        VMEM,
-        [
-            pltpu.VMEM(cotangent.shape, bf16),
-            pltpu.VMEM((tokens, share), bf16),
-            pltpu.VMEM((group_w, share), f32),
-            dma(3),
-        ],
-        mib=SUM_MIB,
-    )(cotangent, activations, own_got, after)
 
 
 def ready(own_sum, near, inverses, beside, after):
@@ -693,20 +668,20 @@
     rows = lax.all_to_all(picked, "dp", split_axis=0, concat_axis=0, tiled=True)
     own_got = swap(own_theirs, CORE)
 
-    (far,) = sum_cores("sum_far", (0,), cotangent, activations, got)
+    (far,) = sum_cores("sum_far", (0,), cotangent, activations, got, got)
     far_come = travel(far, NEAR_X, NEAR_Y)
-    own_sum = sum_own(cotangent, activations, own_got, far)
-    near, rest = sum_cores("sum_near", (1, 2), cotangent, activations, got, own_sum)
+    near, rest, own_sum = sum_cores("sum_near", (1, 2, 3), cotangent, activations, got, own_got, far)
     near_come = travel(near, NEAR_X, NEAR_Y)
 
-    inverses, own = invert(rows, 1.0 / (samples * dp_count))
+    inverses, own, half = invert(rows, 1.0 / (samples * dp_count))
     beside = swap(inverses, 1, "tensor")
     two_off, three_off = swap(own, 2, "tensor"), swap(own, 3, "tensor")
 
     hopped = hop(rest, far_come, inverses)
     come_last = travel(hopped, NEAR_Y, NEAR_X)
 
-    g_parts = invert_group(rows, near_come, hopped, activations.shape[0] / samples)
+    other = swap(half, CORE)
+    g_parts = invert_group(half, other, near_come, hopped, activations.shape[0] / samples)
     so_far, split = ready(own_sum, near_come, inverses, beside, g_parts)
     owned, done = owned_blocks(block_owner, inverses, beside, two_off, three_off, so_far)
     step = finish(split, g_parts, so_far, come_last, done)

time: 60.4 us -> 58.8 us (0.974)
  Pallas kernels: 41.9 us -> 39 us
  waiting for transfers between devices: 2.13 us -> 3.81 us
    pallas_call x2 -> x1, Pallas kernels: 12.3 us -> 8.91 us  [project(): call(project_body, 'project', (rest, one, shaped((count, 7, samples // 2,...]
    pallas_call x2, Pallas kernels: 8.58 us -> 9.77 us  [sum_cores(): call(functools.partial(sum_body, which), name, tuple((shaped(wired, bf16)...]
    ppermute x3, waiting for transfers between devices: 0.51 us -> 1.57 us  [travel(): lax.ppermute(block, 'dp', [(i, i ^ (odd if i % 2 else even)) for i in ran...]
    all_to_all x1, waiting for transfers between devices: 0.23 us -> 1.03 us  [square_device(): rows = lax.all_to_all(picked, 'dp', split_axis=0, concat_axis=0, tiled=True)]
    ppermute x5 -> x6, waiting for transfers between devices: 1.4 us -> 1.21 us  [swap(): return lax.ppermute(block, axis, [(i, i ^ bit) for i in range(count)])]
    ppermute x5 -> x6, starting transfers between devices: 5.21 us -> 5.22 us  [swap(): return lax.ppermute(block, axis, [(i, i ^ bit) for i in range(count)])]
  transfers between devices with their start and end apart: 9 -> 10, of which waited for: 4 -> 5; matrix products, arithmetic and copies ran while one was open for 0% -> 0% of each run, Pallas kernels for 51% -> 47%
where the time goes in v6:
time: 58.8 us; the launch traced here: 58.4 us
  Pallas kernels  39 us (66%)
  starting transfers between devices  14.6 us (25%)
  waiting for transfers between devices  3.81 us (6%)
  between operations  0.94 us (2%)
    pallas_call x2, Pallas kernels, sum_cores(): call(functools.partial(sum_body, which), name, tuple((shaped(wired, bf16)...  9.77 us
    pallas_call x1, Pallas kernels, project(): call(project_body, 'project', (rest, one, shaped((count, 7, samples // 2,...  8.91 us
    pallas_call x1, Pallas kernels, invert(): call(functools.partial(invert_body, scale), 'invert_blocks', (shaped((3,...  7.09 us
    ppermute x6, starting transfers between devices, swap(): return lax.ppermute(block, axis, [(i, i ^ bit) for i in range(count)])  5.22 us
    all_to_all x1, starting transfers between devices, square_device(): rows = lax.all_to_all(picked, 'dp', split_axis=0, concat_axis=0, tiled=True)  5.15 us
    ppermute x3, starting transfers between devices, travel(): lax.ppermute(block, 'dp', [(i, i ^ (odd if i % 2 else even)) for i in ran...  4.26 us
    pallas_call x1, Pallas kernels, invert_group(): call(functools.partial(group_body, scale), 'invert_group', shaped((2 * FA...  4.13 us
    pallas_call x1, Pallas kernels, owned_blocks(): call(owned_body, 'owned', (shaped((4, FACTOR_BLOCK, FACTOR_BLOCK)), shape...  2.66 us
  transfers between devices with their start and end apart: 10, of which 5 were waited for; matrix products, arithmetic and copies ran while one was open for 0% of the time, Pallas kernels for 47%

profile of v6, /device:TPU:0, one launch (start us, length us, event | category | flops | bytes accessed | tf_op | source)
XLA Modules:
  0.0 58.4 jit_solution(10478252487587442504)
XLA Ops:
  0.6 8.9 %project.1 = (f32[3,256,1024]{2,1,0:T(8,128)}, f32[1,256,1024]{2,1,0:T(8,128)}, bf16[8,7,32,256]{3,2,1,0:T(8,128)(2,1)}) custom-call(s32[32]{0:T(128)} %owner.3, s32[1,64]{1,0:T(1,128)} %bitcast.1, bf16[768,256]{1,0:T(8,128)(2,1)} %cot_ref.5, bf16[768,8192]{1,0:T(8,128)(2,1)} %act_ref.5), custom_call_target="tpu_custom_call" | custom-call | flops 4026531840 | bytes 16777216 | tf_op jit(solution)/shard_map/project/pallas_call | solution.py:289
  9.5 0.5 collective-permute-start
  10.1 0.1 collective-permute-start.1
  10.1 5.1 %all-to-all-start = ((bf16[8,7,32,256]{3,2,1,0:T(8,128)(2,1)}), bf16[8,7,32,256]{3,2,1,0:T(8,128)(2,1)}, u32[]{:S(2)}, u32[]{:S(2)}) async-start(bf16[8,7,32,256]{3,2,1,0:T(8,128)(2,1)} %get-tuple-element.19), calls=%async_computation | async-start | bytes 1835008 | tf_op jit(solution)/shard_map/all_to_all | solution.py:668
  15.3 0.4 collective-permute-done.got_ref.own_got_ref
  15.7 3.6 %sum_far.1.refs_0_ = bf16[384,1024]{1,0:T(8,128)(2,1)} custom-call(bf16[768,256]{1,0:T(8,128)(2,1)} %cot_ref.5, bf16[768,8192]{1,0:T(8,128)(2,1)} %act_ref.5, f32[3,256,1024]{2,1,0:T(8,128)} %collective-permute-done.got_ref.own_got_ref, f32[3,256,1024]{2,1,0:T(8,128)} %collective-permute-done.got_ref.own_got_ref), custom_call_target="tpu_custom_call" | custom-call | bytes 4194304 | tf_op jit(solution)/shard_map/sum_far/pallas_call | solution.py:542
  19.3 2.9 %collective-permute-start.5 = (bf16[384,1024]{1,0:T(8,128)(2,1)}, bf16[384,1024]{1,0:T(8,128)(2,1)}, u32[]{:S(2)}, u32[]{:S(2)}) collective-permute-start(bf16[384,1024]{1,0:T(8,128)(2,1)} %sum_far.1.refs_0_), channel_id=1, source_target_pairs={{0,8},{4,20},{8,0},{12,28},{16,24},{20,4},{24,16},{28,12},{1,9},{5... | collective-permute-start | bytes 2359304 | tf_op jit(solution)/shard_map/ppermute | solution.py:662
  22.3 0.0 collective-permute-done.1.own_got_ref
  22.3 6.2 %sum_near.1 = (bf16[384,1024]{1,0:T(8,128)(2,1)}, f32[256,1024]{1,0:T(8,128)}, f32[256,1024]{1,0:T(8,128)}) custom-call(bf16[768,256]{1,0:T(8,128)(2,1)} %cot_ref.5, bf16[768,8192]{1,0:T(8,128)(2,1)} %act_ref.5, f32[3,256,1024]{2,1,0:T(8,128)} %collective-permute-done.got_ref.own_got_ref, f32[1,256,1024]{2,1,0:T(8,128)} %collective-permute-done.1.own_got_ref, ...), custom_call_target="tpu_custom_call" | custom-call | bytes 12582912 | tf_op jit(solution)/shard_map/sum_near/pallas_call | solution.py:542
  28.4 0.0 copy-start
  28.4 0.1 collective-permute-start.2
  28.5 1.0 %all-to-all-done.rows_ref = bf16[8,7,32,256]{3,2,1,0:T(8,128)(2,1)} async-done(((bf16[8,7,32,256]{3,2,1,0:T(8,128)(2,1)}), bf16[8,7,32,256]{3,2,1,0:T(8,128)(2,1)}, u32[]{:S(2)}, u32[]{:S(2)}) %all-to-all-start) | async-done | bytes 917536 | tf_op jit(solution)/shard_map/all_to_all | solution.py:668
  29.6 7.1 %invert_blocks.1 = (bf16[3,208,256]{2,1,0:T(8,128)(2,1)S(1)}, bf16[208,256]{1,0:T(8,128)(2,1)S(1)}, bf16[8,32,256]{2,1,0:T(8,128)(2,1)S(1)}) custom-call(bf16[8,7,32,256]{3,2,1,0:T(8,128)(2,1)} %all-to-all-done.rows_ref), custom_call_target="tpu_custom_call" | custom-call | flops 7247757312 | bytes 2097152 | tf_op jit(solution)/shard_map/invert_blocks/pallas_call | solution.py:567
  36.7 0.0 copy-start.1
  36.7 2.0 %collective-permute-start.3 = (bf16[3,208,256]{2,1,0:T(8,128)(2,1)S(1)}, bf16[3,208,256]{2,1,0:T(8,128)(2,1)S(1)}, u32[]{:S(2)}, u32[]{:S(2)}) collective-permute-start(bf16[3,208,256]{2,1,0:T(8,128)(2,1)S(1)} %get-tuple-element.20._.here), channel_id=1, source_target_pairs={{0,1},{1,0},{2,3},{3,2},{4,5},{5,4},{6,7},{7,6},{8,9},{9,8},{10,11... | collective-permute-start | bytes 958472 | tf_op jit(solution)/shard_map/ppermute | solution.py:659
  38.7 0.0 collective-permute-start.4
  38.7 2.6 %collective-permute-start.7 = (bf16[208,256]{1,0:T(8,128)(2,1)S(1)}, bf16[208,256]{1,0:T(8,128)(2,1)S(1)}, u32[]{:S(2)}, u32[]{:S(2)}) collective-permute-start(bf16[208,256]{1,0:T(8,128)(2,1)S(1)} %get-tuple-element.25), channel_id=1, source_target_pairs={{0,2},{1,3},{2,0},{3,1},{4,6},{5,7},{6,4},{7,5},{8,10},{9,11},{10,... | collective-permute-start | bytes 319496 | tf_op jit(solution)/shard_map/ppermute | solution.py:659
  41.3 0.0 collective-permute-done.5.come
  41.3 0.0 collective-permute-start.8
  41.3 0.0 copy-done
  41.3 2.2 %hop.1.__ = bf16[384,1024]{1,0:T(8,128)(2,1)S(1)} custom-call(f32[256,1024]{1,0:T(8,128)S(1)} %copy-done, bf16[384,1024]{1,0:T(8,128)(2,1)} %collective-permute-done.5.come, bf16[3,208,256]{2,1,0:T(8,128)(2,1)S(1)} %get-tuple-element.20._.here), custom_call_target="tpu_custom_call" | custom-call | tf_op jit(solution)/shard_map/hop/pallas_call | solution.py:594
  43.5 0.0 copy-start.2
  43.6 0.0 collective-permute-done.4.other_ref
  43.6 1.2 %collective-permute-start.6 = (bf16[384,1024]{1,0:T(8,128)(2,1)S(1)}, bf16[384,1024]{1,0:T(8,128)(2,1)S(1)}, u32[]{:S(2)}, u32[]{:S(2)}) collective-permute-start(bf16[384,1024]{1,0:T(8,128)(2,1)S(1)} %hop.1.__), channel_id=1, source_target_pairs={{0,16},{4,12},{8,24},{12,4},{16,0},{20,28},{24,8},{28,20},{1,17},{... | collective-permute-start | bytes 2359304 | tf_op jit(solution)/shard_map/ppermute | solution.py:662
  44.8 0.5 collective-permute-done.2._.near_ref
  45.3 4.1 %invert_group.1._.g_ref = bf16[512,256]{1,0:T(8,128)(2,1)S(1)} custom-call(bf16[8,32,256]{2,1,0:T(8,128)(2,1)S(1)} %get-tuple-element.21.half_ref, bf16[8,32,256]{2,1,0:T(8,128)(2,1)S(1)} %collective-permute-done.4.other_ref, bf16[384,1024]{1,0:T(8,128)(2,1)S(1)} %collective-permute-done.2._.near_ref, bf16[384,1024]{1,0:T(8,128)(2,1)S(1)} %hop.1.__), custom_call_target="tpu_custom_call" | custom-call | tf_op jit(solution)/shard_map/invert_group/pallas_call | solution.py:580
  49.4 0.0 collective-permute-done.3.beside
  49.4 0.0 copy-done.1
  49.5 1.6 %ready.1 = (f32[256,1024]{1,0:T(8,128)S(1)}, bf16[2,4,256,256]{3,2,1,0:T(8,128)(2,1)S(1)}) custom-call(f32[256,1024]{1,0:T(8,128)S(1)} %copy-done.1, bf16[384,1024]{1,0:T(8,128)(2,1)S(1)} %collective-permute-done.2._.near_ref, bf16[3,208,256]{2,1,0:T(8,128)(2,1)S(1)} %get-tuple-element.20._.here, bf16[3,208,256]{2,1,0:T(8,128)(2,1)S(1)} %collective-permute-done.3.beside, ...), custom_call_target="tpu_custom_call" | custom-call | tf_op jit(solution)/shard_map/ready/pallas_call | solution.py:609
  51.1 0.0 collective-permute-done.7.two_off
  51.1 0.8 %collective-permute-done.8.three_off = bf16[208,256]{1,0:T(8,128)(2,1)S(1)} collective-permute-done((bf16[208,256]{1,0:T(8,128)(2,1)S(1)}, bf16[208,256]{1,0:T(8,128)(2,1)S(1)}, u32[]{:S(2)}, u32[]{:S(2)}) %collective-permute-start.8) | collective-permute-done | bytes 106528 | tf_op jit(solution)/shard_map/ppermute | solution.py:659
  51.9 0.0 copy-done.2
  51.9 2.7 %owned.1 = (f32[4,256,256]{2,1,0:T(8,128)}, f32[8,128]{1,0:T(8,128)S(1)}) custom-call(s32[32]{0:T(128)S(1)} %copy-done.2, bf16[3,208,256]{2,1,0:T(8,128)(2,1)S(1)} %get-tuple-element.20._.here, bf16[3,208,256]{2,1,0:T(8,128)(2,1)S(1)} %collective-permute-done.3.beside, bf16[208,256]{1,0:T(8,128)(2,1)S(1)} %collective-permute-done.7.two_off, ...), custom_call_target="tpu_custom_call" | custom-call | flops 20000000000 | tf_op jit(solution)/shard_map/owned/pallas_call | solution.py:620
  54.5 1.1 %collective-permute-done.6.come = bf16[384,1024]{1,0:T(8,128)(2,1)S(1)} collective-permute-done((bf16[384,1024]{1,0:T(8,128)(2,1)S(1)}, bf16[384,1024]{1,0:T(8,128)(2,1)S(1)}, u32[]{:S(2)}, u32[]{:S(2)}) %collective-permute-start.6) | collective-permute-done | bytes 786464 | tf_op jit(solution)/shard_map/ppermute | solution.py:662
  55.6 2.6 %finish.1 = f32[1024,256]{1,0:T(8,128)} custom-call(bf16[2,4,256,256]{3,2,1,0:T(8,128)(2,1)S(1)} %get-tuple-element.23.split_ref, bf16[512,256]{1,0:T(8,128)(2,1)S(1)} %invert_group.1._.g_ref, f32[256,1024]{1,0:T(8,128)S(1)} %get-tuple-element.24._.sum_ref, bf16[384,1024]{1,0:T(8,128)(2,1)S(1)} %collective-permute-done.6.come, f32[8,128]{1,0:T(8,128)S(1)} %get-tuple-element.26._), custom_call_target="tpu_custom_call" | custom-call | bytes 6291456 | tf_op jit(solution)/shard_map/finish/pallas_call | solution.py:634
Async XLA Ops:
  9.5 6.1 %collective-permute-start = (f32[3,256,1024]{2,1,0:T(8,128)}, f32[3,256,1024]{2,1,0:T(8,128)}, u32[]{:S(2)}, u32[]{:S(2)}) collective-permute-start(f32[3,256,1024]{2,1,0:T(8,128)} %get-tuple-element.15), channel_id=1, source_target_pairs={{0,4},{4,0},{8,12},{12,8},{16,20},{20,16},{24,28},{28,24},{1,5},{5... | collective-permute-start | bytes 9437192 | tf_op jit(solution)/shard_map/ppermute | solution.py:659
  10.1 12.2 %collective-permute-start.1 = (f32[1,256,1024]{2,1,0:T(8,128)}, f32[1,256,1024]{2,1,0:T(8,128)}, u32[]{:S(2)}, u32[]{:S(2)}) collective-permute-start(f32[1,256,1024]{2,1,0:T(8,128)} %get-tuple-element.16), channel_id=1, source_target_pairs={{0,4},{4,0},{8,12},{12,8},{16,20},{20,16},{24,28},{28,24},{1,5},{5... | collective-permute-start | bytes 3145736 | tf_op jit(solution)/shard_map/ppermute | solution.py:659
  10.1 19.4 %all-to-all-start = ((bf16[8,7,32,256]{3,2,1,0:T(8,128)(2,1)}), bf16[8,7,32,256]{3,2,1,0:T(8,128)(2,1)}, u32[]{:S(2)}, u32[]{:S(2)}) async-start(bf16[8,7,32,256]{3,2,1,0:T(8,128)(2,1)} %get-tuple-element.19), calls=%async_computation | async-start | bytes 1835008 | tf_op jit(solution)/shard_map/all_to_all | solution.py:668
  19.3 22.0 %collective-permute-start.5 = (bf16[384,1024]{1,0:T(8,128)(2,1)}, bf16[384,1024]{1,0:T(8,128)(2,1)}, u32[]{:S(2)}, u32[]{:S(2)}) collective-permute-start(bf16[384,1024]{1,0:T(8,128)(2,1)} %sum_far.1.refs_0_), channel_id=1, source_target_pairs={{0,8},{4,20},{8,0},{12,28},{16,24},{20,4},{24,16},{28,12},{1,9},{5... | collective-permute-start | bytes 2359304 | tf_op jit(solution)/shard_map/ppermute | solution.py:662
  28.4 12.9 %copy-start = (f32[256,1024]{1,0:T(8,128)S(1)}, f32[256,1024]{1,0:T(8,128)}, u32[]{:S(2)}) copy-start(f32[256,1024]{1,0:T(8,128)} %get-tuple-element.22.rest) | copy-start | bytes 3145732
  28.4 16.9 %collective-permute-start.2 = (bf16[384,1024]{1,0:T(8,128)(2,1)}, bf16[384,1024]{1,0:T(8,128)(2,1)S(1)}, u32[]{:S(2)}, u32[]{:S(2)}) collective-permute-start(bf16[384,1024]{1,0:T(8,128)(2,1)} %get-tuple-element.18), channel_id=1, source_target_pairs={{0,8},{4,20},{8,0},{12,28},{16,24},{20,4},{24,16},{28,12},{1,9},{5... | collective-permute-start | bytes 2359304 | tf_op jit(solution)/shard_map/ppermute | solution.py:662
  36.7 12.8 %copy-start.1 = (f32[256,1024]{1,0:T(8,128)S(1)}, f32[256,1024]{1,0:T(8,128)}, u32[]{:S(2)}) copy-start(f32[256,1024]{1,0:T(8,128)} %get-tuple-element.17.own_ref) | copy-start | bytes 3145732
  36.7 12.8 %collective-permute-start.3 = (bf16[3,208,256]{2,1,0:T(8,128)(2,1)S(1)}, bf16[3,208,256]{2,1,0:T(8,128)(2,1)S(1)}, u32[]{:S(2)}, u32[]{:S(2)}) collective-permute-start(bf16[3,208,256]{2,1,0:T(8,128)(2,1)S(1)} %get-tuple-element.20._.here), channel_id=1, source_target_pairs={{0,1},{1,0},{2,3},{3,2},{4,5},{5,4},{6,7},{7,6},{8,9},{9,8},{10,11... | collective-permute-start | bytes 958472 | tf_op jit(solution)/shard_map/ppermute | solution.py:659
  38.7 4.9 %collective-permute-start.4 = (bf16[8,32,256]{2,1,0:T(8,128)(2,1)S(1)}, bf16[8,32,256]{2,1,0:T(8,128)(2,1)S(1)}, u32[]{:S(2)}, u32[]{:S(2)}) collective-permute-start(bf16[8,32,256]{2,1,0:T(8,128)(2,1)S(1)} %get-tuple-element.21.half_ref), channel_id=1, source_target_pairs={{0,4},{4,0},{8,12},{12,8},{16,20},{20,16},{24,28},{28,24},{1,5},{5... | collective-permute-start | bytes 393224 | tf_op jit(solution)/shard_map/ppermute | solution.py:659
  38.7 12.4 %collective-permute-start.7 = (bf16[208,256]{1,0:T(8,128)(2,1)S(1)}, bf16[208,256]{1,0:T(8,128)(2,1)S(1)}, u32[]{:S(2)}, u32[]{:S(2)}) collective-permute-start(bf16[208,256]{1,0:T(8,128)(2,1)S(1)} %get-tuple-element.25), channel_id=1, source_target_pairs={{0,2},{1,3},{2,0},{3,1},{4,6},{5,7},{6,4},{7,5},{8,10},{9,11},{10,... | collective-permute-start | bytes 319496 | tf_op jit(solution)/shard_map/ppermute | solution.py:659
  41.3 10.6 %collective-permute-start.8 = (bf16[208,256]{1,0:T(8,128)(2,1)S(1)}, bf16[208,256]{1,0:T(8,128)(2,1)S(1)}, u32[]{:S(2)}, u32[]{:S(2)}) collective-permute-start(bf16[208,256]{1,0:T(8,128)(2,1)S(1)} %get-tuple-element.25), channel_id=1, source_target_pairs={{0,3},{1,2},{2,1},{3,0},{4,7},{5,6},{6,5},{7,4},{8,11},{9,10},{10,... | collective-permute-start | bytes 319496 | tf_op jit(solution)/shard_map/ppermute | solution.py:659
  43.5 8.3 %copy-start.2 = (s32[32]{0:T(128)S(1)}, s32[32]{0:T(128)}, u32[]{:S(2)}) copy-start(s32[32]{0:T(128)} %owner.3) | copy-start | bytes 388
  43.6 12.1 %collective-permute-start.6 = (bf16[384,1024]{1,0:T(8,128)(2,1)S(1)}, bf16[384,1024]{1,0:T(8,128)(2,1)S(1)}, u32[]{:S(2)}, u32[]{:S(2)}) collective-permute-start(bf16[384,1024]{1,0:T(8,128)(2,1)S(1)} %hop.1.__), channel_id=1, source_target_pairs={{0,16},{4,12},{8,24},{12,4},{16,0},{20,28},{24,8},{28,20},{1,17},{... | collective-permute-start | bytes 2359304 | tf_op jit(solution)/shard_map/ppermute | solution.py:662

commit v7 on v6

--- a/solution.py
+++ b/solution.py
@@ -466,60 +466,44 @@
     copy.wait()
 
 
-def group_body(scale, half_ref, other_ref, _, __, out_ref, rows, sems):
-    loads = start_all([half_ref, other_ref], [rows.at[0], rows.at[1]], sems)
-    for load in loads:
-        load.wait()
-    parts = two(inverses_of([rows[...].reshape(-1, FACTOR_BLOCK)], scale)[0].T)
+def group_body(scale, half, other, _, __, out_ref):
+    rows = jnp.concatenate([half[...].reshape(-1, FACTOR_BLOCK), other[...].reshape(-1, FACTOR_BLOCK)], axis=0)
+    parts = two(inverses_of([rows], scale)[0].T)
     out_ref[...] = jnp.concatenate(parts, axis=0)
 
 
-def ready_body(own_ref, near_ref, here, beside, _, sum_ref, split, own, near, need, sems):
-    loads = start_all(
-        [here.at[pl.ds(0, 2)], beside.at[pl.ds(0, 2)], own_ref, near_ref],
-        [need.at[pl.ds(0, 2)], need.at[pl.ds(2, 2)], own, near],
-        sems,
-    )
+def ready_body(own, near, here, beside, _, sum_ref, split):
     odd = lax.axis_index("tensor") % 2
-    for k in range(2):
-        loads[k].wait()
+    for k, held in enumerate((here, beside)):
         for p in range(2):
-            high, low = two(unfold(need.at[2 * k + p]))
+            high, low = two(unfold(held.at[p]))
             at = 2 * (odd if k == 0 else 1 - odd) + p
             split[0, at] = high
             split[1, at] = low
-    for load in loads[2:]:
-        load.wait()
     sum_ref[...] = own[...] + decode(near)
 
 
-def owned_body(owner, here, beside, two_off, three_off, _, out_ref, done_ref, held, sems):
-    loads = start_all([here.at[2], beside.at[2], two_off, three_off], [held.at[k] for k in range(4)], sems)
+def owned_body(owner, here, beside, two_off, three_off, _, out_ref, done_ref):
     z = lax.axis_index("tensor")
     me = lax.axis_index("dp")
     count = jnp.int32(0)
     for b in range(owner.shape[0]):
         count = count + jnp.where(owner[b] == me, 1, 0)
-    for k, load in enumerate(loads):
-        load.wait()
+    for k, held in enumerate((here.at[2], beside.at[2], two_off, three_off)):
         slot = z ^ k
-        out_ref[slot] = jnp.where(slot < count, unfold(held.at[k]), 0.0)
+        out_ref[slot] = jnp.where(slot < count, unfold(held), 0.0)
     done_ref[...] = jnp.zeros(done_ref.shape, f32)
 
 
-def finish_body(split_ref, g_ref, sum_ref, come, _, step_out, split, left, total, come_in, step, sems, out_sems):
+def finish_body(split, left, so_far, come, _, step_out, step, out_sems):
     width = FACTOR_BLOCK
-    loads = start_all([g_ref, sum_ref, come, split_ref], [left, total, come_in, split], sems)
 
     def dot(a, c, dims):
         return lax.dot_general(a, c, (dims, ((), ())), preferred_element_type=f32)
 
-    for load in loads[:3]:
-        load.wait()
-    sum_high, sum_low = two(total[...] + decode(come_in))
+    sum_high, sum_low = two(so_far[...] + decode(come))
     both = dot(left[...], sum_high, ((1,), (0,)))
     right_high, right_low = two(both[:width] + (both[width:] + dot(left[:width], sum_low, ((1,), (0,)))))
-    loads[3].wait()
     stores = []
     for b in range(split.shape[1]):
         part = slice(b * width, (b + 1) * width)
@@ -581,9 +565,8 @@
         functools.partial(group_body, scale),
         "invert_group",
         shaped((2 * FACTOR_BLOCK, FACTOR_BLOCK), bf16),
-        [ANY] * 4,
+        [VMEM, VMEM, ANY, ANY],
         VMEM,
-        [pltpu.VMEM((2, *half.shape), bf16), dma(2)],
     )(half, other, after, and_after)
 
 
@@ -605,14 +588,12 @@
 
 def ready(own_sum, near, inverses, beside, after):
     square = (4, FACTOR_BLOCK, FACTOR_BLOCK)
-    held = pltpu.VMEM((4, *inverses.shape[1:]), bf16)
     return call(
         ready_body,
         "ready",
         (shaped(own_sum.shape), shaped((2, *square), bf16)),
-        [ANY] * 5,
+        [VMEM] * 4 + [ANY],
         (VMEM,) * 2,
-        [pltpu.VMEM(own_sum.shape, f32), pltpu.VMEM(near.shape, bf16), held, dma(4)],
     )(own_sum, near, inverses, beside, after)
 
 
@@ -621,9 +602,8 @@
         owned_body,
         "owned",
         (shaped((4, FACTOR_BLOCK, FACTOR_BLOCK)), shaped((8, 128))),
-        [SMEM] + [ANY] * 5,
+        [SMEM] + [VMEM] * 4 + [ANY],
         (VMEM,) * 2,
-        [pltpu.VMEM((4, *two_off.shape), bf16), dma(4)],
         flops=OWNED_FLOPS,
     )(block_owner, inverses, beside, two_off, three_off, after)
 
@@ -635,17 +615,9 @@
         finish_body,
         "finish",
         shaped((share, group_w)),
-        [ANY] * 5,
+        [VMEM] * 4 + [ANY],
         ANY,
-        [
-            pltpu.VMEM(split.shape, bf16),
-            pltpu.VMEM(g_parts.shape, bf16),
-            pltpu.VMEM(so_far.shape, f32),
-            pltpu.VMEM(come.shape, bf16),
-            pltpu.VMEM((blocks, FACTOR_BLOCK, group_w), f32),
-            dma(4),
-            dma(blocks),
-        ],
+        [pltpu.VMEM((blocks, FACTOR_BLOCK, group_w), f32), dma(blocks)],
         moved=6 * MIB,
     )(split, g_parts, so_far, come, after)
 

time: 58.8 us -> 58.7 us (level)
  Pallas kernels: 39 us -> 37.2 us
  waiting for transfers between devices: 3.81 us -> 5.53 us
    ppermute x6, waiting for transfers between devices: 1.21 us -> 2.13 us  [swap(): return lax.ppermute(block, axis, [(i, i ^ bit) for i in range(count)])]
    ppermute x3, waiting for transfers between devices: 1.57 us -> 2.36 us  [travel(): lax.ppermute(block, 'dp', [(i, i ^ (odd if i % 2 else even)) for i in ran...]
    pallas_call x1, Pallas kernels: 2.66 us -> 1.88 us  [owned_blocks(): call(owned_body, 'owned', (shaped((4, FACTOR_BLOCK, FACTOR_BLOCK)), shape...]
  transfers between devices with their start and end apart: 10 -> 10, of which waited for: 5 -> 5; matrix products, arithmetic and copies ran while one was open for 0% -> 0% of each run, Pallas kernels for 47% -> 45%
where the time goes in v7:
time: 58.7 us; the launch traced here: 58.3 us
  Pallas kernels  37.2 us (63%)
  starting transfers between devices  14.6 us (25%)
  waiting for transfers between devices  5.53 us (9%)
  between operations  0.93 us (2%)
    pallas_call x2, Pallas kernels, sum_cores(): call(functools.partial(sum_body, which), name, tuple((shaped(wired, bf16)...  9.77 us
    pallas_call x1, Pallas kernels, project(): call(project_body, 'project', (rest, one, shaped((count, 7, samples // 2,...  8.91 us
    pallas_call x1, Pallas kernels, invert(): call(functools.partial(invert_body, scale), 'invert_blocks', (shaped((3,...  7.09 us
    ppermute x6, starting transfers between devices, swap(): return lax.ppermute(block, axis, [(i, i ^ bit) for i in range(count)])  5.22 us
    all_to_all x1, starting transfers between devices, square_device(): rows = lax.all_to_all(picked, 'dp', split_axis=0, concat_axis=0, tiled=True)  5.15 us
    ppermute x3, starting transfers between devices, travel(): lax.ppermute(block, 'dp', [(i, i ^ (odd if i % 2 else even)) for i in ran...  4.26 us
    pallas_call x1, Pallas kernels, invert_group(): call(functools.partial(group_body, scale), 'invert_group', shaped((2 * FA...  3.58 us
    pallas_call x1, Pallas kernels, hop(): call(hop_body, 'hop', shaped(wired, bf16), [ANY] * 3, ANY, [pltpu.VMEM((H...  2.46 us
  transfers between devices with their start and end apart: 10, of which 5 were waited for; matrix products, arithmetic and copies ran while one was open for 0% of the time, Pallas kernels for 45%

profile of v7, /device:TPU:0, one launch (start us, length us, event | category | flops | bytes accessed | tf_op | source)
XLA Modules:
  0.0 58.3 jit_solution(13003276124780207298)
XLA Ops:
  0.6 8.9 %project.1 = (f32[3,256,1024]{2,1,0:T(8,128)}, f32[1,256,1024]{2,1,0:T(8,128)}, bf16[8,7,32,256]{3,2,1,0:T(8,128)(2,1)}) custom-call(s32[32]{0:T(128)} %owner.3, s32[1,64]{1,0:T(1,128)} %bitcast.1, bf16[768,256]{1,0:T(8,128)(2,1)} %cot_ref.5, bf16[768,8192]{1,0:T(8,128)(2,1)} %act_ref.5), custom_call_target="tpu_custom_call" | custom-call | flops 4026531840 | bytes 16777216 | tf_op jit(solution)/shard_map/project/pallas_call | solution.py:289
  9.5 0.5 collective-permute-start
  10.1 0.1 collective-permute-start.1
  10.1 5.1 %all-to-all-start = ((bf16[8,7,32,256]{3,2,1,0:T(8,128)(2,1)}), bf16[8,7,32,256]{3,2,1,0:T(8,128)(2,1)}, u32[]{:S(2)}, u32[]{:S(2)}) async-start(bf16[8,7,32,256]{3,2,1,0:T(8,128)(2,1)} %get-tuple-element.19), calls=%async_computation | async-start | bytes 1835008 | tf_op jit(solution)/shard_map/all_to_all | solution.py:640
  15.3 0.4 collective-permute-done.got_ref.own_got_ref
  15.7 3.6 %sum_far.1.refs_0_ = bf16[384,1024]{1,0:T(8,128)(2,1)} custom-call(bf16[768,256]{1,0:T(8,128)(2,1)} %cot_ref.5, bf16[768,8192]{1,0:T(8,128)(2,1)} %act_ref.5, f32[3,256,1024]{2,1,0:T(8,128)} %collective-permute-done.got_ref.own_got_ref, f32[3,256,1024]{2,1,0:T(8,128)} %collective-permute-done.got_ref.own_got_ref), custom_call_target="tpu_custom_call" | custom-call | bytes 4194304 | tf_op jit(solution)/shard_map/sum_far/pallas_call | solution.py:526
  19.3 2.9 %collective-permute-start.5 = (bf16[384,1024]{1,0:T(8,128)(2,1)}, bf16[384,1024]{1,0:T(8,128)(2,1)}, u32[]{:S(2)}, u32[]{:S(2)}) collective-permute-start(bf16[384,1024]{1,0:T(8,128)(2,1)} %sum_far.1.refs_0_), channel_id=1, source_target_pairs={{0,8},{4,20},{8,0},{12,28},{16,24},{20,4},{24,16},{28,12},{1,9},{5... | collective-permute-start | bytes 2359304 | tf_op jit(solution)/shard_map/ppermute | solution.py:634
  22.3 0.0 collective-permute-done.1.own_got_ref
  22.3 6.2 %sum_near.1 = (bf16[384,1024]{1,0:T(8,128)(2,1)}, f32[256,1024]{1,0:T(8,128)}, f32[256,1024]{1,0:T(8,128)}) custom-call(bf16[768,256]{1,0:T(8,128)(2,1)} %cot_ref.5, bf16[768,8192]{1,0:T(8,128)(2,1)} %act_ref.5, f32[3,256,1024]{2,1,0:T(8,128)} %collective-permute-done.got_ref.own_got_ref, f32[1,256,1024]{2,1,0:T(8,128)} %collective-permute-done.1.own_got_ref, ...), custom_call_target="tpu_custom_call" | custom-call | bytes 12582912 | tf_op jit(solution)/shard_map/sum_near/pallas_call | solution.py:526
  28.4 0.0 copy-start
  28.4 0.1 collective-permute-start.2
  28.5 1.0 %all-to-all-done.rows_ref = bf16[8,7,32,256]{3,2,1,0:T(8,128)(2,1)} async-done(((bf16[8,7,32,256]{3,2,1,0:T(8,128)(2,1)}), bf16[8,7,32,256]{3,2,1,0:T(8,128)(2,1)}, u32[]{:S(2)}, u32[]{:S(2)}) %all-to-all-start) | async-done | bytes 917536 | tf_op jit(solution)/shard_map/all_to_all | solution.py:640
  29.6 7.1 %invert_blocks.1 = (bf16[3,208,256]{2,1,0:T(8,128)(2,1)S(1)}, bf16[208,256]{1,0:T(8,128)(2,1)S(1)}, bf16[8,32,256]{2,1,0:T(8,128)(2,1)S(1)}) custom-call(bf16[8,7,32,256]{3,2,1,0:T(8,128)(2,1)} %all-to-all-done.rows_ref), custom_call_target="tpu_custom_call" | custom-call | flops 7247757312 | bytes 2097152 | tf_op jit(solution)/shard_map/invert_blocks/pallas_call | solution.py:551
  36.7 0.0 copy-start.1
  36.7 2.0 %collective-permute-start.3 = (bf16[3,208,256]{2,1,0:T(8,128)(2,1)S(1)}, bf16[3,208,256]{2,1,0:T(8,128)(2,1)S(1)}, u32[]{:S(2)}, u32[]{:S(2)}) collective-permute-start(bf16[3,208,256]{2,1,0:T(8,128)(2,1)S(1)} %get-tuple-element.20._.here), channel_id=1, source_target_pairs={{0,1},{1,0},{2,3},{3,2},{4,5},{5,4},{6,7},{7,6},{8,9},{9,8},{10,11... | collective-permute-start | bytes 958472 | tf_op jit(solution)/shard_map/ppermute | solution.py:631
  38.7 0.0 collective-permute-start.4
  38.7 2.6 %collective-permute-start.7 = (bf16[208,256]{1,0:T(8,128)(2,1)S(1)}, bf16[208,256]{1,0:T(8,128)(2,1)S(1)}, u32[]{:S(2)}, u32[]{:S(2)}) collective-permute-start(bf16[208,256]{1,0:T(8,128)(2,1)S(1)} %get-tuple-element.25), channel_id=1, source_target_pairs={{0,2},{1,3},{2,0},{3,1},{4,6},{5,7},{6,4},{7,5},{8,10},{9,11},{10,... | collective-permute-start | bytes 319496 | tf_op jit(solution)/shard_map/ppermute | solution.py:631
  41.3 0.0 collective-permute-done.5.come
  41.3 0.0 collective-permute-start.8
  41.3 0.0 copy-done
  41.3 2.5 %hop.1.__ = bf16[384,1024]{1,0:T(8,128)(2,1)S(1)} custom-call(f32[256,1024]{1,0:T(8,128)S(1)} %copy-done, bf16[384,1024]{1,0:T(8,128)(2,1)} %collective-permute-done.5.come, bf16[3,208,256]{2,1,0:T(8,128)(2,1)S(1)} %get-tuple-element.20._.here), custom_call_target="tpu_custom_call" | custom-call | tf_op jit(solution)/shard_map/hop/pallas_call | solution.py:577
  43.8 0.0 copy-start.2
  43.8 0.0 collective-permute-done.4.other
  43.8 1.2 %collective-permute-start.6 = (bf16[384,1024]{1,0:T(8,128)(2,1)S(1)}, bf16[384,1024]{1,0:T(8,128)(2,1)S(1)}, u32[]{:S(2)}, u32[]{:S(2)}) collective-permute-start(bf16[384,1024]{1,0:T(8,128)(2,1)S(1)} %hop.1.__), channel_id=1, source_target_pairs={{0,16},{4,12},{8,24},{12,4},{16,0},{20,28},{24,8},{28,20},{1,17},{... | collective-permute-start | bytes 2359304 | tf_op jit(solution)/shard_map/ppermute | solution.py:634
  45.0 0.3 collective-permute-done.2._.near
  45.3 3.6 %invert_group.1._.left = bf16[512,256]{1,0:T(8,128)(2,1)S(1)} custom-call(bf16[8,32,256]{2,1,0:T(8,128)(2,1)S(1)} %get-tuple-element.21.half, bf16[8,32,256]{2,1,0:T(8,128)(2,1)S(1)} %collective-permute-done.4.other, bf16[384,1024]{1,0:T(8,128)(2,1)S(1)} %collective-permute-done.2._.near, bf16[384,1024]{1,0:T(8,128)(2,1)S(1)} %hop.1.__), custom_call_target="tpu_custom_call" | custom-call | tf_op jit(solution)/shard_map/invert_group/pallas_call | solution.py:564
  48.9 0.0 collective-permute-done.3.beside
  48.9 0.0 copy-done.1
  48.9 1.2 %ready.1 = (f32[256,1024]{1,0:T(8,128)S(1)}, bf16[2,4,256,256]{3,2,1,0:T(8,128)(2,1)S(1)}) custom-call(f32[256,1024]{1,0:T(8,128)S(1)} %copy-done.1, bf16[384,1024]{1,0:T(8,128)(2,1)S(1)} %collective-permute-done.2._.near, bf16[3,208,256]{2,1,0:T(8,128)(2,1)S(1)} %get-tuple-element.20._.here, bf16[3,208,256]{2,1,0:T(8,128)(2,1)S(1)} %collective-permute-done.3.beside, ...), custom_call_target="tpu_custom_call" | custom-call | tf_op jit(solution)/shard_map/ready/pallas_call | solution.py:591
  50.1 0.0 collective-permute-done.7.two_off
  50.1 1.7 %collective-permute-done.8.three_off = bf16[208,256]{1,0:T(8,128)(2,1)S(1)} collective-permute-done((bf16[208,256]{1,0:T(8,128)(2,1)S(1)}, bf16[208,256]{1,0:T(8,128)(2,1)S(1)}, u32[]{:S(2)}, u32[]{:S(2)}) %collective-permute-start.8) | collective-permute-done | bytes 106528 | tf_op jit(solution)/shard_map/ppermute | solution.py:631
  51.9 0.0 copy-done.2
  51.9 1.9 %owned.1 = (f32[4,256,256]{2,1,0:T(8,128)}, f32[8,128]{1,0:T(8,128)S(1)}) custom-call(s32[32]{0:T(128)S(1)} %copy-done.2, bf16[3,208,256]{2,1,0:T(8,128)(2,1)S(1)} %get-tuple-element.20._.here, bf16[3,208,256]{2,1,0:T(8,128)(2,1)S(1)} %collective-permute-done.3.beside, bf16[208,256]{1,0:T(8,128)(2,1)S(1)} %collective-permute-done.7.two_off, ...), custom_call_target="tpu_custom_call" | custom-call | flops 20000000000 | tf_op jit(solution)/shard_map/owned/pallas_call | solution.py:601
  53.8 2.1 %collective-permute-done.6.come = bf16[384,1024]{1,0:T(8,128)(2,1)S(1)} collective-permute-done((bf16[384,1024]{1,0:T(8,128)(2,1)S(1)}, bf16[384,1024]{1,0:T(8,128)(2,1)S(1)}, u32[]{:S(2)}, u32[]{:S(2)}) %collective-permute-start.6) | collective-permute-done | bytes 786464 | tf_op jit(solution)/shard_map/ppermute | solution.py:634
  55.8 2.3 %finish.1 = f32[1024,256]{1,0:T(8,128)} custom-call(bf16[2,4,256,256]{3,2,1,0:T(8,128)(2,1)S(1)} %get-tuple-element.23.split, bf16[512,256]{1,0:T(8,128)(2,1)S(1)} %invert_group.1._.left, f32[256,1024]{1,0:T(8,128)S(1)} %get-tuple-element.24._.so_far, bf16[384,1024]{1,0:T(8,128)(2,1)S(1)} %collective-permute-done.6.come, f32[8,128]{1,0:T(8,128)S(1)} %get-tuple-element.26._), custom_call_target="tpu_custom_call" | custom-call | bytes 6291456 | tf_op jit(solution)/shard_map/finish/pallas_call | solution.py:614
Async XLA Ops:
  9.5 6.1 %collective-permute-start = (f32[3,256,1024]{2,1,0:T(8,128)}, f32[3,256,1024]{2,1,0:T(8,128)}, u32[]{:S(2)}, u32[]{:S(2)}) collective-permute-start(f32[3,256,1024]{2,1,0:T(8,128)} %get-tuple-element.15), channel_id=1, source_target_pairs={{0,4},{4,0},{8,12},{12,8},{16,20},{20,16},{24,28},{28,24},{1,5},{5... | collective-permute-start | bytes 9437192 | tf_op jit(solution)/shard_map/ppermute | solution.py:631
  10.1 12.2 %collective-permute-start.1 = (f32[1,256,1024]{2,1,0:T(8,128)}, f32[1,256,1024]{2,1,0:T(8,128)}, u32[]{:S(2)}, u32[]{:S(2)}) collective-permute-start(f32[1,256,1024]{2,1,0:T(8,128)} %get-tuple-element.16), channel_id=1, source_target_pairs={{0,4},{4,0},{8,12},{12,8},{16,20},{20,16},{24,28},{28,24},{1,5},{5... | collective-permute-start | bytes 3145736 | tf_op jit(solution)/shard_map/ppermute | solution.py:631
  10.1 19.4 %all-to-all-start = ((bf16[8,7,32,256]{3,2,1,0:T(8,128)(2,1)}), bf16[8,7,32,256]{3,2,1,0:T(8,128)(2,1)}, u32[]{:S(2)}, u32[]{:S(2)}) async-start(bf16[8,7,32,256]{3,2,1,0:T(8,128)(2,1)} %get-tuple-element.19), calls=%async_computation | async-start | bytes 1835008 | tf_op jit(solution)/shard_map/all_to_all | solution.py:640
  19.3 22.0 %collective-permute-start.5 = (bf16[384,1024]{1,0:T(8,128)(2,1)}, bf16[384,1024]{1,0:T(8,128)(2,1)}, u32[]{:S(2)}, u32[]{:S(2)}) collective-permute-start(bf16[384,1024]{1,0:T(8,128)(2,1)} %sum_far.1.refs_0_), channel_id=1, source_target_pairs={{0,8},{4,20},{8,0},{12,28},{16,24},{20,4},{24,16},{28,12},{1,9},{5... | collective-permute-start | bytes 2359304 | tf_op jit(solution)/shard_map/ppermute | solution.py:634
  28.4 12.9 %copy-start = (f32[256,1024]{1,0:T(8,128)S(1)}, f32[256,1024]{1,0:T(8,128)}, u32[]{:S(2)}) copy-start(f32[256,1024]{1,0:T(8,128)} %get-tuple-element.22.rest) | copy-start | bytes 3145732
  28.4 16.9 %collective-permute-start.2 = (bf16[384,1024]{1,0:T(8,128)(2,1)}, bf16[384,1024]{1,0:T(8,128)(2,1)S(1)}, u32[]{:S(2)}, u32[]{:S(2)}) collective-permute-start(bf16[384,1024]{1,0:T(8,128)(2,1)} %get-tuple-element.18), channel_id=1, source_target_pairs={{0,8},{4,20},{8,0},{12,28},{16,24},{20,4},{24,16},{28,12},{1,9},{5... | collective-permute-start | bytes 2359304 | tf_op jit(solution)/shard_map/ppermute | solution.py:634
  36.7 12.2 %copy-start.1 = (f32[256,1024]{1,0:T(8,128)S(1)}, f32[256,1024]{1,0:T(8,128)}, u32[]{:S(2)}) copy-start(f32[256,1024]{1,0:T(8,128)} %get-tuple-element.17.own) | copy-start | bytes 3145732
  36.7 12.2 %collective-permute-start.3 = (bf16[3,208,256]{2,1,0:T(8,128)(2,1)S(1)}, bf16[3,208,256]{2,1,0:T(8,128)(2,1)S(1)}, u32[]{:S(2)}, u32[]{:S(2)}) collective-permute-start(bf16[3,208,256]{2,1,0:T(8,128)(2,1)S(1)} %get-tuple-element.20._.here), channel_id=1, source_target_pairs={{0,1},{1,0},{2,3},{3,2},{4,5},{5,4},{6,7},{7,6},{8,9},{9,8},{10,11... | collective-permute-start | bytes 958472 | tf_op jit(solution)/shard_map/ppermute | solution.py:631
  38.7 5.1 %collective-permute-start.4 = (bf16[8,32,256]{2,1,0:T(8,128)(2,1)S(1)}, bf16[8,32,256]{2,1,0:T(8,128)(2,1)S(1)}, u32[]{:S(2)}, u32[]{:S(2)}) collective-permute-start(bf16[8,32,256]{2,1,0:T(8,128)(2,1)S(1)} %get-tuple-element.21.half), channel_id=1, source_target_pairs={{0,4},{4,0},{8,12},{12,8},{16,20},{20,16},{24,28},{28,24},{1,5},{5... | collective-permute-start | bytes 393224 | tf_op jit(solution)/shard_map/ppermute | solution.py:631
  38.7 11.4 %collective-permute-start.7 = (bf16[208,256]{1,0:T(8,128)(2,1)S(1)}, bf16[208,256]{1,0:T(8,128)(2,1)S(1)}, u32[]{:S(2)}, u32[]{:S(2)}) collective-permute-start(bf16[208,256]{1,0:T(8,128)(2,1)S(1)} %get-tuple-element.25), channel_id=1, source_target_pairs={{0,2},{1,3},{2,0},{3,1},{4,6},{5,7},{6,4},{7,5},{8,10},{9,11},{10,... | collective-permute-start | bytes 319496 | tf_op jit(solution)/shard_map/ppermute | solution.py:631
  41.3 10.6 %collective-permute-start.8 = (bf16[208,256]{1,0:T(8,128)(2,1)S(1)}, bf16[208,256]{1,0:T(8,128)(2,1)S(1)}, u32[]{:S(2)}, u32[]{:S(2)}) collective-permute-start(bf16[208,256]{1,0:T(8,128)(2,1)S(1)} %get-tuple-element.25), channel_id=1, source_target_pairs={{0,3},{1,2},{2,1},{3,0},{4,7},{5,6},{6,5},{7,4},{8,11},{9,10},{10,... | collective-permute-start | bytes 319496 | tf_op jit(solution)/shard_map/ppermute | solution.py:631
  43.8 8.1 %copy-start.2 = (s32[32]{0:T(128)S(1)}, s32[32]{0:T(128)}, u32[]{:S(2)}) copy-start(s32[32]{0:T(128)} %owner.3) | copy-start | bytes 388
  43.8 12.1 %collective-permute-start.6 = (bf16[384,1024]{1,0:T(8,128)(2,1)S(1)}, bf16[384,1024]{1,0:T(8,128)(2,1)S(1)}, u32[]{:S(2)}, u32[]{:S(2)}) collective-permute-start(bf16[384,1024]{1,0:T(8,128)(2,1)S(1)} %hop.1.__), channel_id=1, source_target_pairs={{0,16},{4,12},{8,24},{12,4},{16,0},{20,28},{24,8},{28,20},{1,17},{... | collective-permute-start | bytes 2359304 | tf_op jit(solution)/shard_map/ppermute | solution.py:634

commit v8 on v7

--- a/solution.py
+++ b/solution.py
@@ -131,7 +131,7 @@
 MIB = 1 << 20
 VMEM_MIB = 32
 PROJECT_MIB = 64
-SUM_MIB = 64
+SUM_MIB = 62
 AHEAD = 3
 PROJECT_AHEAD = 6
 HOP_PARTS = 2

time: 58.7 us -> 56.9 us (0.969)
  Pallas kernels: 37.2 us -> 35.3 us
  starting transfers between devices: 14.6 us -> 15.3 us
    ppermute x6, waiting for transfers between devices: 2.13 us -> 0.41 us  [swap(): return lax.ppermute(block, axis, [(i, i ^ bit) for i in range(count)])]
    ppermute x3, waiting for transfers between devices: 2.36 us -> 3.77 us  [travel(): lax.ppermute(block, 'dp', [(i, i ^ (odd if i % 2 else even)) for i in ran...]
    pallas_call x1, Pallas kernels: 7.09 us -> 6.03 us  [invert(): call(functools.partial(invert_body, scale), 'invert_blocks', (shaped((3,...]
    pallas_call x1, Pallas kernels: 2.46 us -> 1.57 us  [hop(): call(hop_body, 'hop', shaped(wired, bf16), [ANY] * 3, ANY, [pltpu.VMEM((H...]
  transfers between devices with their start and end apart: 10 -> 10, of which waited for: 5 -> 4; matrix products, arithmetic and copies ran while one was open for 0% -> 0% of each run, Pallas kernels for 45% -> 43%
where the time goes in v8:
time: 56.9 us; the launch traced here: 56.6 us
  Pallas kernels  35.3 us (62%)
  starting transfers between devices  15.3 us (27%)
  waiting for transfers between devices  5.07 us (9%)
  between operations  0.94 us (2%)
    pallas_call x2, Pallas kernels, sum_cores(): call(functools.partial(sum_body, which), name, tuple((shaped(wired, bf16)...  9.77 us
    pallas_call x1, Pallas kernels, project(): call(project_body, 'project', (rest, one, shaped((count, 7, samples // 2,...  8.91 us
    pallas_call x1, Pallas kernels, invert(): call(functools.partial(invert_body, scale), 'invert_blocks', (shaped((3,...  6.03 us
    ppermute x6, starting transfers between devices, swap(): return lax.ppermute(block, axis, [(i, i ^ bit) for i in range(count)])  5.6 us
    all_to_all x1, starting transfers between devices, square_device(): rows = lax.all_to_all(picked, 'dp', split_axis=0, concat_axis=0, tiled=True)  5.15 us
    ppermute x3, starting transfers between devices, travel(): lax.ppermute(block, 'dp', [(i, i ^ (odd if i % 2 else even)) for i in ran...  4.55 us
    ppermute x3, waiting for transfers between devices, travel(): lax.ppermute(block, 'dp', [(i, i ^ (odd if i % 2 else even)) for i in ran...  3.77 us
    pallas_call x1, Pallas kernels, invert_group(): call(functools.partial(group_body, scale), 'invert_group', shaped((2 * FA...  3.58 us
  transfers between devices with their start and end apart: 10, of which 4 were waited for; matrix products, arithmetic and copies ran while one was open for 0% of the time, Pallas kernels for 43%

profile of v8, /device:TPU:0, one launch (start us, length us, event | category | flops | bytes accessed | tf_op | source)
XLA Modules:
  0.0 56.6 jit_solution(17148482536384801911)
XLA Ops:
  0.6 8.9 %project.1 = (f32[3,256,1024]{2,1,0:T(8,128)}, f32[1,256,1024]{2,1,0:T(8,128)}, bf16[8,7,32,256]{3,2,1,0:T(8,128)(2,1)}) custom-call(s32[32]{0:T(128)} %owner.3, s32[1,64]{1,0:T(1,128)} %bitcast.1, bf16[768,256]{1,0:T(8,128)(2,1)} %cot_ref.5, bf16[768,8192]{1,0:T(8,128)(2,1)} %act_ref.5), custom_call_target="tpu_custom_call" | custom-call | flops 4026531840 | bytes 16777216 | tf_op jit(solution)/shard_map/project/pallas_call | solution.py:289
  9.5 0.5 collective-permute-start
  10.1 0.1 collective-permute-start.1
  10.1 5.1 %all-to-all-start = ((bf16[8,7,32,256]{3,2,1,0:T(8,128)(2,1)}), bf16[8,7,32,256]{3,2,1,0:T(8,128)(2,1)S(1)}, u32[]{:S(2)}, u32[]{:S(2)}) async-start(bf16[8,7,32,256]{3,2,1,0:T(8,128)(2,1)} %get-tuple-element.19), calls=%async_computation | async-start | bytes 1835008 | tf_op jit(solution)/shard_map/all_to_all | solution.py:640
  15.3 0.4 collective-permute-done.got_ref.own_got_ref
  15.7 3.6 %sum_far.1.refs_0_ = bf16[384,1024]{1,0:T(8,128)(2,1)} custom-call(bf16[768,256]{1,0:T(8,128)(2,1)} %cot_ref.5, bf16[768,8192]{1,0:T(8,128)(2,1)} %act_ref.5, f32[3,256,1024]{2,1,0:T(8,128)} %collective-permute-done.got_ref.own_got_ref, f32[3,256,1024]{2,1,0:T(8,128)} %collective-permute-done.got_ref.own_got_ref), custom_call_target="tpu_custom_call" | custom-call | bytes 4194304 | tf_op jit(solution)/shard_map/sum_far/pallas_call | solution.py:526
  19.3 2.9 %collective-permute-start.5 = (bf16[384,1024]{1,0:T(8,128)(2,1)}, bf16[384,1024]{1,0:T(8,128)(2,1)S(1)}, u32[]{:S(2)}, u32[]{:S(2)}) collective-permute-start(bf16[384,1024]{1,0:T(8,128)(2,1)} %sum_far.1.refs_0_), channel_id=1, source_target_pairs={{0,8},{4,20},{8,0},{12,28},{16,24},{20,4},{24,16},{28,12},{1,9},{5... | collective-permute-start | bytes 2359304 | tf_op jit(solution)/shard_map/ppermute | solution.py:634
  22.3 0.0 collective-permute-done.1.own_got_ref
  22.3 6.2 %sum_near.1 = (bf16[384,1024]{1,0:T(8,128)(2,1)}, f32[256,1024]{1,0:T(8,128)}, f32[256,1024]{1,0:T(8,128)}) custom-call(bf16[768,256]{1,0:T(8,128)(2,1)} %cot_ref.5, bf16[768,8192]{1,0:T(8,128)(2,1)} %act_ref.5, f32[3,256,1024]{2,1,0:T(8,128)} %collective-permute-done.got_ref.own_got_ref, f32[1,256,1024]{2,1,0:T(8,128)} %collective-permute-done.1.own_got_ref, ...), custom_call_target="tpu_custom_call" | custom-call | bytes 12582912 | tf_op jit(solution)/shard_map/sum_near/pallas_call | solution.py:526
  28.4 0.0 copy-start
  28.4 0.1 collective-permute-start.2
  28.5 0.9 %all-to-all-done.rows_ref = bf16[8,7,32,256]{3,2,1,0:T(8,128)(2,1)S(1)} async-done(((bf16[8,7,32,256]{3,2,1,0:T(8,128)(2,1)}), bf16[8,7,32,256]{3,2,1,0:T(8,128)(2,1)S(1)}, u32[]{:S(2)}, u32[]{:S(2)}) %all-to-all-start) | async-done | bytes 917536 | tf_op jit(solution)/shard_map/all_to_all | solution.py:640
  29.4 6.0 %invert_blocks.1 = (bf16[3,208,256]{2,1,0:T(8,128)(2,1)S(1)}, bf16[208,256]{1,0:T(8,128)(2,1)S(1)}, bf16[8,32,256]{2,1,0:T(8,128)(2,1)S(1)}) custom-call(bf16[8,7,32,256]{3,2,1,0:T(8,128)(2,1)S(1)} %all-to-all-done.rows_ref), custom_call_target="tpu_custom_call" | custom-call | flops 7247757312 | bytes 2097152 | tf_op jit(solution)/shard_map/invert_blocks/pallas_call | solution.py:551
  35.4 0.0 copy-start.1
  35.5 1.6 %collective-permute-start.3 = (bf16[3,208,256]{2,1,0:T(8,128)(2,1)S(1)}, bf16[3,208,256]{2,1,0:T(8,128)(2,1)S(1)}, u32[]{:S(2)}, u32[]{:S(2)}) collective-permute-start(bf16[3,208,256]{2,1,0:T(8,128)(2,1)S(1)} %get-tuple-element.20._.here), channel_id=1, source_target_pairs={{0,1},{1,0},{2,3},{3,2},{4,5},{5,4},{6,7},{7,6},{8,9},{9,8},{10,11... | collective-permute-start | bytes 958472 | tf_op jit(solution)/shard_map/ppermute | solution.py:631
  37.1 0.0 collective-permute-start.4
  37.1 2.6 %collective-permute-start.7 = (bf16[208,256]{1,0:T(8,128)(2,1)S(1)}, bf16[208,256]{1,0:T(8,128)(2,1)S(1)}, u32[]{:S(2)}, u32[]{:S(2)}) collective-permute-start(bf16[208,256]{1,0:T(8,128)(2,1)S(1)} %get-tuple-element.25), channel_id=1, source_target_pairs={{0,2},{1,3},{2,0},{3,1},{4,6},{5,7},{6,4},{7,5},{8,10},{9,11},{10,... | collective-permute-start | bytes 319496 | tf_op jit(solution)/shard_map/ppermute | solution.py:631
  39.7 0.0 collective-permute-done.5.come
  39.7 0.8 %collective-permute-start.8 = (bf16[208,256]{1,0:T(8,128)(2,1)S(1)}, bf16[208,256]{1,0:T(8,128)(2,1)S(1)}, u32[]{:S(2)}, u32[]{:S(2)}) collective-permute-start(bf16[208,256]{1,0:T(8,128)(2,1)S(1)} %get-tuple-element.25), channel_id=1, source_target_pairs={{0,3},{1,2},{2,1},{3,0},{4,7},{5,6},{6,5},{7,4},{8,11},{9,10},{10,... | collective-permute-start | bytes 319496 | tf_op jit(solution)/shard_map/ppermute | solution.py:631
  40.5 0.0 copy-done
  40.5 1.6 %hop.1.__ = bf16[384,1024]{1,0:T(8,128)(2,1)S(1)} custom-call(f32[256,1024]{1,0:T(8,128)S(1)} %copy-done, bf16[384,1024]{1,0:T(8,128)(2,1)S(1)} %collective-permute-done.5.come, bf16[3,208,256]{2,1,0:T(8,128)(2,1)S(1)} %get-tuple-element.20._.here), custom_call_target="tpu_custom_call" | custom-call | tf_op jit(solution)/shard_map/hop/pallas_call | solution.py:577
  42.0 0.0 copy-start.2
  42.1 0.0 collective-permute-done.4.other
  42.1 1.5 %collective-permute-start.6 = (bf16[384,1024]{1,0:T(8,128)(2,1)S(1)}, bf16[384,1024]{1,0:T(8,128)(2,1)S(1)}, u32[]{:S(2)}, u32[]{:S(2)}) collective-permute-start(bf16[384,1024]{1,0:T(8,128)(2,1)S(1)} %hop.1.__), channel_id=1, source_target_pairs={{0,16},{4,12},{8,24},{12,4},{16,0},{20,28},{24,8},{28,20},{1,17},{... | collective-permute-start | bytes 2359304 | tf_op jit(solution)/shard_map/ppermute | solution.py:634
  43.6 2.4 %collective-permute-done.2._.near = bf16[384,1024]{1,0:T(8,128)(2,1)S(1)} collective-permute-done((bf16[384,1024]{1,0:T(8,128)(2,1)}, bf16[384,1024]{1,0:T(8,128)(2,1)S(1)}, u32[]{:S(2)}, u32[]{:S(2)}) %collective-permute-start.2) | collective-permute-done | bytes 786464 | tf_op jit(solution)/shard_map/ppermute | solution.py:634
  46.0 3.6 %invert_group.1._.left = bf16[512,256]{1,0:T(8,128)(2,1)S(1)} custom-call(bf16[8,32,256]{2,1,0:T(8,128)(2,1)S(1)} %get-tuple-element.21.half, bf16[8,32,256]{2,1,0:T(8,128)(2,1)S(1)} %collective-permute-done.4.other, bf16[384,1024]{1,0:T(8,128)(2,1)S(1)} %collective-permute-done.2._.near, bf16[384,1024]{1,0:T(8,128)(2,1)S(1)} %hop.1.__), custom_call_target="tpu_custom_call" | custom-call | tf_op jit(solution)/shard_map/invert_group/pallas_call | solution.py:564
  49.6 0.0 collective-permute-done.3.beside
  49.6 0.0 copy-done.1
  49.7 1.2 %ready.1 = (f32[256,1024]{1,0:T(8,128)S(1)}, bf16[2,4,256,256]{3,2,1,0:T(8,128)(2,1)S(1)}) custom-call(f32[256,1024]{1,0:T(8,128)S(1)} %copy-done.1, bf16[384,1024]{1,0:T(8,128)(2,1)S(1)} %collective-permute-done.2._.near, bf16[3,208,256]{2,1,0:T(8,128)(2,1)S(1)} %get-tuple-element.20._.here, bf16[3,208,256]{2,1,0:T(8,128)(2,1)S(1)} %collective-permute-done.3.beside, ...), custom_call_target="tpu_custom_call" | custom-call | tf_op jit(solution)/shard_map/ready/pallas_call | solution.py:591
  50.9 0.0 collective-permute-done.7.two_off
  50.9 0.0 collective-permute-done.8.three_off
  50.9 0.0 copy-done.2
  50.9 1.9 %owned.1 = (f32[4,256,256]{2,1,0:T(8,128)}, f32[8,128]{1,0:T(8,128)S(1)}) custom-call(s32[32]{0:T(128)S(1)} %copy-done.2, bf16[3,208,256]{2,1,0:T(8,128)(2,1)S(1)} %get-tuple-element.20._.here, bf16[3,208,256]{2,1,0:T(8,128)(2,1)S(1)} %collective-permute-done.3.beside, bf16[208,256]{1,0:T(8,128)(2,1)S(1)} %collective-permute-done.7.two_off, ...), custom_call_target="tpu_custom_call" | custom-call | flops 20000000000 | tf_op jit(solution)/shard_map/owned/pallas_call | solution.py:601
  52.8 1.3 %collective-permute-done.6.come = bf16[384,1024]{1,0:T(8,128)(2,1)S(1)} collective-permute-done((bf16[384,1024]{1,0:T(8,128)(2,1)S(1)}, bf16[384,1024]{1,0:T(8,128)(2,1)S(1)}, u32[]{:S(2)}, u32[]{:S(2)}) %collective-permute-start.6) | collective-permute-done | bytes 786464 | tf_op jit(solution)/shard_map/ppermute | solution.py:634
  54.1 2.3 %finish.1 = f32[1024,256]{1,0:T(8,128)} custom-call(bf16[2,4,256,256]{3,2,1,0:T(8,128)(2,1)S(1)} %get-tuple-element.23.split, bf16[512,256]{1,0:T(8,128)(2,1)S(1)} %invert_group.1._.left, f32[256,1024]{1,0:T(8,128)S(1)} %get-tuple-element.24._.so_far, bf16[384,1024]{1,0:T(8,128)(2,1)S(1)} %collective-permute-done.6.come, f32[8,128]{1,0:T(8,128)S(1)} %get-tuple-element.26._), custom_call_target="tpu_custom_call" | custom-call | bytes 6291456 | tf_op jit(solution)/shard_map/finish/pallas_call | solution.py:614
Async XLA Ops:
  9.5 6.1 %collective-permute-start = (f32[3,256,1024]{2,1,0:T(8,128)}, f32[3,256,1024]{2,1,0:T(8,128)}, u32[]{:S(2)}, u32[]{:S(2)}) collective-permute-start(f32[3,256,1024]{2,1,0:T(8,128)} %get-tuple-element.15), channel_id=1, source_target_pairs={{0,4},{4,0},{8,12},{12,8},{16,20},{20,16},{24,28},{28,24},{1,5},{5... | collective-permute-start | bytes 9437192 | tf_op jit(solution)/shard_map/ppermute | solution.py:631
  10.1 12.2 %collective-permute-start.1 = (f32[1,256,1024]{2,1,0:T(8,128)}, f32[1,256,1024]{2,1,0:T(8,128)}, u32[]{:S(2)}, u32[]{:S(2)}) collective-permute-start(f32[1,256,1024]{2,1,0:T(8,128)} %get-tuple-element.16), channel_id=1, source_target_pairs={{0,4},{4,0},{8,12},{12,8},{16,20},{20,16},{24,28},{28,24},{1,5},{5... | collective-permute-start | bytes 3145736 | tf_op jit(solution)/shard_map/ppermute | solution.py:631
  10.1 19.3 %all-to-all-start = ((bf16[8,7,32,256]{3,2,1,0:T(8,128)(2,1)}), bf16[8,7,32,256]{3,2,1,0:T(8,128)(2,1)S(1)}, u32[]{:S(2)}, u32[]{:S(2)}) async-start(bf16[8,7,32,256]{3,2,1,0:T(8,128)(2,1)} %get-tuple-element.19), calls=%async_computation | async-start | bytes 1835008 | tf_op jit(solution)/shard_map/all_to_all | solution.py:640
  19.3 20.4 %collective-permute-start.5 = (bf16[384,1024]{1,0:T(8,128)(2,1)}, bf16[384,1024]{1,0:T(8,128)(2,1)S(1)}, u32[]{:S(2)}, u32[]{:S(2)}) collective-permute-start(bf16[384,1024]{1,0:T(8,128)(2,1)} %sum_far.1.refs_0_), channel_id=1, source_target_pairs={{0,8},{4,20},{8,0},{12,28},{16,24},{20,4},{24,16},{28,12},{1,9},{5... | collective-permute-start | bytes 2359304 | tf_op jit(solution)/shard_map/ppermute | solution.py:634
  28.4 12.1 %copy-start = (f32[256,1024]{1,0:T(8,128)S(1)}, f32[256,1024]{1,0:T(8,128)}, u32[]{:S(2)}) copy-start(f32[256,1024]{1,0:T(8,128)} %get-tuple-element.22.rest) | copy-start | bytes 3145732
  28.4 17.6 %collective-permute-start.2 = (bf16[384,1024]{1,0:T(8,128)(2,1)}, bf16[384,1024]{1,0:T(8,128)(2,1)S(1)}, u32[]{:S(2)}, u32[]{:S(2)}) collective-permute-start(bf16[384,1024]{1,0:T(8,128)(2,1)} %get-tuple-element.18), channel_id=1, source_target_pairs={{0,8},{4,20},{8,0},{12,28},{16,24},{20,4},{24,16},{28,12},{1,9},{5... | collective-permute-start | bytes 2359304 | tf_op jit(solution)/shard_map/ppermute | solution.py:634
  35.4 14.2 %copy-start.1 = (f32[256,1024]{1,0:T(8,128)S(1)}, f32[256,1024]{1,0:T(8,128)}, u32[]{:S(2)}) copy-start(f32[256,1024]{1,0:T(8,128)} %get-tuple-element.17.own) | copy-start | bytes 3145732
  35.5 14.2 %collective-permute-start.3 = (bf16[3,208,256]{2,1,0:T(8,128)(2,1)S(1)}, bf16[3,208,256]{2,1,0:T(8,128)(2,1)S(1)}, u32[]{:S(2)}, u32[]{:S(2)}) collective-permute-start(bf16[3,208,256]{2,1,0:T(8,128)(2,1)S(1)} %get-tuple-element.20._.here), channel_id=1, source_target_pairs={{0,1},{1,0},{2,3},{3,2},{4,5},{5,4},{6,7},{7,6},{8,9},{9,8},{10,11... | collective-permute-start | bytes 958472 | tf_op jit(solution)/shard_map/ppermute | solution.py:631
  37.1 5.0 %collective-permute-start.4 = (bf16[8,32,256]{2,1,0:T(8,128)(2,1)S(1)}, bf16[8,32,256]{2,1,0:T(8,128)(2,1)S(1)}, u32[]{:S(2)}, u32[]{:S(2)}) collective-permute-start(bf16[8,32,256]{2,1,0:T(8,128)(2,1)S(1)} %get-tuple-element.21.half), channel_id=1, source_target_pairs={{0,4},{4,0},{8,12},{12,8},{16,20},{20,16},{24,28},{28,24},{1,5},{5... | collective-permute-start | bytes 393224 | tf_op jit(solution)/shard_map/ppermute | solution.py:631
  37.1 13.8 %collective-permute-start.7 = (bf16[208,256]{1,0:T(8,128)(2,1)S(1)}, bf16[208,256]{1,0:T(8,128)(2,1)S(1)}, u32[]{:S(2)}, u32[]{:S(2)}) collective-permute-start(bf16[208,256]{1,0:T(8,128)(2,1)S(1)} %get-tuple-element.25), channel_id=1, source_target_pairs={{0,2},{1,3},{2,0},{3,1},{4,6},{5,7},{6,4},{7,5},{8,10},{9,11},{10,... | collective-permute-start | bytes 319496 | tf_op jit(solution)/shard_map/ppermute | solution.py:631
  39.7 11.2 %collective-permute-start.8 = (bf16[208,256]{1,0:T(8,128)(2,1)S(1)}, bf16[208,256]{1,0:T(8,128)(2,1)S(1)}, u32[]{:S(2)}, u32[]{:S(2)}) collective-permute-start(bf16[208,256]{1,0:T(8,128)(2,1)S(1)} %get-tuple-element.25), channel_id=1, source_target_pairs={{0,3},{1,2},{2,1},{3,0},{4,7},{5,6},{6,5},{7,4},{8,11},{9,10},{10,... | collective-permute-start | bytes 319496 | tf_op jit(solution)/shard_map/ppermute | solution.py:631
  42.0 8.9 %copy-start.2 = (s32[32]{0:T(128)S(1)}, s32[32]{0:T(128)}, u32[]{:S(2)}) copy-start(s32[32]{0:T(128)} %owner.3) | copy-start | bytes 388
  42.1 12.1 %collective-permute-start.6 = (bf16[384,1024]{1,0:T(8,128)(2,1)S(1)}, bf16[384,1024]{1,0:T(8,128)(2,1)S(1)}, u32[]{:S(2)}, u32[]{:S(2)}) collective-permute-start(bf16[384,1024]{1,0:T(8,128)(2,1)S(1)} %hop.1.__), channel_id=1, source_target_pairs={{0,16},{4,12},{8,24},{12,4},{16,0},{20,28},{24,8},{28,20},{1,17},{... | collective-permute-start | bytes 2359304 | tf_op jit(solution)/shard_map/ppermute | solution.py:634

commit v9 on v8

--- a/solution.py
+++ b/solution.py
@@ -134,7 +134,7 @@
 SUM_MIB = 62
 AHEAD = 3
 PROJECT_AHEAD = 6
-HOP_PARTS = 2
+HOP_PARTS = 1
 SUM_PARTS = 2
 OWNED_FLOPS = 20_000_000_000
 ANY = pl.BlockSpec(memory_space=pl.ANY)
@@ -185,7 +185,7 @@
     into[:rows] = high
     base = high.astype(f32)
     left = (x - base) * pl.reciprocal(base, approx=True) * 256.0
-    left = jnp.where(jnp.abs(base) < 1e-30, 0.0, jnp.clip(left, -1.0, 1.0))
+    left = jnp.where(jnp.abs(base) < 1e-35, 0.0, jnp.clip(left, -1.0, 1.0))
     digit = jnp.floor(left * 63.5 + 64.0)
     first, second = digit[: rows // 2], digit[rows // 2 :]
     negative = second >= 64.0

time: 56.9 us -> 56.8 us (level)
  transfers between devices with their start and end apart: 10 -> 10, of which waited for: 4 -> 4; matrix products, arithmetic and copies ran while one was open for 0% -> 0% of each run, Pallas kernels for 43% -> 42%
where the time goes in v9:
time: 56.8 us; the launch traced here: 56.5 us
  Pallas kernels  35.2 us (62%)
  starting transfers between devices  15.3 us (27%)
  waiting for transfers between devices  5.07 us (9%)
  between operations  0.94 us (2%)
    pallas_call x2, Pallas kernels, sum_cores(): call(functools.partial(sum_body, which), name, tuple((shaped(wired, bf16)...  9.77 us
    pallas_call x1, Pallas kernels, project(): call(project_body, 'project', (rest, one, shaped((count, 7, samples // 2,...  8.91 us
    pallas_call x1, Pallas kernels, invert(): call(functools.partial(invert_body, scale), 'invert_blocks', (shaped((3,...  6.03 us
    ppermute x6, starting transfers between devices, swap(): return lax.ppermute(block, axis, [(i, i ^ bit) for i in range(count)])  5.6 us
    all_to_all x1, starting transfers between devices, square_device(): rows = lax.all_to_all(picked, 'dp', split_axis=0, concat_axis=0, tiled=True)  5.15 us
    ppermute x3, starting transfers between devices, travel(): lax.ppermute(block, 'dp', [(i, i ^ (odd if i % 2 else even)) for i in ran...  4.55 us
    ppermute x3, waiting for transfers between devices, travel(): lax.ppermute(block, 'dp', [(i, i ^ (odd if i % 2 else even)) for i in ran...  3.77 us
    pallas_call x1, Pallas kernels, invert_group(): call(functools.partial(group_body, scale), 'invert_group', shaped((2 * FA...  3.58 us
  transfers between devices with their start and end apart: 10, of which 4 were waited for; matrix products, arithmetic and copies ran while one was open for 0% of the time, Pallas kernels for 42%

profile of v9, /device:TPU:0, one launch (start us, length us, event | category | flops | bytes accessed | tf_op | source)
XLA Modules:
  0.0 56.5 jit_solution(7808529065837540227)
XLA Ops:
  0.6 8.9 %project.1 = (f32[3,256,1024]{2,1,0:T(8,128)}, f32[1,256,1024]{2,1,0:T(8,128)}, bf16[8,7,32,256]{3,2,1,0:T(8,128)(2,1)}) custom-call(s32[32]{0:T(128)} %owner.3, s32[1,64]{1,0:T(1,128)} %bitcast.1, bf16[768,256]{1,0:T(8,128)(2,1)} %cot_ref.5, bf16[768,8192]{1,0:T(8,128)(2,1)} %act_ref.5), custom_call_target="tpu_custom_call" | custom-call | flops 4026531840 | bytes 16777216 | tf_op jit(solution)/shard_map/project/pallas_call | solution.py:289
  9.5 0.5 collective-permute-start
  10.1 0.1 collective-permute-start.1
  10.1 5.1 %all-to-all-start = ((bf16[8,7,32,256]{3,2,1,0:T(8,128)(2,1)}), bf16[8,7,32,256]{3,2,1,0:T(8,128)(2,1)S(1)}, u32[]{:S(2)}, u32[]{:S(2)}) async-start(bf16[8,7,32,256]{3,2,1,0:T(8,128)(2,1)} %get-tuple-element.19), calls=%async_computation | async-start | bytes 1835008 | tf_op jit(solution)/shard_map/all_to_all | solution.py:640
  15.3 0.4 collective-permute-done.got_ref.own_got_ref
  15.7 3.6 %sum_far.1.refs_0_ = bf16[384,1024]{1,0:T(8,128)(2,1)} custom-call(bf16[768,256]{1,0:T(8,128)(2,1)} %cot_ref.5, bf16[768,8192]{1,0:T(8,128)(2,1)} %act_ref.5, f32[3,256,1024]{2,1,0:T(8,128)} %collective-permute-done.got_ref.own_got_ref, f32[3,256,1024]{2,1,0:T(8,128)} %collective-permute-done.got_ref.own_got_ref), custom_call_target="tpu_custom_call" | custom-call | bytes 4194304 | tf_op jit(solution)/shard_map/sum_far/pallas_call | solution.py:526
  19.3 2.9 %collective-permute-start.5 = (bf16[384,1024]{1,0:T(8,128)(2,1)}, bf16[384,1024]{1,0:T(8,128)(2,1)S(1)}, u32[]{:S(2)}, u32[]{:S(2)}) collective-permute-start(bf16[384,1024]{1,0:T(8,128)(2,1)} %sum_far.1.refs_0_), channel_id=1, source_target_pairs={{0,8},{4,20},{8,0},{12,28},{16,24},{20,4},{24,16},{28,12},{1,9},{5... | collective-permute-start | bytes 2359304 | tf_op jit(solution)/shard_map/ppermute | solution.py:634
  22.3 0.0 collective-permute-done.1.own_got_ref
  22.3 6.2 %sum_near.1 = (bf16[384,1024]{1,0:T(8,128)(2,1)}, f32[256,1024]{1,0:T(8,128)}, f32[256,1024]{1,0:T(8,128)}) custom-call(bf16[768,256]{1,0:T(8,128)(2,1)} %cot_ref.5, bf16[768,8192]{1,0:T(8,128)(2,1)} %act_ref.5, f32[3,256,1024]{2,1,0:T(8,128)} %collective-permute-done.got_ref.own_got_ref, f32[1,256,1024]{2,1,0:T(8,128)} %collective-permute-done.1.own_got_ref, ...), custom_call_target="tpu_custom_call" | custom-call | bytes 12582912 | tf_op jit(solution)/shard_map/sum_near/pallas_call | solution.py:526
  28.4 0.0 copy-start
  28.4 0.1 collective-permute-start.2
  28.5 0.9 %all-to-all-done.rows_ref = bf16[8,7,32,256]{3,2,1,0:T(8,128)(2,1)S(1)} async-done(((bf16[8,7,32,256]{3,2,1,0:T(8,128)(2,1)}), bf16[8,7,32,256]{3,2,1,0:T(8,128)(2,1)S(1)}, u32[]{:S(2)}, u32[]{:S(2)}) %all-to-all-start) | async-done | bytes 917536 | tf_op jit(solution)/shard_map/all_to_all | solution.py:640
  29.4 6.0 %invert_blocks.1 = (bf16[3,208,256]{2,1,0:T(8,128)(2,1)S(1)}, bf16[208,256]{1,0:T(8,128)(2,1)S(1)}, bf16[8,32,256]{2,1,0:T(8,128)(2,1)S(1)}) custom-call(bf16[8,7,32,256]{3,2,1,0:T(8,128)(2,1)S(1)} %all-to-all-done.rows_ref), custom_call_target="tpu_custom_call" | custom-call | flops 7247757312 | bytes 2097152 | tf_op jit(solution)/shard_map/invert_blocks/pallas_call | solution.py:551
  35.4 0.0 copy-start.1
  35.5 1.6 %collective-permute-start.3 = (bf16[3,208,256]{2,1,0:T(8,128)(2,1)S(1)}, bf16[3,208,256]{2,1,0:T(8,128)(2,1)S(1)}, u32[]{:S(2)}, u32[]{:S(2)}) collective-permute-start(bf16[3,208,256]{2,1,0:T(8,128)(2,1)S(1)} %get-tuple-element.20._.here), channel_id=1, source_target_pairs={{0,1},{1,0},{2,3},{3,2},{4,5},{5,4},{6,7},{7,6},{8,9},{9,8},{10,11... | collective-permute-start | bytes 958472 | tf_op jit(solution)/shard_map/ppermute | solution.py:631
  37.1 0.0 collective-permute-start.4
  37.1 2.6 %collective-permute-start.7 = (bf16[208,256]{1,0:T(8,128)(2,1)S(1)}, bf16[208,256]{1,0:T(8,128)(2,1)S(1)}, u32[]{:S(2)}, u32[]{:S(2)}) collective-permute-start(bf16[208,256]{1,0:T(8,128)(2,1)S(1)} %get-tuple-element.25), channel_id=1, source_target_pairs={{0,2},{1,3},{2,0},{3,1},{4,6},{5,7},{6,4},{7,5},{8,10},{9,11},{10,... | collective-permute-start | bytes 319496 | tf_op jit(solution)/shard_map/ppermute | solution.py:631
  39.7 0.0 collective-permute-done.5.come
  39.7 0.8 %collective-permute-start.8 = (bf16[208,256]{1,0:T(8,128)(2,1)S(1)}, bf16[208,256]{1,0:T(8,128)(2,1)S(1)}, u32[]{:S(2)}, u32[]{:S(2)}) collective-permute-start(bf16[208,256]{1,0:T(8,128)(2,1)S(1)} %get-tuple-element.25), channel_id=1, source_target_pairs={{0,3},{1,2},{2,1},{3,0},{4,7},{5,6},{6,5},{7,4},{8,11},{9,10},{10,... | collective-permute-start | bytes 319496 | tf_op jit(solution)/shard_map/ppermute | solution.py:631
  40.5 0.0 copy-done
  40.5 1.5 %hop.1.__ = bf16[384,1024]{1,0:T(8,128)(2,1)S(1)} custom-call(f32[256,1024]{1,0:T(8,128)S(1)} %copy-done, bf16[384,1024]{1,0:T(8,128)(2,1)S(1)} %collective-permute-done.5.come, bf16[3,208,256]{2,1,0:T(8,128)(2,1)S(1)} %get-tuple-element.20._.here), custom_call_target="tpu_custom_call" | custom-call | tf_op jit(solution)/shard_map/hop/pallas_call | solution.py:577
  42.0 0.0 copy-start.2
  42.0 0.0 collective-permute-done.4.other
  42.0 1.5 %collective-permute-start.6 = (bf16[384,1024]{1,0:T(8,128)(2,1)S(1)}, bf16[384,1024]{1,0:T(8,128)(2,1)S(1)}, u32[]{:S(2)}, u32[]{:S(2)}) collective-permute-start(bf16[384,1024]{1,0:T(8,128)(2,1)S(1)} %hop.1.__), channel_id=1, source_target_pairs={{0,16},{4,12},{8,24},{12,4},{16,0},{20,28},{24,8},{28,20},{1,17},{... | collective-permute-start | bytes 2359304 | tf_op jit(solution)/shard_map/ppermute | solution.py:634
  43.5 2.6 %collective-permute-done.2._.near = bf16[384,1024]{1,0:T(8,128)(2,1)S(1)} collective-permute-done((bf16[384,1024]{1,0:T(8,128)(2,1)}, bf16[384,1024]{1,0:T(8,128)(2,1)S(1)}, u32[]{:S(2)}, u32[]{:S(2)}) %collective-permute-start.2) | collective-permute-done | bytes 786464 | tf_op jit(solution)/shard_map/ppermute | solution.py:634
  46.1 3.6 %invert_group.1._.left = bf16[512,256]{1,0:T(8,128)(2,1)S(1)} custom-call(bf16[8,32,256]{2,1,0:T(8,128)(2,1)S(1)} %get-tuple-element.21.half, bf16[8,32,256]{2,1,0:T(8,128)(2,1)S(1)} %collective-permute-done.4.other, bf16[384,1024]{1,0:T(8,128)(2,1)S(1)} %collective-permute-done.2._.near, bf16[384,1024]{1,0:T(8,128)(2,1)S(1)} %hop.1.__), custom_call_target="tpu_custom_call" | custom-call | tf_op jit(solution)/shard_map/invert_group/pallas_call | solution.py:564
  49.7 0.0 collective-permute-done.3.beside
  49.7 0.0 copy-done.1
  49.7 1.2 %ready.1 = (f32[256,1024]{1,0:T(8,128)S(1)}, bf16[2,4,256,256]{3,2,1,0:T(8,128)(2,1)S(1)}) custom-call(f32[256,1024]{1,0:T(8,128)S(1)} %copy-done.1, bf16[384,1024]{1,0:T(8,128)(2,1)S(1)} %collective-permute-done.2._.near, bf16[3,208,256]{2,1,0:T(8,128)(2,1)S(1)} %get-tuple-element.20._.here, bf16[3,208,256]{2,1,0:T(8,128)(2,1)S(1)} %collective-permute-done.3.beside, ...), custom_call_target="tpu_custom_call" | custom-call | tf_op jit(solution)/shard_map/ready/pallas_call | solution.py:591
  50.9 0.0 collective-permute-done.7.two_off
  51.0 0.0 collective-permute-done.8.three_off
  51.0 0.0 copy-done.2
  51.0 1.9 %owned.1 = (f32[4,256,256]{2,1,0:T(8,128)}, f32[8,128]{1,0:T(8,128)S(1)}) custom-call(s32[32]{0:T(128)S(1)} %copy-done.2, bf16[3,208,256]{2,1,0:T(8,128)(2,1)S(1)} %get-tuple-element.20._.here, bf16[3,208,256]{2,1,0:T(8,128)(2,1)S(1)} %collective-permute-done.3.beside, bf16[208,256]{1,0:T(8,128)(2,1)S(1)} %collective-permute-done.7.two_off, ...), custom_call_target="tpu_custom_call" | custom-call | flops 20000000000 | tf_op jit(solution)/shard_map/owned/pallas_call | solution.py:601
  52.9 1.2 %collective-permute-done.6.come = bf16[384,1024]{1,0:T(8,128)(2,1)S(1)} collective-permute-done((bf16[384,1024]{1,0:T(8,128)(2,1)S(1)}, bf16[384,1024]{1,0:T(8,128)(2,1)S(1)}, u32[]{:S(2)}, u32[]{:S(2)}) %collective-permute-start.6) | collective-permute-done | bytes 786464 | tf_op jit(solution)/shard_map/ppermute | solution.py:634
  54.1 2.3 %finish.1 = f32[1024,256]{1,0:T(8,128)} custom-call(bf16[2,4,256,256]{3,2,1,0:T(8,128)(2,1)S(1)} %get-tuple-element.23.split, bf16[512,256]{1,0:T(8,128)(2,1)S(1)} %invert_group.1._.left, f32[256,1024]{1,0:T(8,128)S(1)} %get-tuple-element.24._.so_far, bf16[384,1024]{1,0:T(8,128)(2,1)S(1)} %collective-permute-done.6.come, f32[8,128]{1,0:T(8,128)S(1)} %get-tuple-element.26._), custom_call_target="tpu_custom_call" | custom-call | bytes 6291456 | tf_op jit(solution)/shard_map/finish/pallas_call | solution.py:614
Async XLA Ops:
  9.5 6.1 %collective-permute-start = (f32[3,256,1024]{2,1,0:T(8,128)}, f32[3,256,1024]{2,1,0:T(8,128)}, u32[]{:S(2)}, u32[]{:S(2)}) collective-permute-start(f32[3,256,1024]{2,1,0:T(8,128)} %get-tuple-element.15), channel_id=1, source_target_pairs={{0,4},{4,0},{8,12},{12,8},{16,20},{20,16},{24,28},{28,24},{1,5},{5... | collective-permute-start | bytes 9437192 | tf_op jit(solution)/shard_map/ppermute | solution.py:631
  10.1 12.2 %collective-permute-start.1 = (f32[1,256,1024]{2,1,0:T(8,128)}, f32[1,256,1024]{2,1,0:T(8,128)}, u32[]{:S(2)}, u32[]{:S(2)}) collective-permute-start(f32[1,256,1024]{2,1,0:T(8,128)} %get-tuple-element.16), channel_id=1, source_target_pairs={{0,4},{4,0},{8,12},{12,8},{16,20},{20,16},{24,28},{28,24},{1,5},{5... | collective-permute-start | bytes 3145736 | tf_op jit(solution)/shard_map/ppermute | solution.py:631
  10.1 19.3 %all-to-all-start = ((bf16[8,7,32,256]{3,2,1,0:T(8,128)(2,1)}), bf16[8,7,32,256]{3,2,1,0:T(8,128)(2,1)S(1)}, u32[]{:S(2)}, u32[]{:S(2)}) async-start(bf16[8,7,32,256]{3,2,1,0:T(8,128)(2,1)} %get-tuple-element.19), calls=%async_computation | async-start | bytes 1835008 | tf_op jit(solution)/shard_map/all_to_all | solution.py:640
  19.3 20.4 %collective-permute-start.5 = (bf16[384,1024]{1,0:T(8,128)(2,1)}, bf16[384,1024]{1,0:T(8,128)(2,1)S(1)}, u32[]{:S(2)}, u32[]{:S(2)}) collective-permute-start(bf16[384,1024]{1,0:T(8,128)(2,1)} %sum_far.1.refs_0_), channel_id=1, source_target_pairs={{0,8},{4,20},{8,0},{12,28},{16,24},{20,4},{24,16},{28,12},{1,9},{5... | collective-permute-start | bytes 2359304 | tf_op jit(solution)/shard_map/ppermute | solution.py:634
  28.4 12.1 %copy-start = (f32[256,1024]{1,0:T(8,128)S(1)}, f32[256,1024]{1,0:T(8,128)}, u32[]{:S(2)}) copy-start(f32[256,1024]{1,0:T(8,128)} %get-tuple-element.22.rest) | copy-start | bytes 3145732
  28.4 17.7 %collective-permute-start.2 = (bf16[384,1024]{1,0:T(8,128)(2,1)}, bf16[384,1024]{1,0:T(8,128)(2,1)S(1)}, u32[]{:S(2)}, u32[]{:S(2)}) collective-permute-start(bf16[384,1024]{1,0:T(8,128)(2,1)} %get-tuple-element.18), channel_id=1, source_target_pairs={{0,8},{4,20},{8,0},{12,28},{16,24},{20,4},{24,16},{28,12},{1,9},{5... | collective-permute-start | bytes 2359304 | tf_op jit(solution)/shard_map/ppermute | solution.py:634
  35.4 14.3 %copy-start.1 = (f32[256,1024]{1,0:T(8,128)S(1)}, f32[256,1024]{1,0:T(8,128)}, u32[]{:S(2)}) copy-start(f32[256,1024]{1,0:T(8,128)} %get-tuple-element.17.own) | copy-start | bytes 3145732
  35.5 14.2 %collective-permute-start.3 = (bf16[3,208,256]{2,1,0:T(8,128)(2,1)S(1)}, bf16[3,208,256]{2,1,0:T(8,128)(2,1)S(1)}, u32[]{:S(2)}, u32[]{:S(2)}) collective-permute-start(bf16[3,208,256]{2,1,0:T(8,128)(2,1)S(1)} %get-tuple-element.20._.here), channel_id=1, source_target_pairs={{0,1},{1,0},{2,3},{3,2},{4,5},{5,4},{6,7},{7,6},{8,9},{9,8},{10,11... | collective-permute-start | bytes 958472 | tf_op jit(solution)/shard_map/ppermute | solution.py:631
  37.1 4.9 %collective-permute-start.4 = (bf16[8,32,256]{2,1,0:T(8,128)(2,1)S(1)}, bf16[8,32,256]{2,1,0:T(8,128)(2,1)S(1)}, u32[]{:S(2)}, u32[]{:S(2)}) collective-permute-start(bf16[8,32,256]{2,1,0:T(8,128)(2,1)S(1)} %get-tuple-element.21.half), channel_id=1, source_target_pairs={{0,4},{4,0},{8,12},{12,8},{16,20},{20,16},{24,28},{28,24},{1,5},{5... | collective-permute-start | bytes 393224 | tf_op jit(solution)/shard_map/ppermute | solution.py:631
  37.1 13.8 %collective-permute-start.7 = (bf16[208,256]{1,0:T(8,128)(2,1)S(1)}, bf16[208,256]{1,0:T(8,128)(2,1)S(1)}, u32[]{:S(2)}, u32[]{:S(2)}) collective-permute-start(bf16[208,256]{1,0:T(8,128)(2,1)S(1)} %get-tuple-element.25), channel_id=1, source_target_pairs={{0,2},{1,3},{2,0},{3,1},{4,6},{5,7},{6,4},{7,5},{8,10},{9,11},{10,... | collective-permute-start | bytes 319496 | tf_op jit(solution)/shard_map/ppermute | solution.py:631
  39.7 11.3 %collective-permute-start.8 = (bf16[208,256]{1,0:T(8,128)(2,1)S(1)}, bf16[208,256]{1,0:T(8,128)(2,1)S(1)}, u32[]{:S(2)}, u32[]{:S(2)}) collective-permute-start(bf16[208,256]{1,0:T(8,128)(2,1)S(1)} %get-tuple-element.25), channel_id=1, source_target_pairs={{0,3},{1,2},{2,1},{3,0},{4,7},{5,6},{6,5},{7,4},{8,11},{9,10},{10,... | collective-permute-start | bytes 319496 | tf_op jit(solution)/shard_map/ppermute | solution.py:631
  42.0 9.0 %copy-start.2 = (s32[32]{0:T(128)S(1)}, s32[32]{0:T(128)}, u32[]{:S(2)}) copy-start(s32[32]{0:T(128)} %owner.3) | copy-start | bytes 388
  42.0 12.1 %collective-permute-start.6 = (bf16[384,1024]{1,0:T(8,128)(2,1)S(1)}, bf16[384,1024]{1,0:T(8,128)(2,1)S(1)}, u32[]{:S(2)}, u32[]{:S(2)}) collective-permute-start(bf16[384,1024]{1,0:T(8,128)(2,1)S(1)} %hop.1.__), channel_id=1, source_target_pairs={{0,16},{4,12},{8,24},{12,4},{16,0},{20,28},{24,8},{28,20},{1,17},{... | collective-permute-start | bytes 2359304 | tf_op jit(solution)/shard_map/ppermute | solution.py:634

commit v10 on v9

--- a/solution.py
+++ b/solution.py
@@ -129,7 +129,7 @@
 
 
 MIB = 1 << 20
-VMEM_MIB = 32
+VMEM_MIB = 24
 PROJECT_MIB = 64
 SUM_MIB = 62
 AHEAD = 3

time: 56.8 us -> 56.8 us (level)
  no operation moved by 1% of the time
where the time goes in v10:
time: 56.8 us; the launch traced here: 56.5 us
  Pallas kernels  35.2 us (62%)
  starting transfers between devices  15.3 us (27%)
  waiting for transfers between devices  5.07 us (9%)
  between operations  0.94 us (2%)
    pallas_call x2, Pallas kernels, sum_cores(): call(functools.partial(sum_body, which), name, tuple((shaped(wired, bf16)...  9.77 us
    pallas_call x1, Pallas kernels, project(): call(project_body, 'project', (rest, one, shaped((count, 7, samples // 2,...  8.91 us
    pallas_call x1, Pallas kernels, invert(): call(functools.partial(invert_body, scale), 'invert_blocks', (shaped((3,...  6.03 us
    ppermute x6, starting transfers between devices, swap(): return lax.ppermute(block, axis, [(i, i ^ bit) for i in range(count)])  5.6 us
    all_to_all x1, starting transfers between devices, square_device(): rows = lax.all_to_all(picked, 'dp', split_axis=0, concat_axis=0, tiled=True)  5.15 us
    ppermute x3, starting transfers between devices, travel(): lax.ppermute(block, 'dp', [(i, i ^ (odd if i % 2 else even)) for i in ran...  4.55 us
    ppermute x3, waiting for transfers between devices, travel(): lax.ppermute(block, 'dp', [(i, i ^ (odd if i % 2 else even)) for i in ran...  3.77 us
    pallas_call x1, Pallas kernels, invert_group(): call(functools.partial(group_body, scale), 'invert_group', shaped((2 * FA...  3.58 us
  transfers between devices with their start and end apart: 10, of which 4 were waited for; matrix products, arithmetic and copies ran while one was open for 0% of the time, Pallas kernels for 42%

profile of v10, /device:TPU:0, one launch (start us, length us, event | category | flops | bytes accessed | tf_op | source)
XLA Modules:
  0.0 56.5 jit_solution(18305996254641767339)
XLA Ops:
  0.6 8.9 %project.1 = (f32[3,256,1024]{2,1,0:T(8,128)}, f32[1,256,1024]{2,1,0:T(8,128)}, bf16[8,7,32,256]{3,2,1,0:T(8,128)(2,1)}) custom-call(s32[32]{0:T(128)} %owner.3, s32[1,64]{1,0:T(1,128)} %bitcast.1, bf16[768,256]{1,0:T(8,128)(2,1)} %cot_ref.5, bf16[768,8192]{1,0:T(8,128)(2,1)} %act_ref.5), custom_call_target="tpu_custom_call" | custom-call | flops 4026531840 | bytes 16777216 | tf_op jit(solution)/shard_map/project/pallas_call | solution.py:289
  9.5 0.5 collective-permute-start
  10.1 0.1 collective-permute-start.1
  10.1 5.1 %all-to-all-start = ((bf16[8,7,32,256]{3,2,1,0:T(8,128)(2,1)}), bf16[8,7,32,256]{3,2,1,0:T(8,128)(2,1)S(1)}, u32[]{:S(2)}, u32[]{:S(2)}) async-start(bf16[8,7,32,256]{3,2,1,0:T(8,128)(2,1)} %get-tuple-element.19), calls=%async_computation | async-start | bytes 1835008 | tf_op jit(solution)/shard_map/all_to_all | solution.py:640
  15.3 0.4 collective-permute-done.got_ref.own_got_ref
  15.7 3.6 %sum_far.1.refs_0_ = bf16[384,1024]{1,0:T(8,128)(2,1)} custom-call(bf16[768,256]{1,0:T(8,128)(2,1)} %cot_ref.5, bf16[768,8192]{1,0:T(8,128)(2,1)} %act_ref.5, f32[3,256,1024]{2,1,0:T(8,128)} %collective-permute-done.got_ref.own_got_ref, f32[3,256,1024]{2,1,0:T(8,128)} %collective-permute-done.got_ref.own_got_ref), custom_call_target="tpu_custom_call" | custom-call | bytes 4194304 | tf_op jit(solution)/shard_map/sum_far/pallas_call | solution.py:526
  19.3 2.9 %collective-permute-start.5 = (bf16[384,1024]{1,0:T(8,128)(2,1)}, bf16[384,1024]{1,0:T(8,128)(2,1)S(1)}, u32[]{:S(2)}, u32[]{:S(2)}) collective-permute-start(bf16[384,1024]{1,0:T(8,128)(2,1)} %sum_far.1.refs_0_), channel_id=1, source_target_pairs={{0,8},{4,20},{8,0},{12,28},{16,24},{20,4},{24,16},{28,12},{1,9},{5... | collective-permute-start | bytes 2359304 | tf_op jit(solution)/shard_map/ppermute | solution.py:634
  22.3 0.0 collective-permute-done.1.own_got_ref
  22.3 6.2 %sum_near.1 = (bf16[384,1024]{1,0:T(8,128)(2,1)}, f32[256,1024]{1,0:T(8,128)}, f32[256,1024]{1,0:T(8,128)}) custom-call(bf16[768,256]{1,0:T(8,128)(2,1)} %cot_ref.5, bf16[768,8192]{1,0:T(8,128)(2,1)} %act_ref.5, f32[3,256,1024]{2,1,0:T(8,128)} %collective-permute-done.got_ref.own_got_ref, f32[1,256,1024]{2,1,0:T(8,128)} %collective-permute-done.1.own_got_ref, ...), custom_call_target="tpu_custom_call" | custom-call | bytes 12582912 | tf_op jit(solution)/shard_map/sum_near/pallas_call | solution.py:526
  28.4 0.0 copy-start
  28.4 0.1 collective-permute-start.2
  28.5 0.9 %all-to-all-done.rows_ref = bf16[8,7,32,256]{3,2,1,0:T(8,128)(2,1)S(1)} async-done(((bf16[8,7,32,256]{3,2,1,0:T(8,128)(2,1)}), bf16[8,7,32,256]{3,2,1,0:T(8,128)(2,1)S(1)}, u32[]{:S(2)}, u32[]{:S(2)}) %all-to-all-start) | async-done | bytes 917536 | tf_op jit(solution)/shard_map/all_to_all | solution.py:640
  29.4 6.0 %invert_blocks.1 = (bf16[3,208,256]{2,1,0:T(8,128)(2,1)S(1)}, bf16[208,256]{1,0:T(8,128)(2,1)S(1)}, bf16[8,32,256]{2,1,0:T(8,128)(2,1)S(1)}) custom-call(bf16[8,7,32,256]{3,2,1,0:T(8,128)(2,1)S(1)} %all-to-all-done.rows_ref), custom_call_target="tpu_custom_call" | custom-call | flops 7247757312 | bytes 2097152 | tf_op jit(solution)/shard_map/invert_blocks/pallas_call | solution.py:551
  35.4 0.0 copy-start.1
  35.5 1.6 %collective-permute-start.3 = (bf16[3,208,256]{2,1,0:T(8,128)(2,1)S(1)}, bf16[3,208,256]{2,1,0:T(8,128)(2,1)S(1)}, u32[]{:S(2)}, u32[]{:S(2)}) collective-permute-start(bf16[3,208,256]{2,1,0:T(8,128)(2,1)S(1)} %get-tuple-element.20._.here), channel_id=1, source_target_pairs={{0,1},{1,0},{2,3},{3,2},{4,5},{5,4},{6,7},{7,6},{8,9},{9,8},{10,11... | collective-permute-start | bytes 958472 | tf_op jit(solution)/shard_map/ppermute | solution.py:631
  37.1 0.0 collective-permute-start.4
  37.1 2.6 %collective-permute-start.7 = (bf16[208,256]{1,0:T(8,128)(2,1)S(1)}, bf16[208,256]{1,0:T(8,128)(2,1)S(1)}, u32[]{:S(2)}, u32[]{:S(2)}) collective-permute-start(bf16[208,256]{1,0:T(8,128)(2,1)S(1)} %get-tuple-element.25), channel_id=1, source_target_pairs={{0,2},{1,3},{2,0},{3,1},{4,6},{5,7},{6,4},{7,5},{8,10},{9,11},{10,... | collective-permute-start | bytes 319496 | tf_op jit(solution)/shard_map/ppermute | solution.py:631
  39.7 0.0 collective-permute-done.5.come
  39.7 0.8 %collective-permute-start.8 = (bf16[208,256]{1,0:T(8,128)(2,1)S(1)}, bf16[208,256]{1,0:T(8,128)(2,1)S(1)}, u32[]{:S(2)}, u32[]{:S(2)}) collective-permute-start(bf16[208,256]{1,0:T(8,128)(2,1)S(1)} %get-tuple-element.25), channel_id=1, source_target_pairs={{0,3},{1,2},{2,1},{3,0},{4,7},{5,6},{6,5},{7,4},{8,11},{9,10},{10,... | collective-permute-start | bytes 319496 | tf_op jit(solution)/shard_map/ppermute | solution.py:631
  40.5 0.0 copy-done
  40.5 1.5 %hop.1.__ = bf16[384,1024]{1,0:T(8,128)(2,1)S(1)} custom-call(f32[256,1024]{1,0:T(8,128)S(1)} %copy-done, bf16[384,1024]{1,0:T(8,128)(2,1)S(1)} %collective-permute-done.5.come, bf16[3,208,256]{2,1,0:T(8,128)(2,1)S(1)} %get-tuple-element.20._.here), custom_call_target="tpu_custom_call" | custom-call | tf_op jit(solution)/shard_map/hop/pallas_call | solution.py:577
  42.0 0.0 copy-start.2
  42.0 0.0 collective-permute-done.4.other
  42.0 1.5 %collective-permute-start.6 = (bf16[384,1024]{1,0:T(8,128)(2,1)S(1)}, bf16[384,1024]{1,0:T(8,128)(2,1)S(1)}, u32[]{:S(2)}, u32[]{:S(2)}) collective-permute-start(bf16[384,1024]{1,0:T(8,128)(2,1)S(1)} %hop.1.__), channel_id=1, source_target_pairs={{0,16},{4,12},{8,24},{12,4},{16,0},{20,28},{24,8},{28,20},{1,17},{... | collective-permute-start | bytes 2359304 | tf_op jit(solution)/shard_map/ppermute | solution.py:634
  43.5 2.6 %collective-permute-done.2._.near = bf16[384,1024]{1,0:T(8,128)(2,1)S(1)} collective-permute-done((bf16[384,1024]{1,0:T(8,128)(2,1)}, bf16[384,1024]{1,0:T(8,128)(2,1)S(1)}, u32[]{:S(2)}, u32[]{:S(2)}) %collective-permute-start.2) | collective-permute-done | bytes 786464 | tf_op jit(solution)/shard_map/ppermute | solution.py:634
  46.1 3.6 %invert_group.1._.left = bf16[512,256]{1,0:T(8,128)(2,1)S(1)} custom-call(bf16[8,32,256]{2,1,0:T(8,128)(2,1)S(1)} %get-tuple-element.21.half, bf16[8,32,256]{2,1,0:T(8,128)(2,1)S(1)} %collective-permute-done.4.other, bf16[384,1024]{1,0:T(8,128)(2,1)S(1)} %collective-permute-done.2._.near, bf16[384,1024]{1,0:T(8,128)(2,1)S(1)} %hop.1.__), custom_call_target="tpu_custom_call" | custom-call | tf_op jit(solution)/shard_map/invert_group/pallas_call | solution.py:564
  49.7 0.0 collective-permute-done.3.beside
  49.7 0.0 copy-done.1
  49.7 1.2 %ready.1 = (f32[256,1024]{1,0:T(8,128)S(1)}, bf16[2,4,256,256]{3,2,1,0:T(8,128)(2,1)S(1)}) custom-call(f32[256,1024]{1,0:T(8,128)S(1)} %copy-done.1, bf16[384,1024]{1,0:T(8,128)(2,1)S(1)} %collective-permute-done.2._.near, bf16[3,208,256]{2,1,0:T(8,128)(2,1)S(1)} %get-tuple-element.20._.here, bf16[3,208,256]{2,1,0:T(8,128)(2,1)S(1)} %collective-permute-done.3.beside, ...), custom_call_target="tpu_custom_call" | custom-call | tf_op jit(solution)/shard_map/ready/pallas_call | solution.py:591
  50.9 0.0 collective-permute-done.7.two_off
  51.0 0.0 collective-permute-done.8.three_off
  51.0 0.0 copy-done.2
  51.0 1.9 %owned.1 = (f32[4,256,256]{2,1,0:T(8,128)}, f32[8,128]{1,0:T(8,128)S(1)}) custom-call(s32[32]{0:T(128)S(1)} %copy-done.2, bf16[3,208,256]{2,1,0:T(8,128)(2,1)S(1)} %get-tuple-element.20._.here, bf16[3,208,256]{2,1,0:T(8,128)(2,1)S(1)} %collective-permute-done.3.beside, bf16[208,256]{1,0:T(8,128)(2,1)S(1)} %collective-permute-done.7.two_off, ...), custom_call_target="tpu_custom_call" | custom-call | flops 20000000000 | tf_op jit(solution)/shard_map/owned/pallas_call | solution.py:601
  52.9 1.2 %collective-permute-done.6.come = bf16[384,1024]{1,0:T(8,128)(2,1)S(1)} collective-permute-done((bf16[384,1024]{1,0:T(8,128)(2,1)S(1)}, bf16[384,1024]{1,0:T(8,128)(2,1)S(1)}, u32[]{:S(2)}, u32[]{:S(2)}) %collective-permute-start.6) | collective-permute-done | bytes 786464 | tf_op jit(solution)/shard_map/ppermute | solution.py:634
  54.1 2.3 %finish.1 = f32[1024,256]{1,0:T(8,128)} custom-call(bf16[2,4,256,256]{3,2,1,0:T(8,128)(2,1)S(1)} %get-tuple-element.23.split, bf16[512,256]{1,0:T(8,128)(2,1)S(1)} %invert_group.1._.left, f32[256,1024]{1,0:T(8,128)S(1)} %get-tuple-element.24._.so_far, bf16[384,1024]{1,0:T(8,128)(2,1)S(1)} %collective-permute-done.6.come, f32[8,128]{1,0:T(8,128)S(1)} %get-tuple-element.26._), custom_call_target="tpu_custom_call" | custom-call | bytes 6291456 | tf_op jit(solution)/shard_map/finish/pallas_call | solution.py:614
Async XLA Ops:
  9.5 6.1 %collective-permute-start = (f32[3,256,1024]{2,1,0:T(8,128)}, f32[3,256,1024]{2,1,0:T(8,128)}, u32[]{:S(2)}, u32[]{:S(2)}) collective-permute-start(f32[3,256,1024]{2,1,0:T(8,128)} %get-tuple-element.15), channel_id=1, source_target_pairs={{0,4},{4,0},{8,12},{12,8},{16,20},{20,16},{24,28},{28,24},{1,5},{5... | collective-permute-start | bytes 9437192 | tf_op jit(solution)/shard_map/ppermute | solution.py:631
  10.1 12.2 %collective-permute-start.1 = (f32[1,256,1024]{2,1,0:T(8,128)}, f32[1,256,1024]{2,1,0:T(8,128)}, u32[]{:S(2)}, u32[]{:S(2)}) collective-permute-start(f32[1,256,1024]{2,1,0:T(8,128)} %get-tuple-element.16), channel_id=1, source_target_pairs={{0,4},{4,0},{8,12},{12,8},{16,20},{20,16},{24,28},{28,24},{1,5},{5... | collective-permute-start | bytes 3145736 | tf_op jit(solution)/shard_map/ppermute | solution.py:631
  10.1 19.3 %all-to-all-start = ((bf16[8,7,32,256]{3,2,1,0:T(8,128)(2,1)}), bf16[8,7,32,256]{3,2,1,0:T(8,128)(2,1)S(1)}, u32[]{:S(2)}, u32[]{:S(2)}) async-start(bf16[8,7,32,256]{3,2,1,0:T(8,128)(2,1)} %get-tuple-element.19), calls=%async_computation | async-start | bytes 1835008 | tf_op jit(solution)/shard_map/all_to_all | solution.py:640
  19.3 20.4 %collective-permute-start.5 = (bf16[384,1024]{1,0:T(8,128)(2,1)}, bf16[384,1024]{1,0:T(8,128)(2,1)S(1)}, u32[]{:S(2)}, u32[]{:S(2)}) collective-permute-start(bf16[384,1024]{1,0:T(8,128)(2,1)} %sum_far.1.refs_0_), channel_id=1, source_target_pairs={{0,8},{4,20},{8,0},{12,28},{16,24},{20,4},{24,16},{28,12},{1,9},{5... | collective-permute-start | bytes 2359304 | tf_op jit(solution)/shard_map/ppermute | solution.py:634
  28.4 12.1 %copy-start = (f32[256,1024]{1,0:T(8,128)S(1)}, f32[256,1024]{1,0:T(8,128)}, u32[]{:S(2)}) copy-start(f32[256,1024]{1,0:T(8,128)} %get-tuple-element.22.rest) | copy-start | bytes 3145732
  28.4 17.7 %collective-permute-start.2 = (bf16[384,1024]{1,0:T(8,128)(2,1)}, bf16[384,1024]{1,0:T(8,128)(2,1)S(1)}, u32[]{:S(2)}, u32[]{:S(2)}) collective-permute-start(bf16[384,1024]{1,0:T(8,128)(2,1)} %get-tuple-element.18), channel_id=1, source_target_pairs={{0,8},{4,20},{8,0},{12,28},{16,24},{20,4},{24,16},{28,12},{1,9},{5... | collective-permute-start | bytes 2359304 | tf_op jit(solution)/shard_map/ppermute | solution.py:634
  35.4 14.3 %copy-start.1 = (f32[256,1024]{1,0:T(8,128)S(1)}, f32[256,1024]{1,0:T(8,128)}, u32[]{:S(2)}) copy-start(f32[256,1024]{1,0:T(8,128)} %get-tuple-element.17.own) | copy-start | bytes 3145732
  35.5 14.2 %collective-permute-start.3 = (bf16[3,208,256]{2,1,0:T(8,128)(2,1)S(1)}, bf16[3,208,256]{2,1,0:T(8,128)(2,1)S(1)}, u32[]{:S(2)}, u32[]{:S(2)}) collective-permute-start(bf16[3,208,256]{2,1,0:T(8,128)(2,1)S(1)} %get-tuple-element.20._.here), channel_id=1, source_target_pairs={{0,1},{1,0},{2,3},{3,2},{4,5},{5,4},{6,7},{7,6},{8,9},{9,8},{10,11... | collective-permute-start | bytes 958472 | tf_op jit(solution)/shard_map/ppermute | solution.py:631
  37.1 4.9 %collective-permute-start.4 = (bf16[8,32,256]{2,1,0:T(8,128)(2,1)S(1)}, bf16[8,32,256]{2,1,0:T(8,128)(2,1)S(1)}, u32[]{:S(2)}, u32[]{:S(2)}) collective-permute-start(bf16[8,32,256]{2,1,0:T(8,128)(2,1)S(1)} %get-tuple-element.21.half), channel_id=1, source_target_pairs={{0,4},{4,0},{8,12},{12,8},{16,20},{20,16},{24,28},{28,24},{1,5},{5... | collective-permute-start | bytes 393224 | tf_op jit(solution)/shard_map/ppermute | solution.py:631
  37.1 13.8 %collective-permute-start.7 = (bf16[208,256]{1,0:T(8,128)(2,1)S(1)}, bf16[208,256]{1,0:T(8,128)(2,1)S(1)}, u32[]{:S(2)}, u32[]{:S(2)}) collective-permute-start(bf16[208,256]{1,0:T(8,128)(2,1)S(1)} %get-tuple-element.25), channel_id=1, source_target_pairs={{0,2},{1,3},{2,0},{3,1},{4,6},{5,7},{6,4},{7,5},{8,10},{9,11},{10,... | collective-permute-start | bytes 319496 | tf_op jit(solution)/shard_map/ppermute | solution.py:631
  39.7 11.3 %collective-permute-start.8 = (bf16[208,256]{1,0:T(8,128)(2,1)S(1)}, bf16[208,256]{1,0:T(8,128)(2,1)S(1)}, u32[]{:S(2)}, u32[]{:S(2)}) collective-permute-start(bf16[208,256]{1,0:T(8,128)(2,1)S(1)} %get-tuple-element.25), channel_id=1, source_target_pairs={{0,3},{1,2},{2,1},{3,0},{4,7},{5,6},{6,5},{7,4},{8,11},{9,10},{10,... | collective-permute-start | bytes 319496 | tf_op jit(solution)/shard_map/ppermute | solution.py:631
  42.0 9.0 %copy-start.2 = (s32[32]{0:T(128)S(1)}, s32[32]{0:T(128)}, u32[]{:S(2)}) copy-start(s32[32]{0:T(128)} %owner.3) | copy-start | bytes 388
  42.0 12.1 %collective-permute-start.6 = (bf16[384,1024]{1,0:T(8,128)(2,1)S(1)}, bf16[384,1024]{1,0:T(8,128)(2,1)S(1)}, u32[]{:S(2)}, u32[]{:S(2)}) collective-permute-start(bf16[384,1024]{1,0:T(8,128)(2,1)S(1)} %hop.1.__), channel_id=1, source_target_pairs={{0,16},{4,12},{8,24},{12,4},{16,0},{20,28},{24,8},{28,20},{1,17},{... | collective-permute-start | bytes 2359304 | tf_op jit(solution)/shard_map/ppermute | solution.py:634
